TPU v7x, 32 devices: a whole 2x2x4 slice. The times are simulated.
32 devices in a mesh: rep: 4 (over z), expert: 8 (over y, x, core).
Axes of the slice: x: 2, y: 2, z: 4, core: 2. Of those that a mesh axis runs over, the one named last changes fastest.
Arguments:
- tokens: bfloat16 [4096, 2048], P(('rep', 'expert')), may hold values from -6 to 6
- norm_gain: float32 [2048], replicated, may hold values from 0.1 to 1.9
- router: bfloat16 [2048, 32], P('rep'), may hold values from -0.125 to 0.125
- routes: int32 [4096, 8], P(('rep', 'expert')), may hold values from 0 to 31, all different within a row; in each aligned block of 128 rows (0 to 127, 128 to 255, ...) at most 48 rows name the same one
- placement: int32 [32], replicated, may hold values from 0 to 31, each once
- w_gate: bfloat16 [32, 2048, 768], P(('rep', 'expert')), may hold values from -0.125 to 0.125
- w_up: bfloat16 [32, 2048, 768], P(('rep', 'expert')), may hold values from -0.125 to 0.125
- w_down: bfloat16 [32, 768, 2048], P(('rep', 'expert')), may hold values from -0.21875 to 0.21875
Outputs:
- moe_out: bfloat16 [4096, 2048], P(('rep', 'expert'))
Inputs may be any that keep to these rules, and one draw needn't show every extreme that they name: `routes`: each token's 8 experts differ. Among the 128 tokens of one device at most 48 rows name any one expert, and in some devices' rows one expert is named exactly 48 times. `placement`: A permutation. Weight slot s lies on the device numbered s over rep then expert.
All inputs are finite; a program needn't handle non-finite values.
Results may differ from a plain program's by a relative error of at most 0.0075.
Values may be sent and summed in bfloat16 or wider, within the bound.
No kernel may reach another device: no remote copies, remote signals or barrier semaphores. Data moves between devices by JAX's collectives and lax.ppermute only.
A program may use at most 128 MiB of HBM per device.

v0:
```python
import jax
import jax.numpy as jnp
from jax import lax
from jax.sharding import PartitionSpec as P


def per_device(tokens, norm_gain, router, routes, placement, w_gate, w_up, w_down):
    tok_rows = tokens.shape[0]
    model_width = tokens.shape[1]
    top_count = routes.shape[1]
    expert_count = placement.shape[0]
    rep_count = lax.axis_size("rep")
    owner_count = lax.axis_size("expert")
    devices = rep_count * owner_count
    capacity = 3 * tok_rows * top_count // (2 * expert_count)
    values = tokens.astype(jnp.float32)
    scale = lax.rsqrt(jnp.mean(values * values, axis=-1, keepdims=True) + 1e-06)
    normed = (values * scale * norm_gain[None, :]).astype(jnp.bfloat16)
    logits = jnp.dot(
        normed,
        lax.all_gather(router, "rep", axis=0, tiled=True),
        preferred_element_type=jnp.float32,
    )
    picked = jnp.take_along_axis(logits, routes, axis=1)
    powers = jnp.exp(picked)
    shares = (powers / jnp.sum(powers, axis=1, keepdims=True)).reshape(-1)
    flat_routes = routes.reshape(-1)
    one_hot = (flat_routes[:, None] == jnp.arange(expert_count, dtype=jnp.int32)[None, :]).astype(
        jnp.int32
    )
    target = jnp.sum(one_hot * placement[None, :], axis=1)
    earlier = jnp.cumsum(one_hot, axis=0) - one_hot
    slot_rank = jnp.sum(earlier * one_hot, axis=1)
    position = target * capacity + slot_rank
    repeated = jnp.repeat(normed, top_count, axis=0)
    outgoing = jnp.zeros((devices * capacity, model_width), jnp.bfloat16).at[position].set(repeated)
    outgoing = outgoing.reshape(devices, capacity, model_width)
    received = lax.all_to_all(outgoing, ("rep", "expert"), split_axis=0, concat_axis=0, tiled=True)
    stacked = received.reshape(-1, model_width)
    gate_proj = jnp.dot(stacked, w_gate[0], preferred_element_type=jnp.float32)
    up_proj = jnp.dot(stacked, w_up[0], preferred_element_type=jnp.float32)
    hidden = (jax.nn.silu(gate_proj) * up_proj).astype(jnp.bfloat16)
    result = jnp.dot(hidden, w_down[0], preferred_element_type=jnp.float32).astype(jnp.bfloat16)
    returned = lax.all_to_all(
        result.reshape(received.shape), ("rep", "expert"), split_axis=0, concat_axis=0, tiled=True
    )
    collected = returned.reshape(devices * capacity, model_width)[position]
    weighted = collected.astype(jnp.float32) * shares[:, None]
    combined = jnp.sum(weighted.reshape(tok_rows, top_count, model_width), axis=1)
    return combined.astype(jnp.bfloat16)


def solution(mesh):
    placed = (
        P(("rep", "expert"), None),
        P(),
        P("rep", None),
        P(("rep", "expert"), None),
        P(),
        P(("rep", "expert"), None, None),
        P(("rep", "expert"), None, None),
        P(("rep", "expert"), None, None),
    )
    return jax.shard_map(
        per_device,
        mesh=mesh,
        in_specs=placed,
        out_specs=P(("rep", "expert"), None),
        check_vma=False,
    )
```

profile of v0, /device:TPU:0, one launch (start us, length us, event | category | flops | bytes accessed | tf_op | source)
XLA Modules:
  0.0 366.6 jit_solution(11629480236912262882)
XLA Ops:
  0.0 0.0 copy-start
  0.0 0.9 copy.19
  0.9 0.1 eq.29
  1.0 0.1 eq.25
  1.1 1.2 fusion.9
  2.4 9.0 %reduce-window.6 = s32[32,8,128]{2,1,0:T(8,128)S(1)} reduce-window(s32[32,8,128]{2,1,0:T(8,128)S(1)} %fusion.15, s32[]{:T(128)} %constant.13.clone.1), window={size=1x1x128 pad=0_0x0_0x127_0}, to_apply=%region_1.0 | reduce-window | flops 4161536 | bytes 262148 | tf_op jit(solution)/shard_map/reduce-window
  11.4 0.1 slice.12
  11.5 0.1 copy.21
  11.7 0.1 copy.22
  11.7 0.1 broadcast_add_fusion
  11.9 0.7 select_reduce_fusion
  12.6 2.0 fusion.11
  14.7 10.7 %scatter_custom_fusion = bf16[1536,2048]{1,0:T(8,128)(2,1)} fusion(s32[1024]{0:T(1024)S(1)} %bitcast.56, bf16[]{:T(256)} %constant.12.clone.1, bf16[128,2048]{1,0:T(8,128)(2,1)} %fusion.11), kind=kCustom, calls=%fused_computation.7 | custom fusion | bytes 6815746 | tf_op jit(solution)/shard_map/scatter | solution.py:36
  25.3 0.0 copy-start.3
  25.3 145.9 %all_to_all.10 = bf16[32,48,2048]{2,1,0:T(8,128)(2,1)S(1)} all-to-all(bf16[32,48,2048]{2,1,0:T(8,128)(2,1)} %bitcast.49), channel_id=1, replica_groups=mesh['rep'=4,'expert'=8] {'rep','expert'}, dimensions={0} | all-to-all | bytes 12582912 | tf_op jit(solution)/shard_map/all_to_all | solution.py:38
  171.2 0.0 copy-done.3
  171.2 0.0 copy-start.4
  171.2 5.2 %fusion.5 = f32[1536,768]{1,0:T(8,128)S(1)} fusion(bf16[1536,2048]{1,0:T(8,128)(2,1)S(1)} %bitcast.51, bf16[1,2048,768]{2,1,0:T(8,128)(2,1)S(1)} %copy-done.3), kind=kOutput, calls=%fused_computation.11 | convolution fusion | flops 4831838208 | bytes 14155776 | tf_op jit(solution)/shard_map/dot_general | solution.py:40
  176.4 0.0 copy-done.4
  176.4 5.6 %multiply_convert_fusion = bf16[1536,768]{1,0:T(8,128)(2,1)S(1)} fusion(f32[1536,768]{1,0:T(8,128)S(1)} %fusion.5, bf16[1536,2048]{1,0:T(8,128)(2,1)S(1)} %bitcast.52, bf16[1,2048,768]{2,1,0:T(8,128)(2,1)S(1)} %copy-done.4), kind=kOutput, calls=%fused_computation.6 | convolution fusion | flops 4838916096 | bytes 16515072 | tf_op jit(solution)/shard_map/dot_general | solution.py:41
  182.0 0.0 copy-done
  182.1 7.0 %convolution_convert_fusion = bf16[1536,2048]{1,0:T(8,128)(2,1)} fusion(bf16[1536,768]{1,0:T(8,128)(2,1)S(1)} %multiply_convert_fusion, bf16[1,768,2048]{2,1,0:T(8,128)(2,1)S(1)} %copy-done), kind=kOutput, calls=%fused_computation.5 | convolution fusion | flops 4834983936 | bytes 11796480 | tf_op jit(solution)/shard_map/dot_general | solution.py:43
  189.1 0.0 copy-start.1
  189.1 0.0 copy-start.2
  189.1 3.9 %all-to-all-start.1 = ((bf16[32,48,2048]{2,1,0:T(8,128)(2,1)}), bf16[32,48,2048]{2,1,0:T(8,128)(2,1)}, u32[]{:S(2)}, u32[]{:S(2)}) async-start(bf16[32,48,2048]{2,1,0:T(8,128)(2,1)} %bitcast.50), calls=%async_computation.1 | async-start | bytes 12582912 | tf_op jit(solution)/shard_map/all_to_all | solution.py:44
  193.0 0.0 copy-done.1
  193.0 0.1 copy.23
  193.1 0.1 reshape.118
  193.2 0.0 copy-done.2
  193.2 145.0 %all_gather.3 = bf16[2048,32]{0,1:T(8,128)(2,1)S(1)} all-gather(bf16[512,32]{0,1:T(8,128)(2,1)S(1)} %copy-done.2), channel_id=1, replica_groups=mesh['rep'=4,'expert'=8] {'rep'}, dimensions={0}, use_global_device_ids=true | all-gather | bytes 163840 | tf_op jit(solution)/shard_map/all_gather | solution.py:21
  338.2 1.3 fusion.17
  339.5 7.0 %gather_fusion.1 = f32[1024]{0:T(1024)S(1)} fusion(f32[128,32]{0,1:T(8,128)S(1)} %fusion.17, s32[1024]{0:T(1024)S(1)} %reshape.118), kind=kCustom, calls=%fused_computation.1 | custom fusion | bytes 16384 | tf_op jit(solution)/shard_map/jit(take_along_axis)/gather | solution.py:24
  346.6 0.1 reshape.121
  346.8 0.1 copy.25
  346.9 0.0 all-to-all-done.1
  346.9 12.4 %gather_fusion = bf16[1024,2048]{1,0:T(8,128)(2,1)} fusion(bf16[1536,2048]{1,0:T(8,128)(2,1)} %bitcast.11, s32[1024]{0:T(1024)S(1)} %broadcast_clamp_fusion), kind=kCustom, calls=%fused_computation | custom fusion | bytes 8392704 | tf_op jit(solution)/shard_map/gather | solution.py:47
  359.3 7.3 %fusion = bf16[128,2048]{1,0:T(8,128)(2,1)} fusion(bf16[1024,2048]{1,0:T(8,128)(2,1)} %gather_fusion, f32[128,8]{1,0:T(8,128)S(1)} %copy.25), kind=kLoop, calls=%fused_computation.4 | loop fusion | flops 6029312 | bytes 4722688 | tf_op jit(solution)/shard_map/reduce_sum | solution.py:49
  (11 shorter events, 0.2 us)
Async XLA Ops:
  0.0 182.0 %copy-start = (bf16[1,768,2048]{2,1,0:T(8,128)(2,1)S(1)}, bf16[1,768,2048]{2,1,0:T(8,128)(2,1)}, u32[]{:S(2)}) copy-start(bf16[1,768,2048]{2,1,0:T(8,128)(2,1)} %param.15) | copy-start | bytes 9437188
  25.3 145.9 %copy-start.3 = (bf16[1,2048,768]{2,1,0:T(8,128)(2,1)S(1)}, bf16[1,2048,768]{2,1,0:T(8,128)(2,1)}, u32[]{:S(2)}) copy-start(bf16[1,2048,768]{2,1,0:T(8,128)(2,1)} %param.13) | copy-start | bytes 9437188
  171.2 5.2 %copy-start.4 = (bf16[1,2048,768]{2,1,0:T(8,128)(2,1)S(1)}, bf16[1,2048,768]{2,1,0:T(8,128)(2,1)}, u32[]{:S(2)}) copy-start(bf16[1,2048,768]{2,1,0:T(8,128)(2,1)} %param.14) | copy-start | bytes 9437188
  189.1 3.9 %copy-start.1 = (s32[128,8]{0,1:T(8,128)S(1)}, s32[128,8]{0,1:T(8,128)}, u32[]{:S(2)}) copy-start(s32[128,8]{0,1:T(8,128)} %param.11) | copy-start | bytes 12292
  189.1 4.1 %copy-start.2 = (bf16[512,32]{0,1:T(8,128)(2,1)S(1)}, bf16[512,32]{0,1:T(8,128)(2,1)}, u32[]{:S(2)}) copy-start(bf16[512,32]{0,1:T(8,128)(2,1)} %param.10) | copy-start | bytes 98308
  189.1 157.8 %all-to-all-start.1 = ((bf16[32,48,2048]{2,1,0:T(8,128)(2,1)}), bf16[32,48,2048]{2,1,0:T(8,128)(2,1)}, u32[]{:S(2)}, u32[]{:S(2)}) async-start(bf16[32,48,2048]{2,1,0:T(8,128)(2,1)} %bitcast.50), calls=%async_computation.1 | async-start | bytes 12582912 | tf_op jit(solution)/shard_map/all_to_all | solution.py:44
where the time goes:
time: 367 us
  blocking collectives  291 us (79%)
  local copies, waits for them, and re-layouts  31.9 us (9%)
  other arithmetic  20.6 us (6%)
  matrix products  19.2 us (5%)
  starting transfers between devices  3.86 us (1%)
    all_to_all x1, blocking collectives, per_device(): lax.all_to_all(outgoing, ('rep', 'expert'), split_axis=0, concat_axis=0,...  146 us
    all_gather x1, blocking collectives, per_device(): lax.all_gather(router, 'rep', axis=0, tiled=True)  145 us
    gather x1, local copies, waits for them, and re-layouts, per_device(): collected = returned.reshape(devices * capacity, model_width)[position]  12.4 us
    scatter x1, local copies, waits for them, and re-layouts, per_device(): jnp.zeros((devices * capacity, model_width), jnp.bfloat16).at[position]  10.7 us
    another operation x3, other arithmetic  9.15 us
    gather x5, local copies, waits for them, and re-layouts, per_device(): picked = jnp.take_along_axis(logits, routes, axis=1)  7.36 us
  transfers between devices with their start and end apart: 1, of which 0 were waited for; matrix products, arithmetic and copies ran while one was open for 2% of the time, Pallas kernels for 0%

commit v1 on v0

v1 whole, which is shorter than its diff:
```python
import functools

import jax
import jax.numpy as jnp
from jax import lax
from jax.experimental import pallas as pl
from jax.experimental.pallas import tpu as pltpu
from jax.sharding import PartitionSpec as P

BF16, F32, I32 = jnp.bfloat16, jnp.float32, jnp.int32
CORES = 2
Y_SIZE = 2
HALVES = 2
MIB = 1 << 20
SMEM = pl.BlockSpec(memory_space=pltpu.SMEM)
VMEM = pl.BlockSpec(memory_space=pltpu.VMEM)
HBM = pl.BlockSpec(memory_space=pltpu.HBM)


def round_up(number, step):
    return -(-number // step) * step


def took(microseconds):
    return pl.CostEstimate(flops=int(microseconds * 1e9), bytes_accessed=0, transcendentals=0)


def params():
    return pltpu.CompilerParams(vmem_limit_bytes=12 * MIB)


def pack_kernel(piece, tokens, gain, routes, router, out_ref):
    rows, width = tokens.shape
    top = routes.shape[0]
    depth = router.shape[1]
    extra = out_ref.shape[0] - rows
    values = tokens[...].astype(F32)
    scale = lax.rsqrt(jnp.mean(values * values, axis=-1, keepdims=True) + 1e-06)
    out_ref[:rows, :] = (values * scale * gain[...]).astype(BF16)
    spread = jnp.concatenate(
        [router[q * piece : (q + 1) * piece, :].astype(F32) for q in range(width // depth)], axis=1
    )
    parts = [jnp.concatenate([routes[...].astype(F32), jnp.zeros((top, width - rows), F32)], axis=1), spread]
    if extra > top + piece:
        parts.insert(1, jnp.zeros((extra - top - piece, width), F32))
    out_ref[rows:, :] = jnp.concatenate(parts, axis=0).astype(BF16)


def router_kernel(rows, piece, plane_ref, *refs):
    blocks, out_ref = refs[:-1], refs[-1]
    pieces = len(blocks)
    depth = out_ref.shape[1] // pieces
    for d, block in enumerate(blocks):
        start = pl.multiple_of(lax.rem(plane_ref[0] - d + pieces, pieces) * depth, depth)
        last = block[rows:, :].astype(F32)[-piece:]
        out_ref[:, pl.ds(start, depth)] = jnp.concatenate(
            [last[:, q * depth : (q + 1) * depth] for q in range(pieces)], axis=0
        ).astype(BF16)


def membership(routes, experts, rows):
    names = lax.broadcasted_iota(I32, (experts, rows), 0).astype(F32)
    member = names == routes[0:1, :]
    for k in range(1, routes.shape[0]):
        member = member | (names == routes[k : k + 1, :])
    return member


def positions(member, groups_ref, rows):
    mine = jnp.dot(
        groups_ref[...].astype(BF16), jnp.where(member, 1.0, 0.0).astype(BF16), preferred_element_type=F32
    )
    earlier = lax.broadcasted_iota(I32, (rows, rows), 0) < lax.broadcasted_iota(I32, (rows, rows), 1)
    rank = jnp.dot(
        mine.astype(BF16), jnp.where(earlier, 1.0, 0.0).astype(BF16), preferred_element_type=F32
    )
    return jnp.where(mine > 0, rank, -1.0)


def select_kernel(rows, cap, top, groups_ref, *refs):
    groups, experts = groups_ref.shape
    blocks, outs = refs[:-groups], refs[-groups:]
    slot = lax.broadcasted_iota(I32, (cap, rows), 0).astype(F32)
    for i, block in enumerate(blocks):
        routes = block[rows : rows + 16, :rows].astype(F32)[:top]
        place = positions(membership(routes, experts, rows), groups_ref, rows)
        pick = jnp.concatenate(
            [jnp.where(slot == place[j : j + 1, :], 1.0, 0.0) for j in range(groups)], axis=0
        ).astype(BF16)
        found = jnp.dot(pick, block[:rows, :], preferred_element_type=F32).astype(BF16)
        for j in range(groups):
            outs[j][i * cap : (i + 1) * cap, :] = found[j * cap : (j + 1) * cap, :]


def experts_kernel(groups, *refs):
    ins, (gate_ref, up_ref, down_ref) = refs[:groups], refs[groups : groups + 3]
    outs, (stacked,) = refs[groups + 3 : -1], refs[-1:]
    size = ins[0].shape[0]
    hidden_width = gate_ref.shape[2]
    for j in range(groups):
        stacked[j * size : (j + 1) * size, :] = ins[j][...]
    gate = jnp.dot(stacked[...], gate_ref[0], preferred_element_type=F32)
    up = jnp.dot(stacked[...], up_ref[0], preferred_element_type=F32)
    hidden = (gate / (1.0 + jnp.exp(-gate)) * up).astype(BF16)
    product = jnp.dot(hidden, down_ref[0], preferred_element_type=F32).astype(BF16)
    for j in range(groups):
        outs[j][...] = product[j * size : (j + 1) * size, :]


def combine_kernel(rows, cap, top, dense, halves, groups_ref, router_ref, *refs):
    groups, experts = groups_ref.shape
    blocks, results, outs = refs[:dense], refs[dense : dense + groups], refs[dense + groups :]
    slot = lax.broadcasted_iota(I32, (cap, rows), 0).astype(F32)
    for i, block in enumerate(blocks):
        routes = block[rows : rows + 16, :rows].astype(F32)[:top]
        member = membership(routes, experts, rows)
        place = positions(member, groups_ref, rows)
        logits = lax.dot_general(
            router_ref[...], block[:rows, :], (((1,), (1,)), ((), ())), preferred_element_type=F32
        )
        powers = jnp.where(member, jnp.exp(logits), 0.0)
        shares = powers / jnp.sum(powers, axis=0, keepdims=True)
        own = jnp.dot(
            groups_ref[...], shares, preferred_element_type=F32, precision=lax.Precision.HIGHEST
        )
        weights = jnp.concatenate(
            [jnp.where(slot == place[j : j + 1, :], own[j : j + 1, :], 0.0) for j in range(groups)], axis=0
        )
        coarse = weights.astype(BF16)
        fine = (weights - coarse.astype(F32)).astype(BF16)
        found = jnp.concatenate(
            [result[i * cap : (i + 1) * cap, :] for result in results], axis=0
        )
        down = (((0,), (0,)), ((), ()))
        summed = lax.dot_general(coarse, found, down, preferred_element_type=F32)
        summed = summed + lax.dot_general(fine, found, down, preferred_element_type=F32)
        parts = outs[:1] if i == 0 else outs[1 + (i - 1) * halves : 1 + i * halves]
        size = rows // len(parts)
        for h, part in enumerate(parts):
            part[...] = summed[h * size : (h + 1) * size].astype(part.dtype)


def add_kernel(starts, own, *refs):
    out_ref = refs[-1]
    cuts = sorted(set(starts)) + [own.shape[0]]
    for low, high in zip(cuts[:-1], cuts[1:]):
        part = own[low:high, :]
        for start, ref in zip(starts, refs[:-1]):
            if start <= low < start + ref.shape[0]:
                part = part + ref[low - start : high - start, :].astype(F32)
        out_ref[low:high, :] = part.astype(BF16)


def per_device(tokens, norm_gain, router, routes, placement, w_gate, w_up, w_down):
    rows, width = tokens.shape
    top = routes.shape[1]
    experts = placement.shape[0]
    reps = lax.axis_size("rep")
    owners = lax.axis_size("expert")
    x_size = owners // (Y_SIZE * CORES)
    cap = round_up(3 * rows * top // (2 * experts), 16)
    plane = lax.axis_index("rep")
    owner = lax.axis_index("expert")
    depth = router.shape[0]
    piece = experts // reps
    extra = round_up(top + piece, 16)
    mixed = x_size == Y_SIZE
    dense = x_size
    steps = [(by, core_by) for by in range(Y_SIZE) for core_by in range(CORES)]

    def moved(y, x, core, by, core_by, along_x):
        if along_x:
            x = (x + by) % x_size
        else:
            y = (y + by) % Y_SIZE
        return (y * x_size + x) * CORES + (core ^ core_by)

    def shift_owner(array, by, core_by, is_dense):
        pairs = []
        for y in range(Y_SIZE):
            for x in range(x_size):
                for core in range(CORES):
                    along_x = is_dense ^ (mixed and core == 1)
                    there = moved(y, x, core, abs(by), core_by, along_x)
                    pairs.append(((y * x_size + x) * CORES + core, there))
        return lax.ppermute(array, "expert", pairs if by >= 0 else [(b, a) for a, b in pairs])

    def shift_plane(array, by):
        return lax.ppermute(array, "rep", [(r, (r + by) % reps) for r in range(reps)])

    core = owner % CORES
    x_at = owner // CORES % x_size
    y_at = owner // CORES // x_size
    slots = []
    for by, core_by in steps:
        there = moved(y_at, x_at, core, by, core_by, False)
        if mixed:
            there = jnp.where(core == 1, moved(y_at, x_at, core, by, core_by, True), there)
        slots.append(plane * owners + there)
    groups = (placement[None, :] == jnp.stack(slots)[:, None]).astype(F32)

    shapes = [(rows, width), (1, width), (top, rows), (experts, depth)]
    packed = pl.pallas_call(
        functools.partial(pack_kernel, piece),
        out_shape=jax.ShapeDtypeStruct((rows + extra, width), BF16),
        in_specs=[pl.BlockSpec(shape, lambda i: (0, 0)) for shape in shapes],
        out_specs=VMEM,
        grid=(1,),
        compiler_params=params(),
        name="pack",
    )(tokens, norm_gain.reshape(1, width), routes.T, router.T)

    def after(array, *others):
        return lax.optimization_barrier((array, *others))[0]

    def after_all(arrays, *others):
        return lax.optimization_barrier((tuple(arrays), *others))[0]

    def select(blocks):
        return pl.pallas_call(
            functools.partial(select_kernel, rows, cap, top),
            out_shape=[jax.ShapeDtypeStruct((dense * cap, width), BF16)] * len(steps),
            in_specs=[VMEM] * (1 + dense),
            out_specs=[VMEM] * len(steps),
            compiler_params=params(),
            cost_estimate=took(1),
            name="select",
        )(groups, *blocks)

    def send_blocks(block):
        return [block] + [shift_owner(block, by, 0, True) for by in range(1, dense)]

    def send_rows(sent):
        return [sent[0]] + [shift_owner(sent[j], *steps[j], False) for j in range(1, len(steps))]

    def whole_router(sources):
        return pl.pallas_call(
            functools.partial(router_kernel, rows, piece),
            out_shape=jax.ShapeDtypeStruct((experts, width), BF16),
            in_specs=[SMEM] + [VMEM] * reps,
            out_specs=VMEM,
            compiler_params=params(),
            cost_estimate=took(1),
            name="router",
        )(plane.reshape(1), *sources)

    def apply_experts(here):
        size, count = here[0].shape[0], len(here)
        results = pl.pallas_call(
            functools.partial(experts_kernel, count),
            out_shape=[jax.ShapeDtypeStruct((size, width), BF16)] * count,
            in_specs=[VMEM] * (count + 3),
            out_specs=[VMEM] * count,
            scratch_shapes=[pltpu.VMEM((size * count, width), BF16)],
            compiler_params=params(),
            cost_estimate=took(4),
            name="experts",
        )(*here, w_gate, w_up, w_down)
        return results

    def shift_back(array, by, core_by, is_dense):
        pairs = []
        for y in range(Y_SIZE):
            for x in range(x_size):
                for core_at in range(CORES):
                    along_x = is_dense ^ (mixed and core_at == 1)
                    there = moved(y, x, core_at, by, core_by, along_x)
                    pairs.append((there, (y * x_size + x) * CORES + core_at))
        return lax.ppermute(array, "expert", pairs)

    def combine(blocks, back, router_full, halves):
        sums = pl.pallas_call(
            functools.partial(combine_kernel, rows, cap, top, dense, halves),
            out_shape=[jax.ShapeDtypeStruct((rows, width), F32)]
            + [jax.ShapeDtypeStruct((rows // halves, width), BF16)] * (halves * (dense - 1)),
            in_specs=[VMEM] * (2 + dense + len(steps)),
            out_specs=[VMEM] * (1 + halves * (dense - 1)),
            compiler_params=params(),
            cost_estimate=took(2),
            name="combine",
        )(groups, router_full, *blocks, *back)
        return sums

    def return_sums(sums):
        halves = (len(sums) - 1) // (dense - 1)
        return [sums[0]] + [
            [shift_back(sums[1 + by * halves + h], by + 1, 0, True) for by in range(dense - 1)]
            for h in range(halves)
        ]

    def add_up(own, *lists):
        starts, parts = [], []
        for pieces in lists:
            size = rows // len(pieces)
            starts += [h * size for h in range(len(pieces))]
            parts += pieces
        return pl.pallas_call(
            functools.partial(add_kernel, starts),
            out_shape=jax.ShapeDtypeStruct((rows, width), BF16),
            in_specs=[VMEM] * (1 + len(parts)),
            out_specs=VMEM,
            compiler_params=params(),
            cost_estimate=took(1),
            name="add",
        )(own, *parts)

    last = reps - 1
    blocks = [send_blocks(packed)]
    sources = [packed]
    for _ in range(last):
        sources.append(shift_plane(sources[-1], 1))
    sent = select(blocks[0])
    here = send_rows(sent)
    mark = sent[0]
    back, travelling = [], []

    def combine_chunk(i, halves, *others):
        back[i][0] = after(back[i][0], *others)
        sums = combine(blocks[i], back[i], router_full, halves)
        return sums[0], return_sums(sums)

    def add_chunk(sums, *others):
        own = after(sums[0], *others)
        lists = [list(column) for column in zip(*sums[1:])]
        part = add_up(own, *lists, *([travelling] if travelling else []))
        travelling[:] = [shift_plane(part, 1)]
        return part

    def send_back(results, *others):
        back = [results[0]]
        for j in range(1, len(steps)):
            rows_back = after(results[j], back[1], *others) if others and j > 1 else results[j]
            back.append(shift_back(rows_back, *steps[j], False))
        return back

    sums = None
    blocks.append(send_blocks(after(sources[1], *here[1:3])))
    for i in range(reps):
        arrived = here
        if 0 < i < last:
            blocks[i + 1][0] = after(blocks[i + 1][0], mark, *sources[i + 2 : i + 3])
            sent = select(blocks[i + 1])
            mark = sent[0]
            here = send_rows([sent[0]] + [after(rows_out, *arrived) for rows_out in sent[1:]])
            if i + 2 <= last:
                blocks.append(send_blocks(after(sources[i + 2], mark, *arrived)))
        if i == 2:
            router_full = whole_router([after(sources[0], mark)] + sources[1:])
        if 1 < i < last:
            mark, sums = combine_chunk(i - 1, 1, mark)
        arrived[0] = after(arrived[0], mark, *(back[i - 1][1:] if 1 < i < last else []))
        results = apply_experts(arrived)
        back.append(send_back(results) if 0 < i < last else list(results))
        mark = results[0]
        if i == 0:
            blocks[1][0] = after(blocks[1][0], mark)
            sent = select(blocks[1])
            mark = sent[0]
            here = send_rows(sent)
            blocks.append(send_blocks(after(sources[2], mark, here[1])))
        if i == last:
            mark = add_chunk(sums, mark)
            mark, sums = combine_chunk(i - 1, HALVES, mark)
            back[last] = send_back(results, mark)
    mark = add_chunk(sums, mark)
    mark, sums = combine_chunk(last, HALVES, mark)
    back[0] = send_back([back[0][0]] + [after(x, mark) for x in back[0][1:]])
    mark = add_chunk(sums)
    back[0][0] = after(back[0][0], mark)
    own = return_sums(combine(blocks[0], back[0], router_full, HALVES))
    return add_up(own[0], *[list(column) for column in zip(*own[1:])], travelling)


def solution(mesh):
    placed = (
        P(("rep", "expert"), None),
        P(),
        P("rep", None),
        P(("rep", "expert"), None),
        P(),
        P(("rep", "expert"), None, None),
        P(("rep", "expert"), None, None),
        P(("rep", "expert"), None, None),
    )
    return jax.shard_map(
        per_device,
        mesh=mesh,
        in_specs=placed,
        out_specs=P(("rep", "expert"), None),
        check_vma=False,
    )
```

time: 367 us -> 160 us (0.44)
  blocking collectives: 291 us -> 0 us
  waiting for transfers between devices: 0.01 us -> 80.1 us
  starting transfers between devices: 3.86 us -> 42.4 us
  Pallas kernels: 0 us -> 29.4 us
  local copies, waits for them, and re-layouts: 31.9 us -> 6.97 us
  other arithmetic: 20.6 us -> 0.95 us
  matrix products: 19.2 us -> 0 us
    all_to_all x1 -> x0, blocking collectives: 146 us -> none  [per_device(): lax.all_to_all(outgoing, ('rep', 'expert'), split_axis=0, concat_axis=0,...]
    all_gather x1 -> x0, blocking collectives: 145 us -> none  [per_device(): lax.all_gather(router, 'rep', axis=0, tiled=True)]
    ppermute x0 -> x41, waiting for transfers between devices: none -> 80.1 us  [the longest x19 43.4 us: shift_back(): return lax.ppermute(array, 'expert', pairs)]
    ppermute x0 -> x41, starting transfers between devices: none -> 42.4 us  [the longest x16 18.7 us: shift_owner(): lax.ppermute(array, 'expert', pairs if by >= 0 else [(b, a) for a, b in p...]
    pallas_call x0 -> x18, Pallas kernels: none -> 29.4 us  [the longest x4 15.3 us: apply_experts(): pl.pallas_call(functools.partial(experts_kernel, count), out_shape=[jax.S...]
    gather x6 -> x0, local copies, waits for them, and re-layouts: 19.8 us -> none  [the longest x1 12.4 us: per_device(): collected = returned.reshape(devices * capacity, model_width)[position]]
    dot_general x4 -> x0, matrix products: 19.2 us -> none  [the longest x1 7.03 us: per_device(): jnp.dot(hidden, w_down[0], preferred_element_type=jnp.float32)]
    scatter x1 -> x0, local copies, waits for them, and re-layouts: 10.7 us -> none  [per_device(): jnp.zeros((devices * capacity, model_width), jnp.bfloat16).at[position]]
  transfers between devices with their start and end apart: 1 -> 41, of which waited for: 0 -> 22; matrix products, arithmetic and copies ran while one was open for 2% -> 1% of each run, Pallas kernels for 0% -> 18%
where the time goes in v1:
time: 160 us
  waiting for transfers between devices  80.1 us (50%)
  starting transfers between devices  42.4 us (26%)
  Pallas kernels  29.4 us (18%)
  local copies, waits for them, and re-layouts  6.97 us (4%)
    ppermute x19, waiting for transfers between devices, shift_back(): return lax.ppermute(array, 'expert', pairs)  43.4 us
    ppermute x6, waiting for transfers between devices, shift_plane(): lax.ppermute(array, 'rep', [(r, (r + by) % reps) for r in range(reps)])  21 us
    ppermute x16, starting transfers between devices, shift_owner(): lax.ppermute(array, 'expert', pairs if by >= 0 else [(b, a) for a, b in p...  18.7 us
    ppermute x16, waiting for transfers between devices, shift_owner(): lax.ppermute(array, 'expert', pairs if by >= 0 else [(b, a) for a, b in p...  15.7 us
    pallas_call x4, Pallas kernels, apply_experts(): pl.pallas_call(functools.partial(experts_kernel, count), out_shape=[jax.S...  15.3 us
    ppermute x19, starting transfers between devices, shift_back(): return lax.ppermute(array, 'expert', pairs)  15 us
    ppermute x6, starting transfers between devices, shift_plane(): lax.ppermute(array, 'rep', [(r, (r + by) % reps) for r in range(reps)])  8.79 us
    pallas_call x4, Pallas kernels, combine(): pl.pallas_call(functools.partial(combine_kernel, rows, cap, top, dense, h...  8.22 us
  transfers between devices with their start and end apart: 41, of which 22 were waited for; matrix products, arithmetic and copies ran while one was open for 1% of the time, Pallas kernels for 18%

profile of v1, /device:TPU:0, one launch (start us, length us, event | category | flops | bytes accessed | tf_op | source)
XLA Modules:
  0.0 160.1 jit_solution(1546991184005399313)
XLA Ops:
  0.0 1.0 copy-done
  1.0 0.8 copy-done.1
  1.8 0.7 copy-done.2
  2.5 0.7 copy-done.3
  3.4 3.0 %collective-permute-start.3 = (bf16[144,2048]{1,0:T(8,128)(2,1)S(1)}, bf16[144,2048]{1,0:T(8,128)(2,1)S(1)}, u32[]{:S(2)}, u32[]{:S(2)}) collective-permute-start(bf16[144,2048]{1,0:T(8,128)(2,1)S(1)} %pack.1.refs_0_), channel_id=1, source_target_pairs={{0,2},{1,5},{2,0},{3,7},{4,6},{5,1},{6,4},{7,3},{8,10},{9,13},{10,... | collective-permute-start | bytes 1769480 | tf_op jit(solution)/shard_map/ppermute | solution.py:186
  6.4 1.6 collective-permute-start
  8.1 0.9 compare_convert_fusion.groups_ref
  9.0 5.3 %collective-permute-done.3.refs_1_ = bf16[144,2048]{1,0:T(8,128)(2,1)S(1)} collective-permute-done((bf16[144,2048]{1,0:T(8,128)(2,1)S(1)}, bf16[144,2048]{1,0:T(8,128)(2,1)S(1)}, u32[]{:S(2)}, u32[]{:S(2)}) %collective-permute-start.3) | collective-permute-done | bytes 589856 | tf_op jit(solution)/shard_map/ppermute | solution.py:186
  14.3 1.0 select.24
  15.4 2.1 %collective-permute-start.5 = (bf16[96,2048]{1,0:T(8,128)(2,1)S(1)}, bf16[96,2048]{1,0:T(8,128)(2,1)S(1)}, u32[]{:S(2)}, u32[]{:S(2)}) collective-permute-start(bf16[96,2048]{1,0:T(8,128)(2,1)S(1)} %get-tuple-element.76), channel_id=1, source_target_pairs={{0,4},{1,3},{2,6},{3,1},{4,0},{5,7},{6,2},{7,5},{8,12},{9,11},{10,... | collective-permute-start | bytes 1179656 | tf_op jit(solution)/shard_map/ppermute | solution.py:186
  17.5 1.2 collective-permute-start.6
  18.8 4.3 %collective-permute-done.refs_0_.refs_1_ = bf16[144,2048]{1,0:T(8,128)(2,1)S(1)} collective-permute-done((bf16[144,2048]{1,0:T(8,128)(2,1)S(1)}, bf16[144,2048]{1,0:T(8,128)(2,1)S(1)}, u32[]{:S(2)}, u32[]{:S(2)}) %collective-permute-start) | collective-permute-done | bytes 589856 | tf_op jit(solution)/shard_map/ppermute | solution.py:189
  23.3 2.0 %collective-permute-start.7 = (bf16[144,2048]{1,0:T(8,128)(2,1)S(1)}, bf16[144,2048]{1,0:T(8,128)(2,1)S(1)}, u32[]{:S(2)}, u32[]{:S(2)}) collective-permute-start(bf16[144,2048]{1,0:T(8,128)(2,1)S(1)} %collective-permute-done.refs_0_.refs_1_), channel_id=1, source_target_pairs={{0,2},{1,5},{2,0},{3,7},{4,6},{5,1},{6,4},{7,3},{8,10},{9,13},{10,... | collective-permute-start | bytes 1769480 | tf_op jit(solution)/shard_map/ppermute | solution.py:186
  25.3 1.6 collective-permute-start.1
  26.8 2.2 %collective-permute-done.6.refs_3_ = bf16[96,2048]{1,0:T(8,128)(2,1)S(1)} collective-permute-done((bf16[96,2048]{1,0:T(8,128)(2,1)S(1)}, bf16[96,2048]{1,0:T(8,128)(2,1)S(1)}, u32[]{:S(2)}, u32[]{:S(2)}) %collective-permute-start.6) | collective-permute-done | bytes 393248 | tf_op jit(solution)/shard_map/ppermute | solution.py:186
  29.0 1.9 %copy-done.5 = bf16[1,2048,768]{2,1,0:T(8,128)(2,1)S(1)} copy-done((bf16[1,2048,768]{2,1,0:T(8,128)(2,1)S(1)}, bf16[1,2048,768]{2,1,0:T(8,128)(2,1)}, u32[]{:S(2)}) %copy-start.5) | copy-done | bytes 3145752
  30.9 1.9 %copy-done.7 = bf16[1,768,2048]{2,1,0:T(8,128)(2,1)S(1)} copy-done((bf16[1,768,2048]{2,1,0:T(8,128)(2,1)S(1)}, bf16[1,768,2048]{2,1,0:T(8,128)(2,1)}, u32[]{:S(2)}) %copy-start.7) | copy-done | bytes 3145752
  32.8 3.8 %experts.4 = (bf16[96,2048]{1,0:T(8,128)(2,1)S(1)}, bf16[96,2048]{1,0:T(8,128)(2,1)S(1)}, bf16[96,2048]{1,0:T(8,128)(2,1)S(1)}, bf16[96,2048]{1,0:T(8,128)(2,1)S(1)}) custom-call(bf16[96,2048]{1,0:T(8,128)(2,1)S(1)} %get-tuple-element.78.refs_0_, bf16[96,2048]{1,0:T(8,128)(2,1)S(1)} %collective-permute-done.4.refs_1_, ...), custom_call_target="tpu_custom_call" | custom-call | flops 4000000000 | tf_op jit(solution)/shard_map/experts/pallas_call | solution.py:249
  36.7 1.1 select.25
  38.1 3.6 %collective-permute-done.1.refs_0_.refs_2_ = bf16[144,2048]{1,0:T(8,128)(2,1)S(1)} collective-permute-done((bf16[144,2048]{1,0:T(8,128)(2,1)S(1)}, bf16[144,2048]{1,0:T(8,128)(2,1)S(1)}, u32[]{:S(2)}, u32[]{:S(2)}) %collective-permute-start.1) | collective-permute-done | bytes 589856 | tf_op jit(solution)/shard_map/ppermute | solution.py:189
  41.7 1.5 collective-permute-start.9
  44.1 13.1 %collective-permute-done.2.refs_0_.refs_3_ = bf16[144,2048]{1,0:T(8,128)(2,1)S(1)} collective-permute-done((bf16[144,2048]{1,0:T(8,128)(2,1)S(1)}, bf16[144,2048]{1,0:T(8,128)(2,1)S(1)}, u32[]{:S(2)}, u32[]{:S(2)}) %collective-permute-start.2) | collective-permute-done | bytes 589856 | tf_op jit(solution)/shard_map/ppermute | solution.py:189
  57.2 0.7 collective-permute-done.9.refs_1_
  57.9 1.0 select.26
  59.1 2.0 %collective-permute-start.12 = (bf16[144,2048]{1,0:T(8,128)(2,1)S(1)}, bf16[144,2048]{1,0:T(8,128)(2,1)S(1)}, u32[]{:S(2)}, u32[]{:S(2)}) collective-permute-start(bf16[144,2048]{1,0:T(8,128)(2,1)S(1)} %collective-permute-done.2.refs_0_.refs_3_), channel_id=1, source_target_pairs={{0,2},{1,5},{2,0},{3,7},{4,6},{5,1},{6,4},{7,3},{8,10},{9,13},{10,... | collective-permute-start | bytes 1769480 | tf_op jit(solution)/shard_map/ppermute | solution.py:186
  61.2 0.8 collective-permute-start.17
  62.0 1.0 collective-permute-start.16
  63.0 3.8 %experts.5 = (bf16[96,2048]{1,0:T(8,128)(2,1)S(1)}, bf16[96,2048]{1,0:T(8,128)(2,1)S(1)}, bf16[96,2048]{1,0:T(8,128)(2,1)S(1)}, bf16[96,2048]{1,0:T(8,128)(2,1)S(1)}) custom-call(bf16[96,2048]{1,0:T(8,128)(2,1)S(1)} %get-tuple-element.90.refs_0_, bf16[96,2048]{1,0:T(8,128)(2,1)S(1)} %collective-permute-done.8.refs_1_, ...), custom_call_target="tpu_custom_call" | custom-call | flops 4000000000 | tf_op jit(solution)/shard_map/experts/pallas_call | solution.py:249
  67.0 5.7 %collective-permute-done.18.refs_3_ = bf16[96,2048]{1,0:T(8,128)(2,1)S(1)} collective-permute-done((bf16[96,2048]{1,0:T(8,128)(2,1)S(1)}, bf16[96,2048]{1,0:T(8,128)(2,1)S(1)}, u32[]{:S(2)}, u32[]{:S(2)}) %collective-permute-start.18) | collective-permute-done | bytes 393248 | tf_op jit(solution)/shard_map/ppermute | solution.py:186
  72.7 0.8 collective-permute-start.14
  73.4 1.4 collective-permute-done.12.refs_1_
  74.8 1.0 select.27
  75.9 2.5 %collective-permute-start.21 = (bf16[96,2048]{1,0:T(8,128)(2,1)S(1)}, bf16[96,2048]{1,0:T(8,128)(2,1)S(1)}, u32[]{:S(2)}, u32[]{:S(2)}) collective-permute-start(bf16[96,2048]{1,0:T(8,128)(2,1)S(1)} %get-tuple-element.114), channel_id=1, source_target_pairs={{0,5},{1,2},{2,7},{3,0},{4,1},{5,6},{6,3},{7,4},{8,13},{9,10},{10,... | collective-permute-start | bytes 1179656 | tf_op jit(solution)/shard_map/ppermute | solution.py:186
  78.4 0.8 collective-permute-start.20
  79.5 3.5 %collective-permute-done.14.refs_4_ = bf16[96,2048]{1,0:T(8,128)(2,1)S(1)} collective-permute-done((bf16[96,2048]{1,0:T(8,128)(2,1)S(1)}, bf16[96,2048]{1,0:T(8,128)(2,1)S(1)}, u32[]{:S(2)}, u32[]{:S(2)}) %collective-permute-start.14) | collective-permute-done | bytes 393248 | tf_op jit(solution)/shard_map/ppermute | solution.py:269
  83.0 3.3 %collective-permute-done.15.refs_5_ = bf16[96,2048]{1,0:T(8,128)(2,1)S(1)} collective-permute-done((bf16[96,2048]{1,0:T(8,128)(2,1)S(1)}, bf16[96,2048]{1,0:T(8,128)(2,1)S(1)}, u32[]{:S(2)}, u32[]{:S(2)}) %collective-permute-start.15) | collective-permute-done | bytes 393248 | tf_op jit(solution)/shard_map/ppermute | solution.py:269
  86.3 2.1 %combine.4 = (f32[128,2048]{1,0:T(8,128)S(1)}, bf16[128,2048]{1,0:T(8,128)(2,1)S(1)}) custom-call(f32[4,32]{1,0:T(4,128)S(1)} %compare_convert_fusion.groups_ref, bf16[32,2048]{1,0:T(8,128)(2,1)S(1)} %router.1.router_ref, bf16[144,2048]{1,0:T(8,128)(2,1)S(1)} %collective-permute-done.refs_0_.refs_1_, bf16[144,2048]{1,0:T(8,128)(2,1)S(1)} %collective-permute-done.7.refs_1_, ...), custom_call_target="tpu_custom_call" | custom-call | flops 2000000000 | tf_op jit(solution)/shard_map/combine/pallas_call | solution.py:272
  88.4 2.5 %collective-permute-start.22 = (bf16[128,2048]{1,0:T(8,128)(2,1)S(1)}, bf16[128,2048]{1,0:T(8,128)(2,1)S(1)}, u32[]{:S(2)}, u32[]{:S(2)}) collective-permute-start(bf16[128,2048]{1,0:T(8,128)(2,1)S(1)} %get-tuple-element.117), channel_id=1, source_target_pairs={{2,0},{5,1},{0,2},{7,3},{6,4},{1,5},{4,6},{3,7},{10,8},{13,9},{8,1... | collective-permute-start | bytes 1572872 | tf_op jit(solution)/shard_map/ppermute | solution.py:269
  90.9 3.8 %experts.6 = (bf16[96,2048]{1,0:T(8,128)(2,1)S(1)}, bf16[96,2048]{1,0:T(8,128)(2,1)S(1)}, bf16[96,2048]{1,0:T(8,128)(2,1)S(1)}, bf16[96,2048]{1,0:T(8,128)(2,1)S(1)}) custom-call(bf16[96,2048]{1,0:T(8,128)(2,1)S(1)} %get-tuple-element.100.refs_0_, bf16[96,2048]{1,0:T(8,128)(2,1)S(1)} %collective-permute-done.16.refs_1_, ...), custom_call_target="tpu_custom_call" | custom-call | flops 4000000000 | tf_op jit(solution)/shard_map/experts/pallas_call | solution.py:249
  94.8 0.7 collective-permute-start.24
  95.5 1.3 collective-permute-start.25
  96.8 3.8 %experts.7 = (bf16[96,2048]{1,0:T(8,128)(2,1)S(1)}, bf16[96,2048]{1,0:T(8,128)(2,1)S(1)}, bf16[96,2048]{1,0:T(8,128)(2,1)S(1)}, bf16[96,2048]{1,0:T(8,128)(2,1)S(1)}) custom-call(bf16[96,2048]{1,0:T(8,128)(2,1)S(1)} %get-tuple-element.108.refs_0_, bf16[96,2048]{1,0:T(8,128)(2,1)S(1)} %collective-permute-done.19.refs_1_, ...), custom_call_target="tpu_custom_call" | custom-call | flops 4000000000 | tf_op jit(solution)/shard_map/experts/pallas_call | solution.py:249
  101.0 1.2 collective-permute-done.22.refs_0_
  102.2 2.4 %collective-permute-start.28 = (bf16[128,2048]{1,0:T(8,128)(2,1)S(1)}, bf16[128,2048]{1,0:T(8,128)(2,1)S(1)}, u32[]{:S(2)}, u32[]{:S(2)}) collective-permute-start(bf16[128,2048]{1,0:T(8,128)(2,1)S(1)} %add.119), channel_id=1, source_target_pairs={{0,8},{8,16},{16,24},{24,0},{1,9},{9,17},{17,25},{25,1},{2,10},{10... | collective-permute-start | bytes 1572872 | tf_op jit(solution)/shard_map/ppermute | solution.py:189
  104.6 2.3 %collective-permute-done.24.refs_4_ = bf16[96,2048]{1,0:T(8,128)(2,1)S(1)} collective-permute-done((bf16[96,2048]{1,0:T(8,128)(2,1)S(1)}, bf16[96,2048]{1,0:T(8,128)(2,1)S(1)}, u32[]{:S(2)}, u32[]{:S(2)}) %collective-permute-start.24) | collective-permute-done | bytes 393248 | tf_op jit(solution)/shard_map/ppermute | solution.py:269
  107.4 2.1 %combine.5 = (f32[128,2048]{1,0:T(8,128)S(1)}, bf16[64,2048]{1,0:T(8,128)(2,1)S(1)}, bf16[64,2048]{1,0:T(8,128)(2,1)S(1)}) custom-call(f32[4,32]{1,0:T(4,128)S(1)} %compare_convert_fusion.groups_ref, bf16[32,2048]{1,0:T(8,128)(2,1)S(1)} %router.1.router_ref, bf16[144,2048]{1,0:T(8,128)(2,1)S(1)} %collective-permute-done.1.refs_0_.refs_2_, ...), custom_call_target="tpu_custom_call" | custom-call | flops 2000000000 | tf_op jit(solution)/shard_map/combine/pallas_call | solution.py:272
  109.5 1.2 collective-permute-start.30
  110.7 1.3 collective-permute-start.31
  112.0 1.2 collective-permute-start.26
  113.2 0.8 collective-permute-start.27
  114.0 10.5 %collective-permute-done.26.refs_0_ = bf16[64,2048]{1,0:T(8,128)(2,1)S(1)} collective-permute-done((bf16[64,2048]{1,0:T(8,128)(2,1)S(1)}, bf16[64,2048]{1,0:T(8,128)(2,1)S(1)}, u32[]{:S(2)}, u32[]{:S(2)}) %collective-permute-start.26) | collective-permute-done | bytes 262176 | tf_op jit(solution)/shard_map/ppermute | solution.py:269
  124.4 2.8 %collective-permute-done.27.refs_1_ = bf16[64,2048]{1,0:T(8,128)(2,1)S(1)} collective-permute-done((bf16[64,2048]{1,0:T(8,128)(2,1)S(1)}, bf16[64,2048]{1,0:T(8,128)(2,1)S(1)}, u32[]{:S(2)}, u32[]{:S(2)}) %collective-permute-start.27) | collective-permute-done | bytes 262176 | tf_op jit(solution)/shard_map/ppermute | solution.py:269
  127.5 1.6 %collective-permute-start.34 = (bf16[128,2048]{1,0:T(8,128)(2,1)S(1)}, bf16[128,2048]{1,0:T(8,128)(2,1)S(1)}, u32[]{:S(2)}, u32[]{:S(2)}) collective-permute-start(bf16[128,2048]{1,0:T(8,128)(2,1)S(1)} %add.120), channel_id=1, source_target_pairs={{0,8},{8,16},{16,24},{24,0},{1,9},{9,17},{17,25},{25,1},{2,10},{10... | collective-permute-start | bytes 1572872 | tf_op jit(solution)/shard_map/ppermute | solution.py:189
  129.1 2.1 %combine.6 = (f32[128,2048]{1,0:T(8,128)S(1)}, bf16[64,2048]{1,0:T(8,128)(2,1)S(1)}, bf16[64,2048]{1,0:T(8,128)(2,1)S(1)}) custom-call(f32[4,32]{1,0:T(4,128)S(1)} %compare_convert_fusion.groups_ref, bf16[32,2048]{1,0:T(8,128)(2,1)S(1)} %router.1.router_ref, bf16[144,2048]{1,0:T(8,128)(2,1)S(1)} %collective-permute-done.2.refs_0_.refs_3_, ...), custom_call_target="tpu_custom_call" | custom-call | flops 2000000000 | tf_op jit(solution)/shard_map/combine/pallas_call | solution.py:272
  131.2 1.5 collective-permute-start.32
  133.8 5.0 %collective-permute-done.32.refs_0_ = bf16[64,2048]{1,0:T(8,128)(2,1)S(1)} collective-permute-done((bf16[64,2048]{1,0:T(8,128)(2,1)S(1)}, bf16[64,2048]{1,0:T(8,128)(2,1)S(1)}, u32[]{:S(2)}, u32[]{:S(2)}) %collective-permute-start.32) | collective-permute-done | bytes 262176 | tf_op jit(solution)/shard_map/ppermute | solution.py:269
  138.8 5.6 %collective-permute-done.33.refs_1_ = bf16[64,2048]{1,0:T(8,128)(2,1)S(1)} collective-permute-done((bf16[64,2048]{1,0:T(8,128)(2,1)S(1)}, bf16[64,2048]{1,0:T(8,128)(2,1)S(1)}, u32[]{:S(2)}, u32[]{:S(2)}) %collective-permute-start.33) | collective-permute-done | bytes 262176 | tf_op jit(solution)/shard_map/ppermute | solution.py:269
  144.6 1.6 %collective-permute-start.40 = (bf16[128,2048]{1,0:T(8,128)(2,1)S(1)}, bf16[128,2048]{1,0:T(8,128)(2,1)S(1)}, u32[]{:S(2)}, u32[]{:S(2)}) collective-permute-start(bf16[128,2048]{1,0:T(8,128)(2,1)S(1)} %add.121), channel_id=1, source_target_pairs={{0,8},{8,16},{16,24},{24,0},{1,9},{9,17},{17,25},{25,1},{2,10},{10... | collective-permute-start | bytes 1572872 | tf_op jit(solution)/shard_map/ppermute | solution.py:189
  146.2 1.6 collective-permute-done.37.refs_5_
  147.8 2.1 %combine.7 = (f32[128,2048]{1,0:T(8,128)S(1)}, bf16[64,2048]{1,0:T(8,128)(2,1)S(1)}, bf16[64,2048]{1,0:T(8,128)(2,1)S(1)}) custom-call(f32[4,32]{1,0:T(4,128)S(1)} %compare_convert_fusion.groups_ref, bf16[32,2048]{1,0:T(8,128)(2,1)S(1)} %router.1.router_ref, bf16[144,2048]{1,0:T(8,128)(2,1)S(1)} %pack.1.refs_0_, ...), custom_call_target="tpu_custom_call" | custom-call | flops 2000000000 | tf_op jit(solution)/shard_map/combine/pallas_call | solution.py:272
  150.5 1.5 collective-permute-start.39
  152.0 4.3 %collective-permute-done.38.refs_0_ = bf16[64,2048]{1,0:T(8,128)(2,1)S(1)} collective-permute-done((bf16[64,2048]{1,0:T(8,128)(2,1)S(1)}, bf16[64,2048]{1,0:T(8,128)(2,1)S(1)}, u32[]{:S(2)}, u32[]{:S(2)}) %collective-permute-start.38) | collective-permute-done | bytes 262176 | tf_op jit(solution)/shard_map/ppermute | solution.py:269
  156.3 2.8 %collective-permute-done.39.refs_1_ = bf16[64,2048]{1,0:T(8,128)(2,1)S(1)} collective-permute-done((bf16[64,2048]{1,0:T(8,128)(2,1)S(1)}, bf16[64,2048]{1,0:T(8,128)(2,1)S(1)}, u32[]{:S(2)}, u32[]{:S(2)}) %collective-permute-start.39) | collective-permute-done | bytes 262176 | tf_op jit(solution)/shard_map/ppermute | solution.py:269
  159.1 1.0 add.122
  (54 shorter events, 5.4 us)
Async XLA Ops:
  0.0 1.0 copy-start
  1.0 0.8 copy-start.1
  1.8 0.7 copy-start.2
  2.5 0.7 copy-start.3
  3.4 10.9 %collective-permute-start.3 = (bf16[144,2048]{1,0:T(8,128)(2,1)S(1)}, bf16[144,2048]{1,0:T(8,128)(2,1)S(1)}, u32[]{:S(2)}, u32[]{:S(2)}) collective-permute-start(bf16[144,2048]{1,0:T(8,128)(2,1)S(1)} %pack.1.refs_0_), channel_id=1, source_target_pairs={{0,2},{1,5},{2,0},{3,7},{4,6},{5,1},{6,4},{7,3},{8,10},{9,13},{10,... | collective-permute-start | bytes 1769480 | tf_op jit(solution)/shard_map/ppermute | solution.py:186
  6.4 16.7 %collective-permute-start = (bf16[144,2048]{1,0:T(8,128)(2,1)S(1)}, bf16[144,2048]{1,0:T(8,128)(2,1)S(1)}, u32[]{:S(2)}, u32[]{:S(2)}) collective-permute-start(bf16[144,2048]{1,0:T(8,128)(2,1)S(1)} %pack.1.refs_0_), channel_id=1, source_target_pairs={{0,8},{8,16},{16,24},{24,0},{1,9},{9,17},{17,25},{25,1},{2,10},{10... | collective-permute-start | bytes 1769480 | tf_op jit(solution)/shard_map/ppermute | solution.py:189
  8.0 21.0 %copy-start.4 = (bf16[1,2048,768]{2,1,0:T(8,128)(2,1)S(1)}, bf16[1,2048,768]{2,1,0:T(8,128)(2,1)}, u32[]{:S(2)}) copy-start(bf16[1,2048,768]{2,1,0:T(8,128)(2,1)} %refs_4_.7) | copy-start | bytes 9437188
  15.3 7.8 %collective-permute-start.4 = (bf16[96,2048]{1,0:T(8,128)(2,1)S(1)}, bf16[96,2048]{1,0:T(8,128)(2,1)S(1)}, u32[]{:S(2)}, u32[]{:S(2)}) collective-permute-start(bf16[96,2048]{1,0:T(8,128)(2,1)S(1)} %get-tuple-element.75), channel_id=1, source_target_pairs={{0,1},{1,0},{2,3},{3,2},{4,5},{5,4},{6,7},{7,6},{8,9},{9,8},{10,11... | collective-permute-start | bytes 1179656 | tf_op jit(solution)/shard_map/ppermute | solution.py:186
  15.4 7.9 %collective-permute-start.5 = (bf16[96,2048]{1,0:T(8,128)(2,1)S(1)}, bf16[96,2048]{1,0:T(8,128)(2,1)S(1)}, u32[]{:S(2)}, u32[]{:S(2)}) collective-permute-start(bf16[96,2048]{1,0:T(8,128)(2,1)S(1)} %get-tuple-element.76), channel_id=1, source_target_pairs={{0,4},{1,3},{2,6},{3,1},{4,0},{5,7},{6,2},{7,5},{8,12},{9,11},{10,... | collective-permute-start | bytes 1179656 | tf_op jit(solution)/shard_map/ppermute | solution.py:186
  17.5 11.5 %collective-permute-start.6 = (bf16[96,2048]{1,0:T(8,128)(2,1)S(1)}, bf16[96,2048]{1,0:T(8,128)(2,1)S(1)}, u32[]{:S(2)}, u32[]{:S(2)}) collective-permute-start(bf16[96,2048]{1,0:T(8,128)(2,1)S(1)} %get-tuple-element.79), channel_id=1, source_target_pairs={{0,5},{1,2},{2,7},{3,0},{4,1},{5,6},{6,3},{7,4},{8,13},{9,10},{10,... | collective-permute-start | bytes 1179656 | tf_op jit(solution)/shard_map/ppermute | solution.py:186
  23.3 13.4 %collective-permute-start.7 = (bf16[144,2048]{1,0:T(8,128)(2,1)S(1)}, bf16[144,2048]{1,0:T(8,128)(2,1)S(1)}, u32[]{:S(2)}, u32[]{:S(2)}) collective-permute-start(bf16[144,2048]{1,0:T(8,128)(2,1)S(1)} %collective-permute-done.refs_0_.refs_1_), channel_id=1, source_target_pairs={{0,2},{1,5},{2,0},{3,7},{4,6},{5,1},{6,4},{7,3},{8,10},{9,13},{10,... | collective-permute-start | bytes 1769480 | tf_op jit(solution)/shard_map/ppermute | solution.py:186
  25.3 16.4 %collective-permute-start.1 = (bf16[144,2048]{1,0:T(8,128)(2,1)S(1)}, bf16[144,2048]{1,0:T(8,128)(2,1)S(1)}, u32[]{:S(2)}, u32[]{:S(2)}) collective-permute-start(bf16[144,2048]{1,0:T(8,128)(2,1)S(1)} %collective-permute-done.refs_0_.refs_1_), channel_id=1, source_target_pairs={{0,8},{8,16},{16,24},{24,0},{1,9},{9,17},{17,25},{25,1},{2,10},{10... | collective-permute-start | bytes 1769480 | tf_op jit(solution)/shard_map/ppermute | solution.py:189
  29.0 1.9 %copy-start.5 = (bf16[1,2048,768]{2,1,0:T(8,128)(2,1)S(1)}, bf16[1,2048,768]{2,1,0:T(8,128)(2,1)}, u32[]{:S(2)}) copy-start(bf16[1,2048,768]{2,1,0:T(8,128)(2,1)} %refs_5_.7) | copy-start | bytes 9437188
  30.9 1.9 %copy-start.7 = (bf16[1,768,2048]{2,1,0:T(8,128)(2,1)S(1)}, bf16[1,768,2048]{2,1,0:T(8,128)(2,1)}, u32[]{:S(2)}) copy-start(bf16[1,768,2048]{2,1,0:T(8,128)(2,1)} %refs_6_.7) | copy-start | bytes 9437188
  36.6 26.4 %copy-start.6 = (bf16[1,2048,768]{2,1,0:T(8,128)(2,1)S(1)}, bf16[1,2048,768]{2,1,0:T(8,128)(2,1)}, u32[]{:S(2)}) copy-start(bf16[1,2048,768]{2,1,0:T(8,128)(2,1)} %refs_5_.7) | copy-start | bytes 9437188
  37.7 4.0 %collective-permute-start.8 = (bf16[96,2048]{1,0:T(8,128)(2,1)S(1)}, bf16[96,2048]{1,0:T(8,128)(2,1)S(1)}, u32[]{:S(2)}, u32[]{:S(2)}) collective-permute-start(bf16[96,2048]{1,0:T(8,128)(2,1)S(1)} %get-tuple-element.83), channel_id=1, source_target_pairs={{0,1},{1,0},{2,3},{3,2},{4,5},{5,4},{6,7},{7,6},{8,9},{9,8},{10,11... | collective-permute-start | bytes 1179656 | tf_op jit(solution)/shard_map/ppermute | solution.py:186
  41.7 15.5 %collective-permute-start.2 = (bf16[144,2048]{1,0:T(8,128)(2,1)S(1)}, bf16[144,2048]{1,0:T(8,128)(2,1)S(1)}, u32[]{:S(2)}, u32[]{:S(2)}) collective-permute-start(bf16[144,2048]{1,0:T(8,128)(2,1)S(1)} %collective-permute-done.1.refs_0_.refs_2_), channel_id=1, source_target_pairs={{0,8},{8,16},{16,24},{24,0},{1,9},{9,17},{17,25},{25,1},{2,10},{10... | collective-permute-start | bytes 1769480 | tf_op jit(solution)/shard_map/ppermute | solution.py:189
  41.7 16.2 %collective-permute-start.9 = (bf16[144,2048]{1,0:T(8,128)(2,1)S(1)}, bf16[144,2048]{1,0:T(8,128)(2,1)S(1)}, u32[]{:S(2)}, u32[]{:S(2)}) collective-permute-start(bf16[144,2048]{1,0:T(8,128)(2,1)S(1)} %collective-permute-done.1.refs_0_.refs_2_), channel_id=1, source_target_pairs={{0,2},{1,5},{2,0},{3,7},{4,6},{5,1},{6,4},{7,3},{8,10},{9,13},{10,... | collective-permute-start | bytes 1769480 | tf_op jit(solution)/shard_map/ppermute | solution.py:186
  43.2 15.7 %collective-permute-start.10 = (bf16[96,2048]{1,0:T(8,128)(2,1)S(1)}, bf16[96,2048]{1,0:T(8,128)(2,1)S(1)}, u32[]{:S(2)}, u32[]{:S(2)}) collective-permute-start(bf16[96,2048]{1,0:T(8,128)(2,1)S(1)} %get-tuple-element.87), channel_id=1, source_target_pairs={{0,4},{1,3},{2,6},{3,1},{4,0},{5,7},{6,2},{7,5},{8,12},{9,11},{10,... | collective-permute-start | bytes 1179656 | tf_op jit(solution)/shard_map/ppermute | solution.py:186
  43.7 15.4 %collective-permute-start.11 = (bf16[96,2048]{1,0:T(8,128)(2,1)S(1)}, bf16[96,2048]{1,0:T(8,128)(2,1)S(1)}, u32[]{:S(2)}, u32[]{:S(2)}) collective-permute-start(bf16[96,2048]{1,0:T(8,128)(2,1)S(1)} %get-tuple-element.88), channel_id=1, source_target_pairs={{0,5},{1,2},{2,7},{3,0},{4,1},{5,6},{6,3},{7,4},{8,13},{9,10},{10,... | collective-permute-start | bytes 1179656 | tf_op jit(solution)/shard_map/ppermute | solution.py:186
  59.1 15.7 %collective-permute-start.12 = (bf16[144,2048]{1,0:T(8,128)(2,1)S(1)}, bf16[144,2048]{1,0:T(8,128)(2,1)S(1)}, u32[]{:S(2)}, u32[]{:S(2)}) collective-permute-start(bf16[144,2048]{1,0:T(8,128)(2,1)S(1)} %collective-permute-done.2.refs_0_.refs_3_), channel_id=1, source_target_pairs={{0,2},{1,5},{2,0},{3,7},{4,6},{5,1},{6,4},{7,3},{8,10},{9,13},{10,... | collective-permute-start | bytes 1769480 | tf_op jit(solution)/shard_map/ppermute | solution.py:186
  61.2 11.5 %collective-permute-start.18 = (bf16[96,2048]{1,0:T(8,128)(2,1)S(1)}, bf16[96,2048]{1,0:T(8,128)(2,1)S(1)}, u32[]{:S(2)}, u32[]{:S(2)}) collective-permute-start(bf16[96,2048]{1,0:T(8,128)(2,1)S(1)} %get-tuple-element.106), channel_id=1, source_target_pairs={{0,5},{1,2},{2,7},{3,0},{4,1},{5,6},{6,3},{7,4},{8,13},{9,10},{10,... | collective-permute-start | bytes 1179656 | tf_op jit(solution)/shard_map/ppermute | solution.py:186
  61.2 14.7 %collective-permute-start.17 = (bf16[96,2048]{1,0:T(8,128)(2,1)S(1)}, bf16[96,2048]{1,0:T(8,128)(2,1)S(1)}, u32[]{:S(2)}, u32[]{:S(2)}) collective-permute-start(bf16[96,2048]{1,0:T(8,128)(2,1)S(1)} %get-tuple-element.104), channel_id=1, source_target_pairs={{0,4},{1,3},{2,6},{3,1},{4,0},{5,7},{6,2},{7,5},{8,12},{9,11},{10,... | collective-permute-start | bytes 1179656 | tf_op jit(solution)/shard_map/ppermute | solution.py:186
  62.0 13.9 %collective-permute-start.16 = (bf16[96,2048]{1,0:T(8,128)(2,1)S(1)}, bf16[96,2048]{1,0:T(8,128)(2,1)S(1)}, u32[]{:S(2)}, u32[]{:S(2)}) collective-permute-start(bf16[96,2048]{1,0:T(8,128)(2,1)S(1)} %get-tuple-element.102), channel_id=1, source_target_pairs={{0,1},{1,0},{2,3},{3,2},{4,5},{5,4},{6,7},{7,6},{8,9},{9,8},{10,11... | collective-permute-start | bytes 1179656 | tf_op jit(solution)/shard_map/ppermute | solution.py:186
  66.9 12.3 %collective-permute-start.13 = (bf16[96,2048]{1,0:T(8,128)(2,1)S(1)}, bf16[96,2048]{1,0:T(8,128)(2,1)S(1)}, u32[]{:S(2)}, u32[]{:S(2)}) collective-permute-start(bf16[96,2048]{1,0:T(8,128)(2,1)S(1)} %get-tuple-element.96), channel_id=1, source_target_pairs={{1,0},{0,1},{3,2},{2,3},{5,4},{4,5},{7,6},{6,7},{9,8},{8,9},{11,10... | collective-permute-start | bytes 1179656 | tf_op jit(solution)/shard_map/ppermute | solution.py:269
  72.7 10.3 %collective-permute-start.14 = (bf16[96,2048]{1,0:T(8,128)(2,1)S(1)}, bf16[96,2048]{1,0:T(8,128)(2,1)S(1)}, u32[]{:S(2)}, u32[]{:S(2)}) collective-permute-start(bf16[96,2048]{1,0:T(8,128)(2,1)S(1)} %get-tuple-element.97), channel_id=1, source_target_pairs={{4,0},{3,1},{6,2},{1,3},{0,4},{7,5},{2,6},{5,7},{12,8},{11,9},{14,... | collective-permute-start | bytes 1179656 | tf_op jit(solution)/shard_map/ppermute | solution.py:269
  74.8 11.5 %collective-permute-start.15 = (bf16[96,2048]{1,0:T(8,128)(2,1)S(1)}, bf16[96,2048]{1,0:T(8,128)(2,1)S(1)}, u32[]{:S(2)}, u32[]{:S(2)}) collective-permute-start(bf16[96,2048]{1,0:T(8,128)(2,1)S(1)} %get-tuple-element.98), channel_id=1, source_target_pairs={{5,0},{2,1},{7,2},{0,3},{1,4},{6,5},{3,6},{4,7},{13,8},{10,9},{15,... | collective-permute-start | bytes 1179656 | tf_op jit(solution)/shard_map/ppermute | solution.py:269
  75.9 18.9 %collective-permute-start.21 = (bf16[96,2048]{1,0:T(8,128)(2,1)S(1)}, bf16[96,2048]{1,0:T(8,128)(2,1)S(1)}, u32[]{:S(2)}, u32[]{:S(2)}) collective-permute-start(bf16[96,2048]{1,0:T(8,128)(2,1)S(1)} %get-tuple-element.114), channel_id=1, source_target_pairs={{0,5},{1,2},{2,7},{3,0},{4,1},{5,6},{6,3},{7,4},{8,13},{9,10},{10,... | collective-permute-start | bytes 1179656 | tf_op jit(solution)/shard_map/ppermute | solution.py:186
  78.4 17.1 %collective-permute-start.20 = (bf16[96,2048]{1,0:T(8,128)(2,1)S(1)}, bf16[96,2048]{1,0:T(8,128)(2,1)S(1)}, u32[]{:S(2)}, u32[]{:S(2)}) collective-permute-start(bf16[96,2048]{1,0:T(8,128)(2,1)S(1)} %get-tuple-element.112), channel_id=1, source_target_pairs={{0,4},{1,3},{2,6},{3,1},{4,0},{5,7},{6,2},{7,5},{8,12},{9,11},{10,... | collective-permute-start | bytes 1179656 | tf_op jit(solution)/shard_map/ppermute | solution.py:186
  79.2 17.6 %collective-permute-start.19 = (bf16[96,2048]{1,0:T(8,128)(2,1)S(1)}, bf16[96,2048]{1,0:T(8,128)(2,1)S(1)}, u32[]{:S(2)}, u32[]{:S(2)}) collective-permute-start(bf16[96,2048]{1,0:T(8,128)(2,1)S(1)} %get-tuple-element.110), channel_id=1, source_target_pairs={{0,1},{1,0},{2,3},{3,2},{4,5},{5,4},{6,7},{7,6},{8,9},{9,8},{10,11... | collective-permute-start | bytes 1179656 | tf_op jit(solution)/shard_map/ppermute | solution.py:186
  88.4 13.8 %collective-permute-start.22 = (bf16[128,2048]{1,0:T(8,128)(2,1)S(1)}, bf16[128,2048]{1,0:T(8,128)(2,1)S(1)}, u32[]{:S(2)}, u32[]{:S(2)}) collective-permute-start(bf16[128,2048]{1,0:T(8,128)(2,1)S(1)} %get-tuple-element.117), channel_id=1, source_target_pairs={{2,0},{5,1},{0,2},{7,3},{6,4},{1,5},{4,6},{3,7},{10,8},{13,9},{8,1... | collective-permute-start | bytes 1572872 | tf_op jit(solution)/shard_map/ppermute | solution.py:269
  94.8 9.8 %collective-permute-start.23 = (bf16[96,2048]{1,0:T(8,128)(2,1)S(1)}, bf16[96,2048]{1,0:T(8,128)(2,1)S(1)}, u32[]{:S(2)}, u32[]{:S(2)}) collective-permute-start(bf16[96,2048]{1,0:T(8,128)(2,1)S(1)} %get-tuple-element.119), channel_id=1, source_target_pairs={{1,0},{0,1},{3,2},{2,3},{5,4},{4,5},{7,6},{6,7},{9,8},{8,9},{11,10... | collective-permute-start | bytes 1179656 | tf_op jit(solution)/shard_map/ppermute | solution.py:269
  94.8 12.1 %collective-permute-start.24 = (bf16[96,2048]{1,0:T(8,128)(2,1)S(1)}, bf16[96,2048]{1,0:T(8,128)(2,1)S(1)}, u32[]{:S(2)}, u32[]{:S(2)}) collective-permute-start(bf16[96,2048]{1,0:T(8,128)(2,1)S(1)} %get-tuple-element.120), channel_id=1, source_target_pairs={{4,0},{3,1},{6,2},{1,3},{0,4},{7,5},{2,6},{5,7},{12,8},{11,9},{14,... | collective-permute-start | bytes 1179656 | tf_op jit(solution)/shard_map/ppermute | solution.py:269
  95.5 11.9 %collective-permute-start.25 = (bf16[96,2048]{1,0:T(8,128)(2,1)S(1)}, bf16[96,2048]{1,0:T(8,128)(2,1)S(1)}, u32[]{:S(2)}, u32[]{:S(2)}) collective-permute-start(bf16[96,2048]{1,0:T(8,128)(2,1)S(1)} %get-tuple-element.121), channel_id=1, source_target_pairs={{5,0},{2,1},{7,2},{0,3},{1,4},{6,5},{3,6},{4,7},{13,8},{10,9},{15,... | collective-permute-start | bytes 1179656 | tf_op jit(solution)/shard_map/ppermute | solution.py:269
  100.7 8.8 %collective-permute-start.29 = (bf16[96,2048]{1,0:T(8,128)(2,1)S(1)}, bf16[96,2048]{1,0:T(8,128)(2,1)S(1)}, u32[]{:S(2)}, u32[]{:S(2)}) collective-permute-start(bf16[96,2048]{1,0:T(8,128)(2,1)S(1)} %get-tuple-element.127), channel_id=1, source_target_pairs={{1,0},{0,1},{3,2},{2,3},{5,4},{4,5},{7,6},{6,7},{9,8},{8,9},{11,10... | collective-permute-start | bytes 1179656 | tf_op jit(solution)/shard_map/ppermute | solution.py:269
  102.2 25.0 %collective-permute-start.28 = (bf16[128,2048]{1,0:T(8,128)(2,1)S(1)}, bf16[128,2048]{1,0:T(8,128)(2,1)S(1)}, u32[]{:S(2)}, u32[]{:S(2)}) collective-permute-start(bf16[128,2048]{1,0:T(8,128)(2,1)S(1)} %add.119), channel_id=1, source_target_pairs={{0,8},{8,16},{16,24},{24,0},{1,9},{9,17},{17,25},{25,1},{2,10},{10... | collective-permute-start | bytes 1572872 | tf_op jit(solution)/shard_map/ppermute | solution.py:189
  109.5 19.6 %collective-permute-start.30 = (bf16[96,2048]{1,0:T(8,128)(2,1)S(1)}, bf16[96,2048]{1,0:T(8,128)(2,1)S(1)}, u32[]{:S(2)}, u32[]{:S(2)}) collective-permute-start(bf16[96,2048]{1,0:T(8,128)(2,1)S(1)} %get-tuple-element.129), channel_id=1, source_target_pairs={{4,0},{3,1},{6,2},{1,3},{0,4},{7,5},{2,6},{5,7},{12,8},{11,9},{14,... | collective-permute-start | bytes 1179656 | tf_op jit(solution)/shard_map/ppermute | solution.py:269
  110.7 18.4 %collective-permute-start.31 = (bf16[96,2048]{1,0:T(8,128)(2,1)S(1)}, bf16[96,2048]{1,0:T(8,128)(2,1)S(1)}, u32[]{:S(2)}, u32[]{:S(2)}) collective-permute-start(bf16[96,2048]{1,0:T(8,128)(2,1)S(1)} %get-tuple-element.131), channel_id=1, source_target_pairs={{5,0},{2,1},{7,2},{0,3},{1,4},{6,5},{3,6},{4,7},{13,8},{10,9},{15,... | collective-permute-start | bytes 1179656 | tf_op jit(solution)/shard_map/ppermute | solution.py:269
  112.0 12.5 %collective-permute-start.26 = (bf16[64,2048]{1,0:T(8,128)(2,1)S(1)}, bf16[64,2048]{1,0:T(8,128)(2,1)S(1)}, u32[]{:S(2)}, u32[]{:S(2)}) collective-permute-start(bf16[64,2048]{1,0:T(8,128)(2,1)S(1)} %get-tuple-element.124), channel_id=1, source_target_pairs={{2,0},{5,1},{0,2},{7,3},{6,4},{1,5},{4,6},{3,7},{10,8},{13,9},{8,1... | collective-permute-start | bytes 786440 | tf_op jit(solution)/shard_map/ppermute | solution.py:269
  113.2 14.1 %collective-permute-start.27 = (bf16[64,2048]{1,0:T(8,128)(2,1)S(1)}, bf16[64,2048]{1,0:T(8,128)(2,1)S(1)}, u32[]{:S(2)}, u32[]{:S(2)}) collective-permute-start(bf16[64,2048]{1,0:T(8,128)(2,1)S(1)} %get-tuple-element.125), channel_id=1, source_target_pairs={{2,0},{5,1},{0,2},{7,3},{6,4},{1,5},{4,6},{3,7},{10,8},{13,9},{8,1... | collective-permute-start | bytes 786440 | tf_op jit(solution)/shard_map/ppermute | solution.py:269
  127.5 16.9 %collective-permute-start.34 = (bf16[128,2048]{1,0:T(8,128)(2,1)S(1)}, bf16[128,2048]{1,0:T(8,128)(2,1)S(1)}, u32[]{:S(2)}, u32[]{:S(2)}) collective-permute-start(bf16[128,2048]{1,0:T(8,128)(2,1)S(1)} %add.120), channel_id=1, source_target_pairs={{0,8},{8,16},{16,24},{24,0},{1,9},{9,17},{17,25},{25,1},{2,10},{10... | collective-permute-start | bytes 1572872 | tf_op jit(solution)/shard_map/ppermute | solution.py:189
  131.2 7.6 %collective-permute-start.32 = (bf16[64,2048]{1,0:T(8,128)(2,1)S(1)}, bf16[64,2048]{1,0:T(8,128)(2,1)S(1)}, u32[]{:S(2)}, u32[]{:S(2)}) collective-permute-start(bf16[64,2048]{1,0:T(8,128)(2,1)S(1)} %get-tuple-element.133), channel_id=1, source_target_pairs={{2,0},{5,1},{0,2},{7,3},{6,4},{1,5},{4,6},{3,7},{10,8},{13,9},{8,1... | collective-permute-start | bytes 786440 | tf_op jit(solution)/shard_map/ppermute | solution.py:269
  132.7 11.7 %collective-permute-start.33 = (bf16[64,2048]{1,0:T(8,128)(2,1)S(1)}, bf16[64,2048]{1,0:T(8,128)(2,1)S(1)}, u32[]{:S(2)}, u32[]{:S(2)}) collective-permute-start(bf16[64,2048]{1,0:T(8,128)(2,1)S(1)} %get-tuple-element.134), channel_id=1, source_target_pairs={{2,0},{5,1},{0,2},{7,3},{6,4},{1,5},{4,6},{3,7},{10,8},{13,9},{8,1... | collective-permute-start | bytes 786440 | tf_op jit(solution)/shard_map/ppermute | solution.py:269
  133.3 13.0 %collective-permute-start.35 = (bf16[96,2048]{1,0:T(8,128)(2,1)S(1)}, bf16[96,2048]{1,0:T(8,128)(2,1)S(1)}, u32[]{:S(2)}, u32[]{:S(2)}) collective-permute-start(bf16[96,2048]{1,0:T(8,128)(2,1)S(1)} %get-tuple-element.137), channel_id=1, source_target_pairs={{1,0},{0,1},{3,2},{2,3},{5,4},{4,5},{7,6},{6,7},{9,8},{8,9},{11,10... | collective-permute-start | bytes 1179656 | tf_op jit(solution)/shard_map/ppermute | solution.py:269
  133.3 13.0 %collective-permute-start.36 = (bf16[96,2048]{1,0:T(8,128)(2,1)S(1)}, bf16[96,2048]{1,0:T(8,128)(2,1)S(1)}, u32[]{:S(2)}, u32[]{:S(2)}) collective-permute-start(bf16[96,2048]{1,0:T(8,128)(2,1)S(1)} %get-tuple-element.139), channel_id=1, source_target_pairs={{4,0},{3,1},{6,2},{1,3},{0,4},{7,5},{2,6},{5,7},{12,8},{11,9},{14,... | collective-permute-start | bytes 1179656 | tf_op jit(solution)/shard_map/ppermute | solution.py:269
  138.8 9.0 %collective-permute-start.37 = (bf16[96,2048]{1,0:T(8,128)(2,1)S(1)}, bf16[96,2048]{1,0:T(8,128)(2,1)S(1)}, u32[]{:S(2)}, u32[]{:S(2)}) collective-permute-start(bf16[96,2048]{1,0:T(8,128)(2,1)S(1)} %get-tuple-element.141), channel_id=1, source_target_pairs={{5,0},{2,1},{7,2},{0,3},{1,4},{6,5},{3,6},{4,7},{13,8},{10,9},{15,... | collective-permute-start | bytes 1179656 | tf_op jit(solution)/shard_map/ppermute | solution.py:269
  144.6 14.6 %collective-permute-start.40 = (bf16[128,2048]{1,0:T(8,128)(2,1)S(1)}, bf16[128,2048]{1,0:T(8,128)(2,1)S(1)}, u32[]{:S(2)}, u32[]{:S(2)}) collective-permute-start(bf16[128,2048]{1,0:T(8,128)(2,1)S(1)} %add.121), channel_id=1, source_target_pairs={{0,8},{8,16},{16,24},{24,0},{1,9},{9,17},{17,25},{25,1},{2,10},{10... | collective-permute-start | bytes 1572872 | tf_op jit(solution)/shard_map/ppermute | solution.py:189
  149.9 6.4 %collective-permute-start.38 = (bf16[64,2048]{1,0:T(8,128)(2,1)S(1)}, bf16[64,2048]{1,0:T(8,128)(2,1)S(1)}, u32[]{:S(2)}, u32[]{:S(2)}) collective-permute-start(bf16[64,2048]{1,0:T(8,128)(2,1)S(1)} %get-tuple-element.143), channel_id=1, source_target_pairs={{2,0},{5,1},{0,2},{7,3},{6,4},{1,5},{4,6},{3,7},{10,8},{13,9},{8,1... | collective-permute-start | bytes 786440 | tf_op jit(solution)/shard_map/ppermute | solution.py:269
  150.5 8.6 %collective-permute-start.39 = (bf16[64,2048]{1,0:T(8,128)(2,1)S(1)}, bf16[64,2048]{1,0:T(8,128)(2,1)S(1)}, u32[]{:S(2)}, u32[]{:S(2)}) collective-permute-start(bf16[64,2048]{1,0:T(8,128)(2,1)S(1)} %get-tuple-element.144), channel_id=1, source_target_pairs={{2,0},{5,1},{0,2},{7,3},{6,4},{1,5},{4,6},{3,7},{10,8},{13,9},{8,1... | collective-permute-start | bytes 786440 | tf_op jit(solution)/shard_map/ppermute | solution.py:269

commit v2 on v1

--- a/solution.py
+++ b/solution.py
@@ -329,7 +329,7 @@
     def send_back(results, *others):
         back = [results[0]]
         for j in range(1, len(steps)):
-            rows_back = after(results[j], back[1], *others) if others and j > 1 else results[j]
+            rows_back = after(results[j], back[1], *others[min(j - 2, 1)]) if others and j > 1 else results[j]
             back.append(shift_back(rows_back, *steps[j], False))
         return back
 
@@ -347,6 +347,8 @@
         if i == 2:
             router_full = whole_router([after(sources[0], mark)] + sources[1:])
         if 1 < i < last:
+            if sums:
+                mark = add_chunk(sums, mark)
             mark, sums = combine_chunk(i - 1, 1, mark)
         arrived[0] = after(arrived[0], mark, *(back[i - 1][1:] if 1 < i < last else []))
         results = apply_experts(arrived)
@@ -357,11 +359,11 @@
             sent = select(blocks[1])
             mark = sent[0]
             here = send_rows(sent)
-            blocks.append(send_blocks(after(sources[2], mark, here[1])))
+            blocks.append(send_blocks(after(sources[2], mark, *here[1:3])))
         if i == last:
             mark = add_chunk(sums, mark)
             mark, sums = combine_chunk(i - 1, HALVES, mark)
-            back[last] = send_back(results, mark)
+            back[last] = send_back(results, [mark], [mark, *sums[1], *travelling])
     mark = add_chunk(sums, mark)
     mark, sums = combine_chunk(last, HALVES, mark)
     back[0] = send_back([back[0][0]] + [after(x, mark) for x in back[0][1:]])

time: 160 us -> 161 us (level)
  starting transfers between devices: 42.4 us -> 53 us
  waiting for transfers between devices: 80.1 us -> 70.2 us
    ppermute x19, waiting for transfers between devices: 43.4 us -> 28.8 us  [shift_back(): return lax.ppermute(array, 'expert', pairs)]
    ppermute x19, starting transfers between devices: 15 us -> 21.5 us  [shift_back(): return lax.ppermute(array, 'expert', pairs)]
    ppermute x16, waiting for transfers between devices: 15.7 us -> 20.2 us  [shift_owner(): lax.ppermute(array, 'expert', pairs if by >= 0 else [(b, a) for a, b in p...]
    ppermute x16, starting transfers between devices: 18.7 us -> 21.2 us  [shift_owner(): lax.ppermute(array, 'expert', pairs if by >= 0 else [(b, a) for a, b in p...]
  transfers between devices with their start and end apart: 41 -> 41, of which waited for: 22 -> 23; matrix products, arithmetic and copies ran while one was open for 1% -> 1% of each run, Pallas kernels for 18% -> 18%
where the time goes in v2:
time: 161 us
  waiting for transfers between devices  70.2 us (44%)
  starting transfers between devices  53 us (33%)
  Pallas kernels  29.4 us (18%)
  local copies, waits for them, and re-layouts  6.97 us (4%)
    ppermute x19, waiting for transfers between devices, shift_back(): return lax.ppermute(array, 'expert', pairs)  28.8 us
    ppermute x19, starting transfers between devices, shift_back(): return lax.ppermute(array, 'expert', pairs)  21.5 us
    ppermute x16, starting transfers between devices, shift_owner(): lax.ppermute(array, 'expert', pairs if by >= 0 else [(b, a) for a, b in p...  21.2 us
    ppermute x6, waiting for transfers between devices, shift_plane(): lax.ppermute(array, 'rep', [(r, (r + by) % reps) for r in range(reps)])  21.1 us
    ppermute x16, waiting for transfers between devices, shift_owner(): lax.ppermute(array, 'expert', pairs if by >= 0 else [(b, a) for a, b in p...  20.2 us
    pallas_call x4, Pallas kernels, apply_experts(): pl.pallas_call(functools.partial(experts_kernel, count), out_shape=[jax.S...  15.3 us
    ppermute x6, starting transfers between devices, shift_plane(): lax.ppermute(array, 'rep', [(r, (r + by) % reps) for r in range(reps)])  10.4 us
    pallas_call x4, Pallas kernels, combine(): pl.pallas_call(functools.partial(combine_kernel, rows, cap, top, dense, h...  8.22 us
  transfers between devices with their start and end apart: 41, of which 23 were waited for; matrix products, arithmetic and copies ran while one was open for 1% of the time, Pallas kernels for 18%

profile of v2, /device:TPU:0, one launch (start us, length us, event | category | flops | bytes accessed | tf_op | source)
XLA Modules:
  0.0 160.8 jit_solution(151493178665445230)
XLA Ops:
  0.0 1.0 copy-done
  1.0 0.8 copy-done.1
  1.8 0.7 copy-done.2
  2.5 0.7 copy-done.3
  3.4 3.0 %collective-permute-start.3 = (bf16[144,2048]{1,0:T(8,128)(2,1)S(1)}, bf16[144,2048]{1,0:T(8,128)(2,1)S(1)}, u32[]{:S(2)}, u32[]{:S(2)}) collective-permute-start(bf16[144,2048]{1,0:T(8,128)(2,1)S(1)} %pack.1.refs_0_), channel_id=1, source_target_pairs={{0,2},{1,5},{2,0},{3,7},{4,6},{5,1},{6,4},{7,3},{8,10},{9,13},{10,... | collective-permute-start | bytes 1769480 | tf_op jit(solution)/shard_map/ppermute | solution.py:186
  6.4 1.6 collective-permute-start
  8.1 0.9 compare_convert_fusion.groups_ref
  9.0 5.3 %collective-permute-done.3.refs_1_ = bf16[144,2048]{1,0:T(8,128)(2,1)S(1)} collective-permute-done((bf16[144,2048]{1,0:T(8,128)(2,1)S(1)}, bf16[144,2048]{1,0:T(8,128)(2,1)S(1)}, u32[]{:S(2)}, u32[]{:S(2)}) %collective-permute-start.3) | collective-permute-done | bytes 589856 | tf_op jit(solution)/shard_map/ppermute | solution.py:186
  14.3 1.0 select.24
  15.4 2.1 %collective-permute-start.5 = (bf16[96,2048]{1,0:T(8,128)(2,1)S(1)}, bf16[96,2048]{1,0:T(8,128)(2,1)S(1)}, u32[]{:S(2)}, u32[]{:S(2)}) collective-permute-start(bf16[96,2048]{1,0:T(8,128)(2,1)S(1)} %get-tuple-element.76), channel_id=1, source_target_pairs={{0,4},{1,3},{2,6},{3,1},{4,0},{5,7},{6,2},{7,5},{8,12},{9,11},{10,... | collective-permute-start | bytes 1179656 | tf_op jit(solution)/shard_map/ppermute | solution.py:186
  17.5 1.2 collective-permute-start.6
  18.8 4.3 %collective-permute-done.refs_0_.refs_1_ = bf16[144,2048]{1,0:T(8,128)(2,1)S(1)} collective-permute-done((bf16[144,2048]{1,0:T(8,128)(2,1)S(1)}, bf16[144,2048]{1,0:T(8,128)(2,1)S(1)}, u32[]{:S(2)}, u32[]{:S(2)}) %collective-permute-start) | collective-permute-done | bytes 589856 | tf_op jit(solution)/shard_map/ppermute | solution.py:189
  23.3 2.0 %collective-permute-start.7 = (bf16[144,2048]{1,0:T(8,128)(2,1)S(1)}, bf16[144,2048]{1,0:T(8,128)(2,1)S(1)}, u32[]{:S(2)}, u32[]{:S(2)}) collective-permute-start(bf16[144,2048]{1,0:T(8,128)(2,1)S(1)} %collective-permute-done.refs_0_.refs_1_), channel_id=1, source_target_pairs={{0,2},{1,5},{2,0},{3,7},{4,6},{5,1},{6,4},{7,3},{8,10},{9,13},{10,... | collective-permute-start | bytes 1769480 | tf_op jit(solution)/shard_map/ppermute | solution.py:186
  25.3 1.6 collective-permute-start.1
  26.8 2.2 %collective-permute-done.6.refs_3_ = bf16[96,2048]{1,0:T(8,128)(2,1)S(1)} collective-permute-done((bf16[96,2048]{1,0:T(8,128)(2,1)S(1)}, bf16[96,2048]{1,0:T(8,128)(2,1)S(1)}, u32[]{:S(2)}, u32[]{:S(2)}) %collective-permute-start.6) | collective-permute-done | bytes 393248 | tf_op jit(solution)/shard_map/ppermute | solution.py:186
  29.0 1.9 %copy-done.5 = bf16[1,2048,768]{2,1,0:T(8,128)(2,1)S(1)} copy-done((bf16[1,2048,768]{2,1,0:T(8,128)(2,1)S(1)}, bf16[1,2048,768]{2,1,0:T(8,128)(2,1)}, u32[]{:S(2)}) %copy-start.5) | copy-done | bytes 3145752
  30.9 1.9 %copy-done.7 = bf16[1,768,2048]{2,1,0:T(8,128)(2,1)S(1)} copy-done((bf16[1,768,2048]{2,1,0:T(8,128)(2,1)S(1)}, bf16[1,768,2048]{2,1,0:T(8,128)(2,1)}, u32[]{:S(2)}) %copy-start.7) | copy-done | bytes 3145752
  32.8 3.8 %experts.4 = (bf16[96,2048]{1,0:T(8,128)(2,1)S(1)}, bf16[96,2048]{1,0:T(8,128)(2,1)S(1)}, bf16[96,2048]{1,0:T(8,128)(2,1)S(1)}, bf16[96,2048]{1,0:T(8,128)(2,1)S(1)}) custom-call(bf16[96,2048]{1,0:T(8,128)(2,1)S(1)} %get-tuple-element.78.refs_0_, bf16[96,2048]{1,0:T(8,128)(2,1)S(1)} %collective-permute-done.4.refs_1_, ...), custom_call_target="tpu_custom_call" | custom-call | flops 4000000000 | tf_op jit(solution)/shard_map/experts/pallas_call | solution.py:249
  36.7 1.1 select.25
  38.1 2.3 %collective-permute-start.9 = (bf16[96,2048]{1,0:T(8,128)(2,1)S(1)}, bf16[96,2048]{1,0:T(8,128)(2,1)S(1)}, u32[]{:S(2)}, u32[]{:S(2)}) collective-permute-start(bf16[96,2048]{1,0:T(8,128)(2,1)S(1)} %get-tuple-element.84), channel_id=1, source_target_pairs={{0,4},{1,3},{2,6},{3,1},{4,0},{5,7},{6,2},{7,5},{8,12},{9,11},{10,... | collective-permute-start | bytes 1179656 | tf_op jit(solution)/shard_map/ppermute | solution.py:186
  40.4 1.3 collective-permute-done.1.refs_0_.refs_2_
  41.9 4.2 %collective-permute-done.9.refs_2_ = bf16[96,2048]{1,0:T(8,128)(2,1)S(1)} collective-permute-done((bf16[96,2048]{1,0:T(8,128)(2,1)S(1)}, bf16[96,2048]{1,0:T(8,128)(2,1)S(1)}, u32[]{:S(2)}, u32[]{:S(2)}) %collective-permute-start.9) | collective-permute-done | bytes 393248 | tf_op jit(solution)/shard_map/ppermute | solution.py:186
  46.1 2.0 %collective-permute-start.10 = (bf16[144,2048]{1,0:T(8,128)(2,1)S(1)}, bf16[144,2048]{1,0:T(8,128)(2,1)S(1)}, u32[]{:S(2)}, u32[]{:S(2)}) collective-permute-start(bf16[144,2048]{1,0:T(8,128)(2,1)S(1)} %collective-permute-done.1.refs_0_.refs_2_), channel_id=1, source_target_pairs={{0,2},{1,5},{2,0},{3,7},{4,6},{5,1},{6,4},{7,3},{8,10},{9,13},{10,... | collective-permute-start | bytes 1769480 | tf_op jit(solution)/shard_map/ppermute | solution.py:186
  48.1 9.1 %collective-permute-done.2.refs_0_.refs_3_ = bf16[144,2048]{1,0:T(8,128)(2,1)S(1)} collective-permute-done((bf16[144,2048]{1,0:T(8,128)(2,1)S(1)}, bf16[144,2048]{1,0:T(8,128)(2,1)S(1)}, u32[]{:S(2)}, u32[]{:S(2)}) %collective-permute-start.2) | collective-permute-done | bytes 589856 | tf_op jit(solution)/shard_map/ppermute | solution.py:189
  57.2 3.0 %collective-permute-done.10.refs_1_ = bf16[144,2048]{1,0:T(8,128)(2,1)S(1)} collective-permute-done((bf16[144,2048]{1,0:T(8,128)(2,1)S(1)}, bf16[144,2048]{1,0:T(8,128)(2,1)S(1)}, u32[]{:S(2)}, u32[]{:S(2)}) %collective-permute-start.10) | collective-permute-done | bytes 589856 | tf_op jit(solution)/shard_map/ppermute | solution.py:186
  60.2 1.0 select.26
  61.3 1.5 collective-permute-start.12
  62.8 2.0 %collective-permute-start.17 = (bf16[96,2048]{1,0:T(8,128)(2,1)S(1)}, bf16[96,2048]{1,0:T(8,128)(2,1)S(1)}, u32[]{:S(2)}, u32[]{:S(2)}) collective-permute-start(bf16[96,2048]{1,0:T(8,128)(2,1)S(1)} %get-tuple-element.104), channel_id=1, source_target_pairs={{0,4},{1,3},{2,6},{3,1},{4,0},{5,7},{6,2},{7,5},{8,12},{9,11},{10,... | collective-permute-start | bytes 1179656 | tf_op jit(solution)/shard_map/ppermute | solution.py:186
  64.8 3.8 %experts.5 = (bf16[96,2048]{1,0:T(8,128)(2,1)S(1)}, bf16[96,2048]{1,0:T(8,128)(2,1)S(1)}, bf16[96,2048]{1,0:T(8,128)(2,1)S(1)}, bf16[96,2048]{1,0:T(8,128)(2,1)S(1)}) custom-call(bf16[96,2048]{1,0:T(8,128)(2,1)S(1)} %get-tuple-element.90.refs_0_, bf16[96,2048]{1,0:T(8,128)(2,1)S(1)} %collective-permute-done.8.refs_1_, ...), custom_call_target="tpu_custom_call" | custom-call | flops 4000000000 | tf_op jit(solution)/shard_map/experts/pallas_call | solution.py:249
  69.2 5.0 %collective-permute-done.18.refs_3_ = bf16[96,2048]{1,0:T(8,128)(2,1)S(1)} collective-permute-done((bf16[96,2048]{1,0:T(8,128)(2,1)S(1)}, bf16[96,2048]{1,0:T(8,128)(2,1)S(1)}, u32[]{:S(2)}, u32[]{:S(2)}) %collective-permute-start.18) | collective-permute-done | bytes 393248 | tf_op jit(solution)/shard_map/ppermute | solution.py:186
  74.2 2.0 %collective-permute-start.14 = (bf16[96,2048]{1,0:T(8,128)(2,1)S(1)}, bf16[96,2048]{1,0:T(8,128)(2,1)S(1)}, u32[]{:S(2)}, u32[]{:S(2)}) collective-permute-start(bf16[96,2048]{1,0:T(8,128)(2,1)S(1)} %get-tuple-element.97), channel_id=1, source_target_pairs={{4,0},{3,1},{6,2},{1,3},{0,4},{7,5},{2,6},{5,7},{12,8},{11,9},{14,... | collective-permute-start | bytes 1179656 | tf_op jit(solution)/shard_map/ppermute | solution.py:269
  76.7 1.0 select.27
  77.7 3.7 %collective-permute-start.21 = (bf16[96,2048]{1,0:T(8,128)(2,1)S(1)}, bf16[96,2048]{1,0:T(8,128)(2,1)S(1)}, u32[]{:S(2)}, u32[]{:S(2)}) collective-permute-start(bf16[96,2048]{1,0:T(8,128)(2,1)S(1)} %get-tuple-element.114), channel_id=1, source_target_pairs={{0,5},{1,2},{2,7},{3,0},{4,1},{5,6},{6,3},{7,4},{8,13},{9,10},{10,... | collective-permute-start | bytes 1179656 | tf_op jit(solution)/shard_map/ppermute | solution.py:186
  82.3 1.9 %collective-permute-done.14.refs_4_ = bf16[96,2048]{1,0:T(8,128)(2,1)S(1)} collective-permute-done((bf16[96,2048]{1,0:T(8,128)(2,1)S(1)}, bf16[96,2048]{1,0:T(8,128)(2,1)S(1)}, u32[]{:S(2)}, u32[]{:S(2)}) %collective-permute-start.14) | collective-permute-done | bytes 393248 | tf_op jit(solution)/shard_map/ppermute | solution.py:269
  84.2 3.9 %collective-permute-done.15.refs_5_ = bf16[96,2048]{1,0:T(8,128)(2,1)S(1)} collective-permute-done((bf16[96,2048]{1,0:T(8,128)(2,1)S(1)}, bf16[96,2048]{1,0:T(8,128)(2,1)S(1)}, u32[]{:S(2)}, u32[]{:S(2)}) %collective-permute-start.15) | collective-permute-done | bytes 393248 | tf_op jit(solution)/shard_map/ppermute | solution.py:269
  88.1 2.1 %combine.4 = (f32[128,2048]{1,0:T(8,128)S(1)}, bf16[128,2048]{1,0:T(8,128)(2,1)S(1)}) custom-call(f32[4,32]{1,0:T(4,128)S(1)} %compare_convert_fusion.groups_ref, bf16[32,2048]{1,0:T(8,128)(2,1)S(1)} %router.1.router_ref, bf16[144,2048]{1,0:T(8,128)(2,1)S(1)} %collective-permute-done.refs_0_.refs_1_, bf16[144,2048]{1,0:T(8,128)(2,1)S(1)} %collective-permute-done.7.refs_1_, ...), custom_call_target="tpu_custom_call" | custom-call | flops 2000000000 | tf_op jit(solution)/shard_map/combine/pallas_call | solution.py:272
  90.2 1.2 collective-permute-start.22
  91.4 3.8 %experts.6 = (bf16[96,2048]{1,0:T(8,128)(2,1)S(1)}, bf16[96,2048]{1,0:T(8,128)(2,1)S(1)}, bf16[96,2048]{1,0:T(8,128)(2,1)S(1)}, bf16[96,2048]{1,0:T(8,128)(2,1)S(1)}) custom-call(bf16[96,2048]{1,0:T(8,128)(2,1)S(1)} %get-tuple-element.100.refs_0_, bf16[96,2048]{1,0:T(8,128)(2,1)S(1)} %collective-permute-done.16.refs_1_, ...), custom_call_target="tpu_custom_call" | custom-call | flops 4000000000 | tf_op jit(solution)/shard_map/experts/pallas_call | solution.py:249
  95.2 1.7 %collective-permute-start.23 = (bf16[96,2048]{1,0:T(8,128)(2,1)S(1)}, bf16[96,2048]{1,0:T(8,128)(2,1)S(1)}, u32[]{:S(2)}, u32[]{:S(2)}) collective-permute-start(bf16[96,2048]{1,0:T(8,128)(2,1)S(1)} %get-tuple-element.119), channel_id=1, source_target_pairs={{1,0},{0,1},{3,2},{2,3},{5,4},{4,5},{7,6},{6,7},{9,8},{8,9},{11,10... | collective-permute-start | bytes 1179656 | tf_op jit(solution)/shard_map/ppermute | solution.py:269
  97.2 3.4 %collective-permute-start.25 = (bf16[96,2048]{1,0:T(8,128)(2,1)S(1)}, bf16[96,2048]{1,0:T(8,128)(2,1)S(1)}, u32[]{:S(2)}, u32[]{:S(2)}) collective-permute-start(bf16[96,2048]{1,0:T(8,128)(2,1)S(1)} %get-tuple-element.121), channel_id=1, source_target_pairs={{5,0},{2,1},{7,2},{0,3},{1,4},{6,5},{3,6},{4,7},{13,8},{10,9},{15,... | collective-permute-start | bytes 1179656 | tf_op jit(solution)/shard_map/ppermute | solution.py:269
  100.6 3.8 %experts.7 = (bf16[96,2048]{1,0:T(8,128)(2,1)S(1)}, bf16[96,2048]{1,0:T(8,128)(2,1)S(1)}, bf16[96,2048]{1,0:T(8,128)(2,1)S(1)}, bf16[96,2048]{1,0:T(8,128)(2,1)S(1)}) custom-call(bf16[96,2048]{1,0:T(8,128)(2,1)S(1)} %get-tuple-element.108.refs_0_, bf16[96,2048]{1,0:T(8,128)(2,1)S(1)} %collective-permute-done.19.refs_1_, ...), custom_call_target="tpu_custom_call" | custom-call | flops 4000000000 | tf_op jit(solution)/shard_map/experts/pallas_call | solution.py:249
  104.7 2.6 %collective-permute-start.28 = (bf16[128,2048]{1,0:T(8,128)(2,1)S(1)}, bf16[128,2048]{1,0:T(8,128)(2,1)S(1)}, u32[]{:S(2)}, u32[]{:S(2)}) collective-permute-start(bf16[128,2048]{1,0:T(8,128)(2,1)S(1)} %add.119), channel_id=1, source_target_pairs={{0,8},{8,16},{16,24},{24,0},{1,9},{9,17},{17,25},{25,1},{2,10},{10... | collective-permute-start | bytes 1572872 | tf_op jit(solution)/shard_map/ppermute | solution.py:189
  107.3 2.2 %collective-permute-done.25.refs_5_ = bf16[96,2048]{1,0:T(8,128)(2,1)S(1)} collective-permute-done((bf16[96,2048]{1,0:T(8,128)(2,1)S(1)}, bf16[96,2048]{1,0:T(8,128)(2,1)S(1)}, u32[]{:S(2)}, u32[]{:S(2)}) %collective-permute-start.25) | collective-permute-done | bytes 393248 | tf_op jit(solution)/shard_map/ppermute | solution.py:269
  109.5 2.1 %combine.5 = (f32[128,2048]{1,0:T(8,128)S(1)}, bf16[64,2048]{1,0:T(8,128)(2,1)S(1)}, bf16[64,2048]{1,0:T(8,128)(2,1)S(1)}) custom-call(f32[4,32]{1,0:T(4,128)S(1)} %compare_convert_fusion.groups_ref, bf16[32,2048]{1,0:T(8,128)(2,1)S(1)} %router.1.router_ref, bf16[144,2048]{1,0:T(8,128)(2,1)S(1)} %collective-permute-done.1.refs_0_.refs_2_, ...), custom_call_target="tpu_custom_call" | custom-call | flops 2000000000 | tf_op jit(solution)/shard_map/combine/pallas_call | solution.py:272
  112.2 1.5 collective-permute-start.27
  113.7 2.0 %collective-permute-start.30 = (bf16[96,2048]{1,0:T(8,128)(2,1)S(1)}, bf16[96,2048]{1,0:T(8,128)(2,1)S(1)}, u32[]{:S(2)}, u32[]{:S(2)}) collective-permute-start(bf16[96,2048]{1,0:T(8,128)(2,1)S(1)} %get-tuple-element.129), channel_id=1, source_target_pairs={{4,0},{3,1},{6,2},{1,3},{0,4},{7,5},{2,6},{5,7},{12,8},{11,9},{14,... | collective-permute-start | bytes 1179656 | tf_op jit(solution)/shard_map/ppermute | solution.py:269
  115.7 3.4 %collective-permute-done.26.refs_0_ = bf16[64,2048]{1,0:T(8,128)(2,1)S(1)} collective-permute-done((bf16[64,2048]{1,0:T(8,128)(2,1)S(1)}, bf16[64,2048]{1,0:T(8,128)(2,1)S(1)}, u32[]{:S(2)}, u32[]{:S(2)}) %collective-permute-start.26) | collective-permute-done | bytes 262176 | tf_op jit(solution)/shard_map/ppermute | solution.py:269
  119.4 2.3 %collective-permute-start.31 = (bf16[96,2048]{1,0:T(8,128)(2,1)S(1)}, bf16[96,2048]{1,0:T(8,128)(2,1)S(1)}, u32[]{:S(2)}, u32[]{:S(2)}) collective-permute-start(bf16[96,2048]{1,0:T(8,128)(2,1)S(1)} %get-tuple-element.131), channel_id=1, source_target_pairs={{5,0},{2,1},{7,2},{0,3},{1,4},{6,5},{3,6},{4,7},{13,8},{10,9},{15,... | collective-permute-start | bytes 1179656 | tf_op jit(solution)/shard_map/ppermute | solution.py:269
  121.8 2.9 %collective-permute-done.27.refs_1_ = bf16[64,2048]{1,0:T(8,128)(2,1)S(1)} collective-permute-done((bf16[64,2048]{1,0:T(8,128)(2,1)S(1)}, bf16[64,2048]{1,0:T(8,128)(2,1)S(1)}, u32[]{:S(2)}, u32[]{:S(2)}) %collective-permute-start.27) | collective-permute-done | bytes 262176 | tf_op jit(solution)/shard_map/ppermute | solution.py:269
  124.9 2.2 %collective-permute-start.34 = (bf16[128,2048]{1,0:T(8,128)(2,1)S(1)}, bf16[128,2048]{1,0:T(8,128)(2,1)S(1)}, u32[]{:S(2)}, u32[]{:S(2)}) collective-permute-start(bf16[128,2048]{1,0:T(8,128)(2,1)S(1)} %add.120), channel_id=1, source_target_pairs={{0,8},{8,16},{16,24},{24,0},{1,9},{9,17},{17,25},{25,1},{2,10},{10... | collective-permute-start | bytes 1572872 | tf_op jit(solution)/shard_map/ppermute | solution.py:189
  127.0 2.4 %collective-permute-done.31.refs_5_ = bf16[96,2048]{1,0:T(8,128)(2,1)S(1)} collective-permute-done((bf16[96,2048]{1,0:T(8,128)(2,1)S(1)}, bf16[96,2048]{1,0:T(8,128)(2,1)S(1)}, u32[]{:S(2)}, u32[]{:S(2)}) %collective-permute-start.31) | collective-permute-done | bytes 393248 | tf_op jit(solution)/shard_map/ppermute | solution.py:269
  129.4 2.1 %combine.6 = (f32[128,2048]{1,0:T(8,128)S(1)}, bf16[64,2048]{1,0:T(8,128)(2,1)S(1)}, bf16[64,2048]{1,0:T(8,128)(2,1)S(1)}) custom-call(f32[4,32]{1,0:T(4,128)S(1)} %compare_convert_fusion.groups_ref, bf16[32,2048]{1,0:T(8,128)(2,1)S(1)} %router.1.router_ref, bf16[144,2048]{1,0:T(8,128)(2,1)S(1)} %collective-permute-done.2.refs_0_.refs_3_, ...), custom_call_target="tpu_custom_call" | custom-call | flops 2000000000 | tf_op jit(solution)/shard_map/combine/pallas_call | solution.py:272
  131.5 1.8 %collective-permute-start.32 = (bf16[64,2048]{1,0:T(8,128)(2,1)S(1)}, bf16[64,2048]{1,0:T(8,128)(2,1)S(1)}, u32[]{:S(2)}, u32[]{:S(2)}) collective-permute-start(bf16[64,2048]{1,0:T(8,128)(2,1)S(1)} %get-tuple-element.133), channel_id=1, source_target_pairs={{2,0},{5,1},{0,2},{7,3},{6,4},{1,5},{4,6},{3,7},{10,8},{13,9},{8,1... | collective-permute-start | bytes 786440 | tf_op jit(solution)/shard_map/ppermute | solution.py:269
  133.6 1.7 %collective-permute-start.36 = (bf16[96,2048]{1,0:T(8,128)(2,1)S(1)}, bf16[96,2048]{1,0:T(8,128)(2,1)S(1)}, u32[]{:S(2)}, u32[]{:S(2)}) collective-permute-start(bf16[96,2048]{1,0:T(8,128)(2,1)S(1)} %get-tuple-element.139), channel_id=1, source_target_pairs={{4,0},{3,1},{6,2},{1,3},{0,4},{7,5},{2,6},{5,7},{12,8},{11,9},{14,... | collective-permute-start | bytes 1179656 | tf_op jit(solution)/shard_map/ppermute | solution.py:269
  135.3 6.0 %collective-permute-done.34.refs_2_ = bf16[128,2048]{1,0:T(8,128)(2,1)S(1)} collective-permute-done((bf16[128,2048]{1,0:T(8,128)(2,1)S(1)}, bf16[128,2048]{1,0:T(8,128)(2,1)S(1)}, u32[]{:S(2)}, u32[]{:S(2)}) %collective-permute-start.34) | collective-permute-done | bytes 524320 | tf_op jit(solution)/shard_map/ppermute | solution.py:189
  141.3 3.4 %collective-permute-done.33.refs_1_ = bf16[64,2048]{1,0:T(8,128)(2,1)S(1)} collective-permute-done((bf16[64,2048]{1,0:T(8,128)(2,1)S(1)}, bf16[64,2048]{1,0:T(8,128)(2,1)S(1)}, u32[]{:S(2)}, u32[]{:S(2)}) %collective-permute-start.33) | collective-permute-done | bytes 262176 | tf_op jit(solution)/shard_map/ppermute | solution.py:269
  144.9 2.2 %collective-permute-start.40 = (bf16[128,2048]{1,0:T(8,128)(2,1)S(1)}, bf16[128,2048]{1,0:T(8,128)(2,1)S(1)}, u32[]{:S(2)}, u32[]{:S(2)}) collective-permute-start(bf16[128,2048]{1,0:T(8,128)(2,1)S(1)} %add.121), channel_id=1, source_target_pairs={{0,8},{8,16},{16,24},{24,0},{1,9},{9,17},{17,25},{25,1},{2,10},{10... | collective-permute-start | bytes 1572872 | tf_op jit(solution)/shard_map/ppermute | solution.py:189
  147.0 1.4 collective-permute-done.37.refs_5_
  148.5 2.1 %combine.7 = (f32[128,2048]{1,0:T(8,128)S(1)}, bf16[64,2048]{1,0:T(8,128)(2,1)S(1)}, bf16[64,2048]{1,0:T(8,128)(2,1)S(1)}) custom-call(f32[4,32]{1,0:T(4,128)S(1)} %compare_convert_fusion.groups_ref, bf16[32,2048]{1,0:T(8,128)(2,1)S(1)} %router.1.router_ref, bf16[144,2048]{1,0:T(8,128)(2,1)S(1)} %pack.1.refs_0_, ...), custom_call_target="tpu_custom_call" | custom-call | flops 2000000000 | tf_op jit(solution)/shard_map/combine/pallas_call | solution.py:272
  150.5 0.9 collective-permute-start.38
  151.4 1.2 collective-permute-start.39
  152.6 4.3 %collective-permute-done.38.refs_0_ = bf16[64,2048]{1,0:T(8,128)(2,1)S(1)} collective-permute-done((bf16[64,2048]{1,0:T(8,128)(2,1)S(1)}, bf16[64,2048]{1,0:T(8,128)(2,1)S(1)}, u32[]{:S(2)}, u32[]{:S(2)}) %collective-permute-start.38) | collective-permute-done | bytes 262176 | tf_op jit(solution)/shard_map/ppermute | solution.py:269
  157.0 2.8 %collective-permute-done.39.refs_1_ = bf16[64,2048]{1,0:T(8,128)(2,1)S(1)} collective-permute-done((bf16[64,2048]{1,0:T(8,128)(2,1)S(1)}, bf16[64,2048]{1,0:T(8,128)(2,1)S(1)}, u32[]{:S(2)}, u32[]{:S(2)}) %collective-permute-start.39) | collective-permute-done | bytes 262176 | tf_op jit(solution)/shard_map/ppermute | solution.py:269
  159.8 1.0 add.122
  (54 shorter events, 5.5 us)
Async XLA Ops:
  0.0 1.0 copy-start
  1.0 0.8 copy-start.1
  1.8 0.7 copy-start.2
  2.5 0.7 copy-start.3
  3.4 10.9 %collective-permute-start.3 = (bf16[144,2048]{1,0:T(8,128)(2,1)S(1)}, bf16[144,2048]{1,0:T(8,128)(2,1)S(1)}, u32[]{:S(2)}, u32[]{:S(2)}) collective-permute-start(bf16[144,2048]{1,0:T(8,128)(2,1)S(1)} %pack.1.refs_0_), channel_id=1, source_target_pairs={{0,2},{1,5},{2,0},{3,7},{4,6},{5,1},{6,4},{7,3},{8,10},{9,13},{10,... | collective-permute-start | bytes 1769480 | tf_op jit(solution)/shard_map/ppermute | solution.py:186
  6.4 16.7 %collective-permute-start = (bf16[144,2048]{1,0:T(8,128)(2,1)S(1)}, bf16[144,2048]{1,0:T(8,128)(2,1)S(1)}, u32[]{:S(2)}, u32[]{:S(2)}) collective-permute-start(bf16[144,2048]{1,0:T(8,128)(2,1)S(1)} %pack.1.refs_0_), channel_id=1, source_target_pairs={{0,8},{8,16},{16,24},{24,0},{1,9},{9,17},{17,25},{25,1},{2,10},{10... | collective-permute-start | bytes 1769480 | tf_op jit(solution)/shard_map/ppermute | solution.py:189
  8.0 21.0 %copy-start.4 = (bf16[1,2048,768]{2,1,0:T(8,128)(2,1)S(1)}, bf16[1,2048,768]{2,1,0:T(8,128)(2,1)}, u32[]{:S(2)}) copy-start(bf16[1,2048,768]{2,1,0:T(8,128)(2,1)} %refs_4_.7) | copy-start | bytes 9437188
  15.3 7.8 %collective-permute-start.4 = (bf16[96,2048]{1,0:T(8,128)(2,1)S(1)}, bf16[96,2048]{1,0:T(8,128)(2,1)S(1)}, u32[]{:S(2)}, u32[]{:S(2)}) collective-permute-start(bf16[96,2048]{1,0:T(8,128)(2,1)S(1)} %get-tuple-element.75), channel_id=1, source_target_pairs={{0,1},{1,0},{2,3},{3,2},{4,5},{5,4},{6,7},{7,6},{8,9},{9,8},{10,11... | collective-permute-start | bytes 1179656 | tf_op jit(solution)/shard_map/ppermute | solution.py:186
  15.4 7.9 %collective-permute-start.5 = (bf16[96,2048]{1,0:T(8,128)(2,1)S(1)}, bf16[96,2048]{1,0:T(8,128)(2,1)S(1)}, u32[]{:S(2)}, u32[]{:S(2)}) collective-permute-start(bf16[96,2048]{1,0:T(8,128)(2,1)S(1)} %get-tuple-element.76), channel_id=1, source_target_pairs={{0,4},{1,3},{2,6},{3,1},{4,0},{5,7},{6,2},{7,5},{8,12},{9,11},{10,... | collective-permute-start | bytes 1179656 | tf_op jit(solution)/shard_map/ppermute | solution.py:186
  17.5 11.5 %collective-permute-start.6 = (bf16[96,2048]{1,0:T(8,128)(2,1)S(1)}, bf16[96,2048]{1,0:T(8,128)(2,1)S(1)}, u32[]{:S(2)}, u32[]{:S(2)}) collective-permute-start(bf16[96,2048]{1,0:T(8,128)(2,1)S(1)} %get-tuple-element.79), channel_id=1, source_target_pairs={{0,5},{1,2},{2,7},{3,0},{4,1},{5,6},{6,3},{7,4},{8,13},{9,10},{10,... | collective-permute-start | bytes 1179656 | tf_op jit(solution)/shard_map/ppermute | solution.py:186
  23.3 13.4 %collective-permute-start.7 = (bf16[144,2048]{1,0:T(8,128)(2,1)S(1)}, bf16[144,2048]{1,0:T(8,128)(2,1)S(1)}, u32[]{:S(2)}, u32[]{:S(2)}) collective-permute-start(bf16[144,2048]{1,0:T(8,128)(2,1)S(1)} %collective-permute-done.refs_0_.refs_1_), channel_id=1, source_target_pairs={{0,2},{1,5},{2,0},{3,7},{4,6},{5,1},{6,4},{7,3},{8,10},{9,13},{10,... | collective-permute-start | bytes 1769480 | tf_op jit(solution)/shard_map/ppermute | solution.py:186
  25.3 16.4 %collective-permute-start.1 = (bf16[144,2048]{1,0:T(8,128)(2,1)S(1)}, bf16[144,2048]{1,0:T(8,128)(2,1)S(1)}, u32[]{:S(2)}, u32[]{:S(2)}) collective-permute-start(bf16[144,2048]{1,0:T(8,128)(2,1)S(1)} %collective-permute-done.refs_0_.refs_1_), channel_id=1, source_target_pairs={{0,8},{8,16},{16,24},{24,0},{1,9},{9,17},{17,25},{25,1},{2,10},{10... | collective-permute-start | bytes 1769480 | tf_op jit(solution)/shard_map/ppermute | solution.py:189
  29.0 1.9 %copy-start.5 = (bf16[1,2048,768]{2,1,0:T(8,128)(2,1)S(1)}, bf16[1,2048,768]{2,1,0:T(8,128)(2,1)}, u32[]{:S(2)}) copy-start(bf16[1,2048,768]{2,1,0:T(8,128)(2,1)} %refs_5_.7) | copy-start | bytes 9437188
  30.9 1.9 %copy-start.7 = (bf16[1,768,2048]{2,1,0:T(8,128)(2,1)S(1)}, bf16[1,768,2048]{2,1,0:T(8,128)(2,1)}, u32[]{:S(2)}) copy-start(bf16[1,768,2048]{2,1,0:T(8,128)(2,1)} %refs_6_.7) | copy-start | bytes 9437188
  36.6 28.2 %copy-start.6 = (bf16[1,2048,768]{2,1,0:T(8,128)(2,1)S(1)}, bf16[1,2048,768]{2,1,0:T(8,128)(2,1)}, u32[]{:S(2)}) copy-start(bf16[1,2048,768]{2,1,0:T(8,128)(2,1)} %refs_5_.7) | copy-start | bytes 9437188
  37.7 4.2 %collective-permute-start.8 = (bf16[96,2048]{1,0:T(8,128)(2,1)S(1)}, bf16[96,2048]{1,0:T(8,128)(2,1)S(1)}, u32[]{:S(2)}, u32[]{:S(2)}) collective-permute-start(bf16[96,2048]{1,0:T(8,128)(2,1)S(1)} %get-tuple-element.83), channel_id=1, source_target_pairs={{0,1},{1,0},{2,3},{3,2},{4,5},{5,4},{6,7},{7,6},{8,9},{9,8},{10,11... | collective-permute-start | bytes 1179656 | tf_op jit(solution)/shard_map/ppermute | solution.py:186
  38.1 8.1 %collective-permute-start.9 = (bf16[96,2048]{1,0:T(8,128)(2,1)S(1)}, bf16[96,2048]{1,0:T(8,128)(2,1)S(1)}, u32[]{:S(2)}, u32[]{:S(2)}) collective-permute-start(bf16[96,2048]{1,0:T(8,128)(2,1)S(1)} %get-tuple-element.84), channel_id=1, source_target_pairs={{0,4},{1,3},{2,6},{3,1},{4,0},{5,7},{6,2},{7,5},{8,12},{9,11},{10,... | collective-permute-start | bytes 1179656 | tf_op jit(solution)/shard_map/ppermute | solution.py:186
  41.7 15.6 %collective-permute-start.2 = (bf16[144,2048]{1,0:T(8,128)(2,1)S(1)}, bf16[144,2048]{1,0:T(8,128)(2,1)S(1)}, u32[]{:S(2)}, u32[]{:S(2)}) collective-permute-start(bf16[144,2048]{1,0:T(8,128)(2,1)S(1)} %collective-permute-done.1.refs_0_.refs_2_), channel_id=1, source_target_pairs={{0,8},{8,16},{16,24},{24,0},{1,9},{9,17},{17,25},{25,1},{2,10},{10... | collective-permute-start | bytes 1769480 | tf_op jit(solution)/shard_map/ppermute | solution.py:189
  46.1 14.1 %collective-permute-start.10 = (bf16[144,2048]{1,0:T(8,128)(2,1)S(1)}, bf16[144,2048]{1,0:T(8,128)(2,1)S(1)}, u32[]{:S(2)}, u32[]{:S(2)}) collective-permute-start(bf16[144,2048]{1,0:T(8,128)(2,1)S(1)} %collective-permute-done.1.refs_0_.refs_2_), channel_id=1, source_target_pairs={{0,2},{1,5},{2,0},{3,7},{4,6},{5,1},{6,4},{7,3},{8,10},{9,13},{10,... | collective-permute-start | bytes 1769480 | tf_op jit(solution)/shard_map/ppermute | solution.py:186
  48.1 13.1 %collective-permute-start.11 = (bf16[96,2048]{1,0:T(8,128)(2,1)S(1)}, bf16[96,2048]{1,0:T(8,128)(2,1)S(1)}, u32[]{:S(2)}, u32[]{:S(2)}) collective-permute-start(bf16[96,2048]{1,0:T(8,128)(2,1)S(1)} %get-tuple-element.88), channel_id=1, source_target_pairs={{0,5},{1,2},{2,7},{3,0},{4,1},{5,6},{6,3},{7,4},{8,13},{9,10},{10,... | collective-permute-start | bytes 1179656 | tf_op jit(solution)/shard_map/ppermute | solution.py:186
  61.3 15.4 %collective-permute-start.12 = (bf16[144,2048]{1,0:T(8,128)(2,1)S(1)}, bf16[144,2048]{1,0:T(8,128)(2,1)S(1)}, u32[]{:S(2)}, u32[]{:S(2)}) collective-permute-start(bf16[144,2048]{1,0:T(8,128)(2,1)S(1)} %collective-permute-done.2.refs_0_.refs_3_), channel_id=1, source_target_pairs={{0,2},{1,5},{2,0},{3,7},{4,6},{5,1},{6,4},{7,3},{8,10},{9,13},{10,... | collective-permute-start | bytes 1769480 | tf_op jit(solution)/shard_map/ppermute | solution.py:186
  62.8 11.4 %collective-permute-start.18 = (bf16[96,2048]{1,0:T(8,128)(2,1)S(1)}, bf16[96,2048]{1,0:T(8,128)(2,1)S(1)}, u32[]{:S(2)}, u32[]{:S(2)}) collective-permute-start(bf16[96,2048]{1,0:T(8,128)(2,1)S(1)} %get-tuple-element.106), channel_id=1, source_target_pairs={{0,5},{1,2},{2,7},{3,0},{4,1},{5,6},{6,3},{7,4},{8,13},{9,10},{10,... | collective-permute-start | bytes 1179656 | tf_op jit(solution)/shard_map/ppermute | solution.py:186
  62.8 14.9 %collective-permute-start.17 = (bf16[96,2048]{1,0:T(8,128)(2,1)S(1)}, bf16[96,2048]{1,0:T(8,128)(2,1)S(1)}, u32[]{:S(2)}, u32[]{:S(2)}) collective-permute-start(bf16[96,2048]{1,0:T(8,128)(2,1)S(1)} %get-tuple-element.104), channel_id=1, source_target_pairs={{0,4},{1,3},{2,6},{3,1},{4,0},{5,7},{6,2},{7,5},{8,12},{9,11},{10,... | collective-permute-start | bytes 1179656 | tf_op jit(solution)/shard_map/ppermute | solution.py:186
  64.8 12.9 %collective-permute-start.16 = (bf16[96,2048]{1,0:T(8,128)(2,1)S(1)}, bf16[96,2048]{1,0:T(8,128)(2,1)S(1)}, u32[]{:S(2)}, u32[]{:S(2)}) collective-permute-start(bf16[96,2048]{1,0:T(8,128)(2,1)S(1)} %get-tuple-element.102), channel_id=1, source_target_pairs={{0,1},{1,0},{2,3},{3,2},{4,5},{5,4},{6,7},{7,6},{8,9},{9,8},{10,11... | collective-permute-start | bytes 1179656 | tf_op jit(solution)/shard_map/ppermute | solution.py:186
  68.7 13.1 %collective-permute-start.13 = (bf16[96,2048]{1,0:T(8,128)(2,1)S(1)}, bf16[96,2048]{1,0:T(8,128)(2,1)S(1)}, u32[]{:S(2)}, u32[]{:S(2)}) collective-permute-start(bf16[96,2048]{1,0:T(8,128)(2,1)S(1)} %get-tuple-element.96), channel_id=1, source_target_pairs={{1,0},{0,1},{3,2},{2,3},{5,4},{4,5},{7,6},{6,7},{9,8},{8,9},{11,10... | collective-permute-start | bytes 1179656 | tf_op jit(solution)/shard_map/ppermute | solution.py:269
  74.2 10.0 %collective-permute-start.14 = (bf16[96,2048]{1,0:T(8,128)(2,1)S(1)}, bf16[96,2048]{1,0:T(8,128)(2,1)S(1)}, u32[]{:S(2)}, u32[]{:S(2)}) collective-permute-start(bf16[96,2048]{1,0:T(8,128)(2,1)S(1)} %get-tuple-element.97), channel_id=1, source_target_pairs={{4,0},{3,1},{6,2},{1,3},{0,4},{7,5},{2,6},{5,7},{12,8},{11,9},{14,... | collective-permute-start | bytes 1179656 | tf_op jit(solution)/shard_map/ppermute | solution.py:269
  76.7 11.5 %collective-permute-start.15 = (bf16[96,2048]{1,0:T(8,128)(2,1)S(1)}, bf16[96,2048]{1,0:T(8,128)(2,1)S(1)}, u32[]{:S(2)}, u32[]{:S(2)}) collective-permute-start(bf16[96,2048]{1,0:T(8,128)(2,1)S(1)} %get-tuple-element.98), channel_id=1, source_target_pairs={{5,0},{2,1},{7,2},{0,3},{1,4},{6,5},{3,6},{4,7},{13,8},{10,9},{15,... | collective-permute-start | bytes 1179656 | tf_op jit(solution)/shard_map/ppermute | solution.py:269
  77.7 19.2 %collective-permute-start.21 = (bf16[96,2048]{1,0:T(8,128)(2,1)S(1)}, bf16[96,2048]{1,0:T(8,128)(2,1)S(1)}, u32[]{:S(2)}, u32[]{:S(2)}) collective-permute-start(bf16[96,2048]{1,0:T(8,128)(2,1)S(1)} %get-tuple-element.114), channel_id=1, source_target_pairs={{0,5},{1,2},{2,7},{3,0},{4,1},{5,6},{6,3},{7,4},{8,13},{9,10},{10,... | collective-permute-start | bytes 1179656 | tf_op jit(solution)/shard_map/ppermute | solution.py:186
  81.4 15.8 %collective-permute-start.20 = (bf16[96,2048]{1,0:T(8,128)(2,1)S(1)}, bf16[96,2048]{1,0:T(8,128)(2,1)S(1)}, u32[]{:S(2)}, u32[]{:S(2)}) collective-permute-start(bf16[96,2048]{1,0:T(8,128)(2,1)S(1)} %get-tuple-element.112), channel_id=1, source_target_pairs={{0,4},{1,3},{2,6},{3,1},{4,0},{5,7},{6,2},{7,5},{8,12},{9,11},{10,... | collective-permute-start | bytes 1179656 | tf_op jit(solution)/shard_map/ppermute | solution.py:186
  81.7 18.8 %collective-permute-start.19 = (bf16[96,2048]{1,0:T(8,128)(2,1)S(1)}, bf16[96,2048]{1,0:T(8,128)(2,1)S(1)}, u32[]{:S(2)}, u32[]{:S(2)}) collective-permute-start(bf16[96,2048]{1,0:T(8,128)(2,1)S(1)} %get-tuple-element.110), channel_id=1, source_target_pairs={{0,1},{1,0},{2,3},{3,2},{4,5},{5,4},{6,7},{7,6},{8,9},{9,8},{10,11... | collective-permute-start | bytes 1179656 | tf_op jit(solution)/shard_map/ppermute | solution.py:186
  90.2 14.4 %collective-permute-start.22 = (bf16[128,2048]{1,0:T(8,128)(2,1)S(1)}, bf16[128,2048]{1,0:T(8,128)(2,1)S(1)}, u32[]{:S(2)}, u32[]{:S(2)}) collective-permute-start(bf16[128,2048]{1,0:T(8,128)(2,1)S(1)} %get-tuple-element.117), channel_id=1, source_target_pairs={{2,0},{5,1},{0,2},{7,3},{6,4},{1,5},{4,6},{3,7},{10,8},{13,9},{8,1... | collective-permute-start | bytes 1572872 | tf_op jit(solution)/shard_map/ppermute | solution.py:269
  95.2 12.1 %collective-permute-start.23 = (bf16[96,2048]{1,0:T(8,128)(2,1)S(1)}, bf16[96,2048]{1,0:T(8,128)(2,1)S(1)}, u32[]{:S(2)}, u32[]{:S(2)}) collective-permute-start(bf16[96,2048]{1,0:T(8,128)(2,1)S(1)} %get-tuple-element.119), channel_id=1, source_target_pairs={{1,0},{0,1},{3,2},{2,3},{5,4},{4,5},{7,6},{6,7},{9,8},{8,9},{11,10... | collective-permute-start | bytes 1179656 | tf_op jit(solution)/shard_map/ppermute | solution.py:269
  96.9 10.4 %collective-permute-start.24 = (bf16[96,2048]{1,0:T(8,128)(2,1)S(1)}, bf16[96,2048]{1,0:T(8,128)(2,1)S(1)}, u32[]{:S(2)}, u32[]{:S(2)}) collective-permute-start(bf16[96,2048]{1,0:T(8,128)(2,1)S(1)} %get-tuple-element.120), channel_id=1, source_target_pairs={{4,0},{3,1},{6,2},{1,3},{0,4},{7,5},{2,6},{5,7},{12,8},{11,9},{14,... | collective-permute-start | bytes 1179656 | tf_op jit(solution)/shard_map/ppermute | solution.py:269
  97.2 12.3 %collective-permute-start.25 = (bf16[96,2048]{1,0:T(8,128)(2,1)S(1)}, bf16[96,2048]{1,0:T(8,128)(2,1)S(1)}, u32[]{:S(2)}, u32[]{:S(2)}) collective-permute-start(bf16[96,2048]{1,0:T(8,128)(2,1)S(1)} %get-tuple-element.121), channel_id=1, source_target_pairs={{5,0},{2,1},{7,2},{0,3},{1,4},{6,5},{3,6},{4,7},{13,8},{10,9},{15,... | collective-permute-start | bytes 1179656 | tf_op jit(solution)/shard_map/ppermute | solution.py:269
  104.7 14.8 %collective-permute-start.28 = (bf16[128,2048]{1,0:T(8,128)(2,1)S(1)}, bf16[128,2048]{1,0:T(8,128)(2,1)S(1)}, u32[]{:S(2)}, u32[]{:S(2)}) collective-permute-start(bf16[128,2048]{1,0:T(8,128)(2,1)S(1)} %add.119), channel_id=1, source_target_pairs={{0,8},{8,16},{16,24},{24,0},{1,9},{9,17},{17,25},{25,1},{2,10},{10... | collective-permute-start | bytes 1572872 | tf_op jit(solution)/shard_map/ppermute | solution.py:189
  107.3 6.4 %collective-permute-start.29 = (bf16[96,2048]{1,0:T(8,128)(2,1)S(1)}, bf16[96,2048]{1,0:T(8,128)(2,1)S(1)}, u32[]{:S(2)}, u32[]{:S(2)}) collective-permute-start(bf16[96,2048]{1,0:T(8,128)(2,1)S(1)} %get-tuple-element.127), channel_id=1, source_target_pairs={{1,0},{0,1},{3,2},{2,3},{5,4},{4,5},{7,6},{6,7},{9,8},{8,9},{11,10... | collective-permute-start | bytes 1179656 | tf_op jit(solution)/shard_map/ppermute | solution.py:269
  111.6 7.5 %collective-permute-start.26 = (bf16[64,2048]{1,0:T(8,128)(2,1)S(1)}, bf16[64,2048]{1,0:T(8,128)(2,1)S(1)}, u32[]{:S(2)}, u32[]{:S(2)}) collective-permute-start(bf16[64,2048]{1,0:T(8,128)(2,1)S(1)} %get-tuple-element.124), channel_id=1, source_target_pairs={{2,0},{5,1},{0,2},{7,3},{6,4},{1,5},{4,6},{3,7},{10,8},{13,9},{8,1... | collective-permute-start | bytes 786440 | tf_op jit(solution)/shard_map/ppermute | solution.py:269
  112.2 12.4 %collective-permute-start.27 = (bf16[64,2048]{1,0:T(8,128)(2,1)S(1)}, bf16[64,2048]{1,0:T(8,128)(2,1)S(1)}, u32[]{:S(2)}, u32[]{:S(2)}) collective-permute-start(bf16[64,2048]{1,0:T(8,128)(2,1)S(1)} %get-tuple-element.125), channel_id=1, source_target_pairs={{2,0},{5,1},{0,2},{7,3},{6,4},{1,5},{4,6},{3,7},{10,8},{13,9},{8,1... | collective-permute-start | bytes 786440 | tf_op jit(solution)/shard_map/ppermute | solution.py:269
  113.7 13.4 %collective-permute-start.30 = (bf16[96,2048]{1,0:T(8,128)(2,1)S(1)}, bf16[96,2048]{1,0:T(8,128)(2,1)S(1)}, u32[]{:S(2)}, u32[]{:S(2)}) collective-permute-start(bf16[96,2048]{1,0:T(8,128)(2,1)S(1)} %get-tuple-element.129), channel_id=1, source_target_pairs={{4,0},{3,1},{6,2},{1,3},{0,4},{7,5},{2,6},{5,7},{12,8},{11,9},{14,... | collective-permute-start | bytes 1179656 | tf_op jit(solution)/shard_map/ppermute | solution.py:269
  119.4 10.0 %collective-permute-start.31 = (bf16[96,2048]{1,0:T(8,128)(2,1)S(1)}, bf16[96,2048]{1,0:T(8,128)(2,1)S(1)}, u32[]{:S(2)}, u32[]{:S(2)}) collective-permute-start(bf16[96,2048]{1,0:T(8,128)(2,1)S(1)} %get-tuple-element.131), channel_id=1, source_target_pairs={{5,0},{2,1},{7,2},{0,3},{1,4},{6,5},{3,6},{4,7},{13,8},{10,9},{15,... | collective-permute-start | bytes 1179656 | tf_op jit(solution)/shard_map/ppermute | solution.py:269
  124.9 16.4 %collective-permute-start.34 = (bf16[128,2048]{1,0:T(8,128)(2,1)S(1)}, bf16[128,2048]{1,0:T(8,128)(2,1)S(1)}, u32[]{:S(2)}, u32[]{:S(2)}) collective-permute-start(bf16[128,2048]{1,0:T(8,128)(2,1)S(1)} %add.120), channel_id=1, source_target_pairs={{0,8},{8,16},{16,24},{24,0},{1,9},{9,17},{17,25},{25,1},{2,10},{10... | collective-permute-start | bytes 1572872 | tf_op jit(solution)/shard_map/ppermute | solution.py:189
  131.5 9.8 %collective-permute-start.32 = (bf16[64,2048]{1,0:T(8,128)(2,1)S(1)}, bf16[64,2048]{1,0:T(8,128)(2,1)S(1)}, u32[]{:S(2)}, u32[]{:S(2)}) collective-permute-start(bf16[64,2048]{1,0:T(8,128)(2,1)S(1)} %get-tuple-element.133), channel_id=1, source_target_pairs={{2,0},{5,1},{0,2},{7,3},{6,4},{1,5},{4,6},{3,7},{10,8},{13,9},{8,1... | collective-permute-start | bytes 786440 | tf_op jit(solution)/shard_map/ppermute | solution.py:269
  133.3 11.4 %collective-permute-start.33 = (bf16[64,2048]{1,0:T(8,128)(2,1)S(1)}, bf16[64,2048]{1,0:T(8,128)(2,1)S(1)}, u32[]{:S(2)}, u32[]{:S(2)}) collective-permute-start(bf16[64,2048]{1,0:T(8,128)(2,1)S(1)} %get-tuple-element.134), channel_id=1, source_target_pairs={{2,0},{5,1},{0,2},{7,3},{6,4},{1,5},{4,6},{3,7},{10,8},{13,9},{8,1... | collective-permute-start | bytes 786440 | tf_op jit(solution)/shard_map/ppermute | solution.py:269
  133.6 13.5 %collective-permute-start.35 = (bf16[96,2048]{1,0:T(8,128)(2,1)S(1)}, bf16[96,2048]{1,0:T(8,128)(2,1)S(1)}, u32[]{:S(2)}, u32[]{:S(2)}) collective-permute-start(bf16[96,2048]{1,0:T(8,128)(2,1)S(1)} %get-tuple-element.137), channel_id=1, source_target_pairs={{1,0},{0,1},{3,2},{2,3},{5,4},{4,5},{7,6},{6,7},{9,8},{8,9},{11,10... | collective-permute-start | bytes 1179656 | tf_op jit(solution)/shard_map/ppermute | solution.py:269
  133.6 13.5 %collective-permute-start.36 = (bf16[96,2048]{1,0:T(8,128)(2,1)S(1)}, bf16[96,2048]{1,0:T(8,128)(2,1)S(1)}, u32[]{:S(2)}, u32[]{:S(2)}) collective-permute-start(bf16[96,2048]{1,0:T(8,128)(2,1)S(1)} %get-tuple-element.139), channel_id=1, source_target_pairs={{4,0},{3,1},{6,2},{1,3},{0,4},{7,5},{2,6},{5,7},{12,8},{11,9},{14,... | collective-permute-start | bytes 1179656 | tf_op jit(solution)/shard_map/ppermute | solution.py:269
  141.3 7.2 %collective-permute-start.37 = (bf16[96,2048]{1,0:T(8,128)(2,1)S(1)}, bf16[96,2048]{1,0:T(8,128)(2,1)S(1)}, u32[]{:S(2)}, u32[]{:S(2)}) collective-permute-start(bf16[96,2048]{1,0:T(8,128)(2,1)S(1)} %get-tuple-element.141), channel_id=1, source_target_pairs={{5,0},{2,1},{7,2},{0,3},{1,4},{6,5},{3,6},{4,7},{13,8},{10,9},{15,... | collective-permute-start | bytes 1179656 | tf_op jit(solution)/shard_map/ppermute | solution.py:269
  144.9 14.9 %collective-permute-start.40 = (bf16[128,2048]{1,0:T(8,128)(2,1)S(1)}, bf16[128,2048]{1,0:T(8,128)(2,1)S(1)}, u32[]{:S(2)}, u32[]{:S(2)}) collective-permute-start(bf16[128,2048]{1,0:T(8,128)(2,1)S(1)} %add.121), channel_id=1, source_target_pairs={{0,8},{8,16},{16,24},{24,0},{1,9},{9,17},{17,25},{25,1},{2,10},{10... | collective-permute-start | bytes 1572872 | tf_op jit(solution)/shard_map/ppermute | solution.py:189
  150.5 6.4 %collective-permute-start.38 = (bf16[64,2048]{1,0:T(8,128)(2,1)S(1)}, bf16[64,2048]{1,0:T(8,128)(2,1)S(1)}, u32[]{:S(2)}, u32[]{:S(2)}) collective-permute-start(bf16[64,2048]{1,0:T(8,128)(2,1)S(1)} %get-tuple-element.143), channel_id=1, source_target_pairs={{2,0},{5,1},{0,2},{7,3},{6,4},{1,5},{4,6},{3,7},{10,8},{13,9},{8,1... | collective-permute-start | bytes 786440 | tf_op jit(solution)/shard_map/ppermute | solution.py:269
  151.4 8.4 %collective-permute-start.39 = (bf16[64,2048]{1,0:T(8,128)(2,1)S(1)}, bf16[64,2048]{1,0:T(8,128)(2,1)S(1)}, u32[]{:S(2)}, u32[]{:S(2)}) collective-permute-start(bf16[64,2048]{1,0:T(8,128)(2,1)S(1)} %get-tuple-element.144), channel_id=1, source_target_pairs={{2,0},{5,1},{0,2},{7,3},{6,4},{1,5},{4,6},{3,7},{10,8},{13,9},{8,1... | collective-permute-start | bytes 786440 | tf_op jit(solution)/shard_map/ppermute | solution.py:269

commit v3 on v2

--- a/solution.py
+++ b/solution.py
@@ -359,7 +359,7 @@
             sent = select(blocks[1])
             mark = sent[0]
             here = send_rows(sent)
-            blocks.append(send_blocks(after(sources[2], mark, *here[1:3])))
+            blocks.append(send_blocks(after(sources[2], mark, here[1])))
         if i == last:
             mark = add_chunk(sums, mark)
             mark, sums = combine_chunk(i - 1, HALVES, mark)

time: 161 us -> 159 us (0.988)
  starting transfers between devices: 53 us -> 42.9 us
  waiting for transfers between devices: 70.2 us -> 77.8 us
    ppermute x19, waiting for transfers between devices: 28.8 us -> 35 us  [shift_back(): return lax.ppermute(array, 'expert', pairs)]
    ppermute x6, waiting for transfers between devices: 21.1 us -> 27.1 us  [shift_plane(): lax.ppermute(array, 'rep', [(r, (r + by) % reps) for r in range(reps)])]
    ppermute x19, starting transfers between devices: 21.5 us -> 15.6 us  [shift_back(): return lax.ppermute(array, 'expert', pairs)]
    ppermute x16, waiting for transfers between devices: 20.2 us -> 15.7 us  [shift_owner(): lax.ppermute(array, 'expert', pairs if by >= 0 else [(b, a) for a, b in p...]
    ppermute x16, starting transfers between devices: 21.2 us -> 18.7 us  [shift_owner(): lax.ppermute(array, 'expert', pairs if by >= 0 else [(b, a) for a, b in p...]
    ppermute x6, starting transfers between devices: 10.4 us -> 8.67 us  [shift_plane(): lax.ppermute(array, 'rep', [(r, (r + by) % reps) for r in range(reps)])]
where the time goes in v3:
time: 159 us; the launch traced here: 158 us
  waiting for transfers between devices  77.8 us (49%)
  starting transfers between devices  42.9 us (27%)
  Pallas kernels  29.4 us (18%)
  local copies, waits for them, and re-layouts  6.97 us (4%)
    ppermute x19, waiting for transfers between devices, shift_back(): return lax.ppermute(array, 'expert', pairs)  35 us
    ppermute x6, waiting for transfers between devices, shift_plane(): lax.ppermute(array, 'rep', [(r, (r + by) % reps) for r in range(reps)])  27.1 us
    ppermute x16, starting transfers between devices, shift_owner(): lax.ppermute(array, 'expert', pairs if by >= 0 else [(b, a) for a, b in p...  18.7 us
    ppermute x16, waiting for transfers between devices, shift_owner(): lax.ppermute(array, 'expert', pairs if by >= 0 else [(b, a) for a, b in p...  15.7 us
    ppermute x19, starting transfers between devices, shift_back(): return lax.ppermute(array, 'expert', pairs)  15.6 us
    pallas_call x4, Pallas kernels, apply_experts(): pl.pallas_call(functools.partial(experts_kernel, count), out_shape=[jax.S...  15.3 us
    ppermute x6, starting transfers between devices, shift_plane(): lax.ppermute(array, 'rep', [(r, (r + by) % reps) for r in range(reps)])  8.67 us
    pallas_call x4, Pallas kernels, combine(): pl.pallas_call(functools.partial(combine_kernel, rows, cap, top, dense, h...  8.22 us
  transfers between devices with their start and end apart: 41, of which 23 were waited for; matrix products, arithmetic and copies ran while one was open for 1% of the time, Pallas kernels for 18%

profile of v3, /device:TPU:0, one launch (start us, length us, event | category | flops | bytes accessed | tf_op | source)
XLA Modules:
  0.0 158.3 jit_solution(297008869849585699)
XLA Ops:
  0.0 1.0 copy-done
  1.0 0.8 copy-done.1
  1.8 0.7 copy-done.2
  3.4 3.0 %collective-permute-start.3 = (bf16[144,2048]{1,0:T(8,128)(2,1)S(1)}, bf16[144,2048]{1,0:T(8,128)(2,1)S(1)}, u32[]{:S(2)}, u32[]{:S(2)}) collective-permute-start(bf16[144,2048]{1,0:T(8,128)(2,1)S(1)} %pack.1.refs_0_), channel_id=1, source_target_pairs={{0,2},{1,5},{2,0},{3,7},{4,6},{5,1},{6,4},{7,3},{8,10},{9,13},{10,... | collective-permute-start | bytes 1769480 | tf_op jit(solution)/shard_map/ppermute | solution.py:186
  6.4 1.6 collective-permute-start
  8.1 0.9 compare_convert_fusion.groups_ref
  9.0 5.3 %collective-permute-done.3.refs_1_ = bf16[144,2048]{1,0:T(8,128)(2,1)S(1)} collective-permute-done((bf16[144,2048]{1,0:T(8,128)(2,1)S(1)}, bf16[144,2048]{1,0:T(8,128)(2,1)S(1)}, u32[]{:S(2)}, u32[]{:S(2)}) %collective-permute-start.3) | collective-permute-done | bytes 589856 | tf_op jit(solution)/shard_map/ppermute | solution.py:186
  14.3 1.0 select.24
  15.4 2.1 %collective-permute-start.5 = (bf16[96,2048]{1,0:T(8,128)(2,1)S(1)}, bf16[96,2048]{1,0:T(8,128)(2,1)S(1)}, u32[]{:S(2)}, u32[]{:S(2)}) collective-permute-start(bf16[96,2048]{1,0:T(8,128)(2,1)S(1)} %get-tuple-element.76), channel_id=1, source_target_pairs={{0,4},{1,3},{2,6},{3,1},{4,0},{5,7},{6,2},{7,5},{8,12},{9,11},{10,... | collective-permute-start | bytes 1179656 | tf_op jit(solution)/shard_map/ppermute | solution.py:186
  17.5 1.2 collective-permute-start.6
  18.8 4.3 %collective-permute-done.refs_0_.refs_1_ = bf16[144,2048]{1,0:T(8,128)(2,1)S(1)} collective-permute-done((bf16[144,2048]{1,0:T(8,128)(2,1)S(1)}, bf16[144,2048]{1,0:T(8,128)(2,1)S(1)}, u32[]{:S(2)}, u32[]{:S(2)}) %collective-permute-start) | collective-permute-done | bytes 589856 | tf_op jit(solution)/shard_map/ppermute | solution.py:189
  23.3 2.0 %collective-permute-start.7 = (bf16[144,2048]{1,0:T(8,128)(2,1)S(1)}, bf16[144,2048]{1,0:T(8,128)(2,1)S(1)}, u32[]{:S(2)}, u32[]{:S(2)}) collective-permute-start(bf16[144,2048]{1,0:T(8,128)(2,1)S(1)} %collective-permute-done.refs_0_.refs_1_), channel_id=1, source_target_pairs={{0,2},{1,5},{2,0},{3,7},{4,6},{5,1},{6,4},{7,3},{8,10},{9,13},{10,... | collective-permute-start | bytes 1769480 | tf_op jit(solution)/shard_map/ppermute | solution.py:186
  25.3 1.6 collective-permute-start.1
  26.8 2.2 %collective-permute-done.6.refs_3_ = bf16[96,2048]{1,0:T(8,128)(2,1)S(1)} collective-permute-done((bf16[96,2048]{1,0:T(8,128)(2,1)S(1)}, bf16[96,2048]{1,0:T(8,128)(2,1)S(1)}, u32[]{:S(2)}, u32[]{:S(2)}) %collective-permute-start.6) | collective-permute-done | bytes 393248 | tf_op jit(solution)/shard_map/ppermute | solution.py:186
  29.0 1.9 %copy-done.5 = bf16[1,2048,768]{2,1,0:T(8,128)(2,1)S(1)} copy-done((bf16[1,2048,768]{2,1,0:T(8,128)(2,1)S(1)}, bf16[1,2048,768]{2,1,0:T(8,128)(2,1)}, u32[]{:S(2)}) %copy-start.5) | copy-done | bytes 3145752
  30.9 1.9 %copy-done.7 = bf16[1,768,2048]{2,1,0:T(8,128)(2,1)S(1)} copy-done((bf16[1,768,2048]{2,1,0:T(8,128)(2,1)S(1)}, bf16[1,768,2048]{2,1,0:T(8,128)(2,1)}, u32[]{:S(2)}) %copy-start.7) | copy-done | bytes 3145752
  32.8 3.8 %experts.4 = (bf16[96,2048]{1,0:T(8,128)(2,1)S(1)}, bf16[96,2048]{1,0:T(8,128)(2,1)S(1)}, bf16[96,2048]{1,0:T(8,128)(2,1)S(1)}, bf16[96,2048]{1,0:T(8,128)(2,1)S(1)}) custom-call(bf16[96,2048]{1,0:T(8,128)(2,1)S(1)} %get-tuple-element.78.refs_0_, bf16[96,2048]{1,0:T(8,128)(2,1)S(1)} %collective-permute-done.4.refs_1_, ...), custom_call_target="tpu_custom_call" | custom-call | flops 4000000000 | tf_op jit(solution)/shard_map/experts/pallas_call | solution.py:249
  36.7 1.1 select.25
  38.1 3.6 %collective-permute-done.1.refs_0_.refs_2_ = bf16[144,2048]{1,0:T(8,128)(2,1)S(1)} collective-permute-done((bf16[144,2048]{1,0:T(8,128)(2,1)S(1)}, bf16[144,2048]{1,0:T(8,128)(2,1)S(1)}, u32[]{:S(2)}, u32[]{:S(2)}) %collective-permute-start.1) | collective-permute-done | bytes 589856 | tf_op jit(solution)/shard_map/ppermute | solution.py:189
  41.7 1.5 collective-permute-start.9
  44.1 13.1 %collective-permute-done.2.refs_0_.refs_3_ = bf16[144,2048]{1,0:T(8,128)(2,1)S(1)} collective-permute-done((bf16[144,2048]{1,0:T(8,128)(2,1)S(1)}, bf16[144,2048]{1,0:T(8,128)(2,1)S(1)}, u32[]{:S(2)}, u32[]{:S(2)}) %collective-permute-start.2) | collective-permute-done | bytes 589856 | tf_op jit(solution)/shard_map/ppermute | solution.py:189
  57.9 1.0 select.26
  59.1 2.0 %collective-permute-start.12 = (bf16[144,2048]{1,0:T(8,128)(2,1)S(1)}, bf16[144,2048]{1,0:T(8,128)(2,1)S(1)}, u32[]{:S(2)}, u32[]{:S(2)}) collective-permute-start(bf16[144,2048]{1,0:T(8,128)(2,1)S(1)} %collective-permute-done.2.refs_0_.refs_3_), channel_id=1, source_target_pairs={{0,2},{1,5},{2,0},{3,7},{4,6},{5,1},{6,4},{7,3},{8,10},{9,13},{10,... | collective-permute-start | bytes 1769480 | tf_op jit(solution)/shard_map/ppermute | solution.py:186
  61.2 0.8 collective-permute-start.17
  62.0 1.0 collective-permute-start.16
  63.0 3.8 %experts.5 = (bf16[96,2048]{1,0:T(8,128)(2,1)S(1)}, bf16[96,2048]{1,0:T(8,128)(2,1)S(1)}, bf16[96,2048]{1,0:T(8,128)(2,1)S(1)}, bf16[96,2048]{1,0:T(8,128)(2,1)S(1)}) custom-call(bf16[96,2048]{1,0:T(8,128)(2,1)S(1)} %get-tuple-element.90.refs_0_, bf16[96,2048]{1,0:T(8,128)(2,1)S(1)} %collective-permute-done.8.refs_1_, ...), custom_call_target="tpu_custom_call" | custom-call | flops 4000000000 | tf_op jit(solution)/shard_map/experts/pallas_call | solution.py:249
  67.0 5.7 %collective-permute-done.18.refs_3_ = bf16[96,2048]{1,0:T(8,128)(2,1)S(1)} collective-permute-done((bf16[96,2048]{1,0:T(8,128)(2,1)S(1)}, bf16[96,2048]{1,0:T(8,128)(2,1)S(1)}, u32[]{:S(2)}, u32[]{:S(2)}) %collective-permute-start.18) | collective-permute-done | bytes 393248 | tf_op jit(solution)/shard_map/ppermute | solution.py:186
  72.7 0.8 collective-permute-start.14
  73.4 1.4 collective-permute-done.12.refs_1_
  74.8 1.0 select.27
  75.9 2.5 %collective-permute-start.21 = (bf16[96,2048]{1,0:T(8,128)(2,1)S(1)}, bf16[96,2048]{1,0:T(8,128)(2,1)S(1)}, u32[]{:S(2)}, u32[]{:S(2)}) collective-permute-start(bf16[96,2048]{1,0:T(8,128)(2,1)S(1)} %get-tuple-element.114), channel_id=1, source_target_pairs={{0,5},{1,2},{2,7},{3,0},{4,1},{5,6},{6,3},{7,4},{8,13},{9,10},{10,... | collective-permute-start | bytes 1179656 | tf_op jit(solution)/shard_map/ppermute | solution.py:186
  78.4 0.8 collective-permute-start.20
  79.5 3.5 %collective-permute-done.14.refs_4_ = bf16[96,2048]{1,0:T(8,128)(2,1)S(1)} collective-permute-done((bf16[96,2048]{1,0:T(8,128)(2,1)S(1)}, bf16[96,2048]{1,0:T(8,128)(2,1)S(1)}, u32[]{:S(2)}, u32[]{:S(2)}) %collective-permute-start.14) | collective-permute-done | bytes 393248 | tf_op jit(solution)/shard_map/ppermute | solution.py:269
  83.0 3.3 %collective-permute-done.15.refs_5_ = bf16[96,2048]{1,0:T(8,128)(2,1)S(1)} collective-permute-done((bf16[96,2048]{1,0:T(8,128)(2,1)S(1)}, bf16[96,2048]{1,0:T(8,128)(2,1)S(1)}, u32[]{:S(2)}, u32[]{:S(2)}) %collective-permute-start.15) | collective-permute-done | bytes 393248 | tf_op jit(solution)/shard_map/ppermute | solution.py:269
  86.3 2.1 %combine.4 = (f32[128,2048]{1,0:T(8,128)S(1)}, bf16[128,2048]{1,0:T(8,128)(2,1)S(1)}) custom-call(f32[4,32]{1,0:T(4,128)S(1)} %compare_convert_fusion.groups_ref, bf16[32,2048]{1,0:T(8,128)(2,1)S(1)} %router.1.router_ref, bf16[144,2048]{1,0:T(8,128)(2,1)S(1)} %collective-permute-done.refs_0_.refs_1_, bf16[144,2048]{1,0:T(8,128)(2,1)S(1)} %collective-permute-done.7.refs_1_, ...), custom_call_target="tpu_custom_call" | custom-call | flops 2000000000 | tf_op jit(solution)/shard_map/combine/pallas_call | solution.py:272
  88.4 2.5 %collective-permute-start.22 = (bf16[128,2048]{1,0:T(8,128)(2,1)S(1)}, bf16[128,2048]{1,0:T(8,128)(2,1)S(1)}, u32[]{:S(2)}, u32[]{:S(2)}) collective-permute-start(bf16[128,2048]{1,0:T(8,128)(2,1)S(1)} %get-tuple-element.117), channel_id=1, source_target_pairs={{2,0},{5,1},{0,2},{7,3},{6,4},{1,5},{4,6},{3,7},{10,8},{13,9},{8,1... | collective-permute-start | bytes 1572872 | tf_op jit(solution)/shard_map/ppermute | solution.py:269
  90.9 3.8 %experts.6 = (bf16[96,2048]{1,0:T(8,128)(2,1)S(1)}, bf16[96,2048]{1,0:T(8,128)(2,1)S(1)}, bf16[96,2048]{1,0:T(8,128)(2,1)S(1)}, bf16[96,2048]{1,0:T(8,128)(2,1)S(1)}) custom-call(bf16[96,2048]{1,0:T(8,128)(2,1)S(1)} %get-tuple-element.100.refs_0_, bf16[96,2048]{1,0:T(8,128)(2,1)S(1)} %collective-permute-done.16.refs_1_, ...), custom_call_target="tpu_custom_call" | custom-call | flops 4000000000 | tf_op jit(solution)/shard_map/experts/pallas_call | solution.py:249
  95.5 1.3 collective-permute-start.25
  96.8 3.8 %experts.7 = (bf16[96,2048]{1,0:T(8,128)(2,1)S(1)}, bf16[96,2048]{1,0:T(8,128)(2,1)S(1)}, bf16[96,2048]{1,0:T(8,128)(2,1)S(1)}, bf16[96,2048]{1,0:T(8,128)(2,1)S(1)}) custom-call(bf16[96,2048]{1,0:T(8,128)(2,1)S(1)} %get-tuple-element.108.refs_0_, bf16[96,2048]{1,0:T(8,128)(2,1)S(1)} %collective-permute-done.19.refs_1_, ...), custom_call_target="tpu_custom_call" | custom-call | flops 4000000000 | tf_op jit(solution)/shard_map/experts/pallas_call | solution.py:249
  100.7 1.5 collective-permute-done.22.refs_0_
  102.2 2.4 %collective-permute-start.28 = (bf16[128,2048]{1,0:T(8,128)(2,1)S(1)}, bf16[128,2048]{1,0:T(8,128)(2,1)S(1)}, u32[]{:S(2)}, u32[]{:S(2)}) collective-permute-start(bf16[128,2048]{1,0:T(8,128)(2,1)S(1)} %add.119), channel_id=1, source_target_pairs={{0,8},{8,16},{16,24},{24,0},{1,9},{9,17},{17,25},{25,1},{2,10},{10... | collective-permute-start | bytes 1572872 | tf_op jit(solution)/shard_map/ppermute | solution.py:189
  104.6 2.3 %collective-permute-done.24.refs_4_ = bf16[96,2048]{1,0:T(8,128)(2,1)S(1)} collective-permute-done((bf16[96,2048]{1,0:T(8,128)(2,1)S(1)}, bf16[96,2048]{1,0:T(8,128)(2,1)S(1)}, u32[]{:S(2)}, u32[]{:S(2)}) %collective-permute-start.24) | collective-permute-done | bytes 393248 | tf_op jit(solution)/shard_map/ppermute | solution.py:269
  107.4 2.1 %combine.5 = (f32[128,2048]{1,0:T(8,128)S(1)}, bf16[64,2048]{1,0:T(8,128)(2,1)S(1)}, bf16[64,2048]{1,0:T(8,128)(2,1)S(1)}) custom-call(f32[4,32]{1,0:T(4,128)S(1)} %compare_convert_fusion.groups_ref, bf16[32,2048]{1,0:T(8,128)(2,1)S(1)} %router.1.router_ref, bf16[144,2048]{1,0:T(8,128)(2,1)S(1)} %collective-permute-done.1.refs_0_.refs_2_, ...), custom_call_target="tpu_custom_call" | custom-call | flops 2000000000 | tf_op jit(solution)/shard_map/combine/pallas_call | solution.py:272
  109.5 1.4 collective-permute-start.26
  110.8 0.7 collective-permute-start.27
  111.6 1.1 collective-permute-start.30
  112.7 4.4 %collective-permute-done.26.refs_0_ = bf16[64,2048]{1,0:T(8,128)(2,1)S(1)} collective-permute-done((bf16[64,2048]{1,0:T(8,128)(2,1)S(1)}, bf16[64,2048]{1,0:T(8,128)(2,1)S(1)}, u32[]{:S(2)}, u32[]{:S(2)}) %collective-permute-start.26) | collective-permute-done | bytes 262176 | tf_op jit(solution)/shard_map/ppermute | solution.py:269
  117.7 5.0 %collective-permute-done.27.refs_1_ = bf16[64,2048]{1,0:T(8,128)(2,1)S(1)} collective-permute-done((bf16[64,2048]{1,0:T(8,128)(2,1)S(1)}, bf16[64,2048]{1,0:T(8,128)(2,1)S(1)}, u32[]{:S(2)}, u32[]{:S(2)}) %collective-permute-start.27) | collective-permute-done | bytes 262176 | tf_op jit(solution)/shard_map/ppermute | solution.py:269
  122.9 1.5 collective-permute-start.34
  124.4 2.8 %collective-permute-done.31.refs_5_ = bf16[96,2048]{1,0:T(8,128)(2,1)S(1)} collective-permute-done((bf16[96,2048]{1,0:T(8,128)(2,1)S(1)}, bf16[96,2048]{1,0:T(8,128)(2,1)S(1)}, u32[]{:S(2)}, u32[]{:S(2)}) %collective-permute-start.31) | collective-permute-done | bytes 393248 | tf_op jit(solution)/shard_map/ppermute | solution.py:269
  127.2 2.1 %combine.6 = (f32[128,2048]{1,0:T(8,128)S(1)}, bf16[64,2048]{1,0:T(8,128)(2,1)S(1)}, bf16[64,2048]{1,0:T(8,128)(2,1)S(1)}) custom-call(f32[4,32]{1,0:T(4,128)S(1)} %compare_convert_fusion.groups_ref, bf16[32,2048]{1,0:T(8,128)(2,1)S(1)} %router.1.router_ref, bf16[144,2048]{1,0:T(8,128)(2,1)S(1)} %collective-permute-done.2.refs_0_.refs_3_, ...), custom_call_target="tpu_custom_call" | custom-call | flops 2000000000 | tf_op jit(solution)/shard_map/combine/pallas_call | solution.py:272
  129.3 1.3 collective-permute-start.32
  130.6 0.8 collective-permute-start.33
  131.4 1.2 collective-permute-start.36
  132.6 6.0 %collective-permute-done.34.refs_2_ = bf16[128,2048]{1,0:T(8,128)(2,1)S(1)} collective-permute-done((bf16[128,2048]{1,0:T(8,128)(2,1)S(1)}, bf16[128,2048]{1,0:T(8,128)(2,1)S(1)}, u32[]{:S(2)}, u32[]{:S(2)}) %collective-permute-start.34) | collective-permute-done | bytes 524320 | tf_op jit(solution)/shard_map/ppermute | solution.py:189
  138.6 0.9 collective-permute-start.37
  139.5 3.0 %collective-permute-done.33.refs_1_ = bf16[64,2048]{1,0:T(8,128)(2,1)S(1)} collective-permute-done((bf16[64,2048]{1,0:T(8,128)(2,1)S(1)}, bf16[64,2048]{1,0:T(8,128)(2,1)S(1)}, u32[]{:S(2)}, u32[]{:S(2)}) %collective-permute-start.33) | collective-permute-done | bytes 262176 | tf_op jit(solution)/shard_map/ppermute | solution.py:269
  142.7 1.6 %collective-permute-start.40 = (bf16[128,2048]{1,0:T(8,128)(2,1)S(1)}, bf16[128,2048]{1,0:T(8,128)(2,1)S(1)}, u32[]{:S(2)}, u32[]{:S(2)}) collective-permute-start(bf16[128,2048]{1,0:T(8,128)(2,1)S(1)} %add.121), channel_id=1, source_target_pairs={{0,8},{8,16},{16,24},{24,0},{1,9},{9,17},{17,25},{25,1},{2,10},{10... | collective-permute-start | bytes 1572872 | tf_op jit(solution)/shard_map/ppermute | solution.py:189
  144.3 1.7 %collective-permute-done.37.refs_5_ = bf16[96,2048]{1,0:T(8,128)(2,1)S(1)} collective-permute-done((bf16[96,2048]{1,0:T(8,128)(2,1)S(1)}, bf16[96,2048]{1,0:T(8,128)(2,1)S(1)}, u32[]{:S(2)}, u32[]{:S(2)}) %collective-permute-start.37) | collective-permute-done | bytes 393248 | tf_op jit(solution)/shard_map/ppermute | solution.py:269
  146.0 2.1 %combine.7 = (f32[128,2048]{1,0:T(8,128)S(1)}, bf16[64,2048]{1,0:T(8,128)(2,1)S(1)}, bf16[64,2048]{1,0:T(8,128)(2,1)S(1)}) custom-call(f32[4,32]{1,0:T(4,128)S(1)} %compare_convert_fusion.groups_ref, bf16[32,2048]{1,0:T(8,128)(2,1)S(1)} %router.1.router_ref, bf16[144,2048]{1,0:T(8,128)(2,1)S(1)} %pack.1.refs_0_, ...), custom_call_target="tpu_custom_call" | custom-call | flops 2000000000 | tf_op jit(solution)/shard_map/combine/pallas_call | solution.py:272
  148.1 1.6 %collective-permute-start.38 = (bf16[64,2048]{1,0:T(8,128)(2,1)S(1)}, bf16[64,2048]{1,0:T(8,128)(2,1)S(1)}, u32[]{:S(2)}, u32[]{:S(2)}) collective-permute-start(bf16[64,2048]{1,0:T(8,128)(2,1)S(1)} %get-tuple-element.143), channel_id=1, source_target_pairs={{2,0},{5,1},{0,2},{7,3},{6,4},{1,5},{4,6},{3,7},{10,8},{13,9},{8,1... | collective-permute-start | bytes 786440 | tf_op jit(solution)/shard_map/ppermute | solution.py:269
  150.2 4.3 %collective-permute-done.38.refs_0_ = bf16[64,2048]{1,0:T(8,128)(2,1)S(1)} collective-permute-done((bf16[64,2048]{1,0:T(8,128)(2,1)S(1)}, bf16[64,2048]{1,0:T(8,128)(2,1)S(1)}, u32[]{:S(2)}, u32[]{:S(2)}) %collective-permute-start.38) | collective-permute-done | bytes 262176 | tf_op jit(solution)/shard_map/ppermute | solution.py:269
  154.5 2.8 %collective-permute-done.39.refs_1_ = bf16[64,2048]{1,0:T(8,128)(2,1)S(1)} collective-permute-done((bf16[64,2048]{1,0:T(8,128)(2,1)S(1)}, bf16[64,2048]{1,0:T(8,128)(2,1)S(1)}, u32[]{:S(2)}, u32[]{:S(2)}) %collective-permute-start.39) | collective-permute-done | bytes 262176 | tf_op jit(solution)/shard_map/ppermute | solution.py:269
  157.3 1.0 add.122
  (54 shorter events, 6.6 us)
Async XLA Ops:
  0.0 1.0 copy-start
  1.0 0.8 copy-start.1
  1.8 0.7 copy-start.2
  2.5 0.7 copy-start.3
  3.4 10.9 %collective-permute-start.3 = (bf16[144,2048]{1,0:T(8,128)(2,1)S(1)}, bf16[144,2048]{1,0:T(8,128)(2,1)S(1)}, u32[]{:S(2)}, u32[]{:S(2)}) collective-permute-start(bf16[144,2048]{1,0:T(8,128)(2,1)S(1)} %pack.1.refs_0_), channel_id=1, source_target_pairs={{0,2},{1,5},{2,0},{3,7},{4,6},{5,1},{6,4},{7,3},{8,10},{9,13},{10,... | collective-permute-start | bytes 1769480 | tf_op jit(solution)/shard_map/ppermute | solution.py:186
  6.4 16.7 %collective-permute-start = (bf16[144,2048]{1,0:T(8,128)(2,1)S(1)}, bf16[144,2048]{1,0:T(8,128)(2,1)S(1)}, u32[]{:S(2)}, u32[]{:S(2)}) collective-permute-start(bf16[144,2048]{1,0:T(8,128)(2,1)S(1)} %pack.1.refs_0_), channel_id=1, source_target_pairs={{0,8},{8,16},{16,24},{24,0},{1,9},{9,17},{17,25},{25,1},{2,10},{10... | collective-permute-start | bytes 1769480 | tf_op jit(solution)/shard_map/ppermute | solution.py:189
  8.0 21.0 %copy-start.4 = (bf16[1,2048,768]{2,1,0:T(8,128)(2,1)S(1)}, bf16[1,2048,768]{2,1,0:T(8,128)(2,1)}, u32[]{:S(2)}) copy-start(bf16[1,2048,768]{2,1,0:T(8,128)(2,1)} %refs_4_.7) | copy-start | bytes 9437188
  15.3 7.8 %collective-permute-start.4 = (bf16[96,2048]{1,0:T(8,128)(2,1)S(1)}, bf16[96,2048]{1,0:T(8,128)(2,1)S(1)}, u32[]{:S(2)}, u32[]{:S(2)}) collective-permute-start(bf16[96,2048]{1,0:T(8,128)(2,1)S(1)} %get-tuple-element.75), channel_id=1, source_target_pairs={{0,1},{1,0},{2,3},{3,2},{4,5},{5,4},{6,7},{7,6},{8,9},{9,8},{10,11... | collective-permute-start | bytes 1179656 | tf_op jit(solution)/shard_map/ppermute | solution.py:186
  15.4 7.9 %collective-permute-start.5 = (bf16[96,2048]{1,0:T(8,128)(2,1)S(1)}, bf16[96,2048]{1,0:T(8,128)(2,1)S(1)}, u32[]{:S(2)}, u32[]{:S(2)}) collective-permute-start(bf16[96,2048]{1,0:T(8,128)(2,1)S(1)} %get-tuple-element.76), channel_id=1, source_target_pairs={{0,4},{1,3},{2,6},{3,1},{4,0},{5,7},{6,2},{7,5},{8,12},{9,11},{10,... | collective-permute-start | bytes 1179656 | tf_op jit(solution)/shard_map/ppermute | solution.py:186
  17.5 11.5 %collective-permute-start.6 = (bf16[96,2048]{1,0:T(8,128)(2,1)S(1)}, bf16[96,2048]{1,0:T(8,128)(2,1)S(1)}, u32[]{:S(2)}, u32[]{:S(2)}) collective-permute-start(bf16[96,2048]{1,0:T(8,128)(2,1)S(1)} %get-tuple-element.79), channel_id=1, source_target_pairs={{0,5},{1,2},{2,7},{3,0},{4,1},{5,6},{6,3},{7,4},{8,13},{9,10},{10,... | collective-permute-start | bytes 1179656 | tf_op jit(solution)/shard_map/ppermute | solution.py:186
  23.3 13.4 %collective-permute-start.7 = (bf16[144,2048]{1,0:T(8,128)(2,1)S(1)}, bf16[144,2048]{1,0:T(8,128)(2,1)S(1)}, u32[]{:S(2)}, u32[]{:S(2)}) collective-permute-start(bf16[144,2048]{1,0:T(8,128)(2,1)S(1)} %collective-permute-done.refs_0_.refs_1_), channel_id=1, source_target_pairs={{0,2},{1,5},{2,0},{3,7},{4,6},{5,1},{6,4},{7,3},{8,10},{9,13},{10,... | collective-permute-start | bytes 1769480 | tf_op jit(solution)/shard_map/ppermute | solution.py:186
  25.3 16.4 %collective-permute-start.1 = (bf16[144,2048]{1,0:T(8,128)(2,1)S(1)}, bf16[144,2048]{1,0:T(8,128)(2,1)S(1)}, u32[]{:S(2)}, u32[]{:S(2)}) collective-permute-start(bf16[144,2048]{1,0:T(8,128)(2,1)S(1)} %collective-permute-done.refs_0_.refs_1_), channel_id=1, source_target_pairs={{0,8},{8,16},{16,24},{24,0},{1,9},{9,17},{17,25},{25,1},{2,10},{10... | collective-permute-start | bytes 1769480 | tf_op jit(solution)/shard_map/ppermute | solution.py:189
  29.0 1.9 %copy-start.5 = (bf16[1,2048,768]{2,1,0:T(8,128)(2,1)S(1)}, bf16[1,2048,768]{2,1,0:T(8,128)(2,1)}, u32[]{:S(2)}) copy-start(bf16[1,2048,768]{2,1,0:T(8,128)(2,1)} %refs_5_.7) | copy-start | bytes 9437188
  30.9 1.9 %copy-start.7 = (bf16[1,768,2048]{2,1,0:T(8,128)(2,1)S(1)}, bf16[1,768,2048]{2,1,0:T(8,128)(2,1)}, u32[]{:S(2)}) copy-start(bf16[1,768,2048]{2,1,0:T(8,128)(2,1)} %refs_6_.7) | copy-start | bytes 9437188
  36.6 26.4 %copy-start.6 = (bf16[1,2048,768]{2,1,0:T(8,128)(2,1)S(1)}, bf16[1,2048,768]{2,1,0:T(8,128)(2,1)}, u32[]{:S(2)}) copy-start(bf16[1,2048,768]{2,1,0:T(8,128)(2,1)} %refs_5_.7) | copy-start | bytes 9437188
  37.7 4.0 %collective-permute-start.8 = (bf16[96,2048]{1,0:T(8,128)(2,1)S(1)}, bf16[96,2048]{1,0:T(8,128)(2,1)S(1)}, u32[]{:S(2)}, u32[]{:S(2)}) collective-permute-start(bf16[96,2048]{1,0:T(8,128)(2,1)S(1)} %get-tuple-element.83), channel_id=1, source_target_pairs={{0,1},{1,0},{2,3},{3,2},{4,5},{5,4},{6,7},{7,6},{8,9},{9,8},{10,11... | collective-permute-start | bytes 1179656 | tf_op jit(solution)/shard_map/ppermute | solution.py:186
  41.7 15.5 %collective-permute-start.2 = (bf16[144,2048]{1,0:T(8,128)(2,1)S(1)}, bf16[144,2048]{1,0:T(8,128)(2,1)S(1)}, u32[]{:S(2)}, u32[]{:S(2)}) collective-permute-start(bf16[144,2048]{1,0:T(8,128)(2,1)S(1)} %collective-permute-done.1.refs_0_.refs_2_), channel_id=1, source_target_pairs={{0,8},{8,16},{16,24},{24,0},{1,9},{9,17},{17,25},{25,1},{2,10},{10... | collective-permute-start | bytes 1769480 | tf_op jit(solution)/shard_map/ppermute | solution.py:189
  41.7 16.2 %collective-permute-start.9 = (bf16[144,2048]{1,0:T(8,128)(2,1)S(1)}, bf16[144,2048]{1,0:T(8,128)(2,1)S(1)}, u32[]{:S(2)}, u32[]{:S(2)}) collective-permute-start(bf16[144,2048]{1,0:T(8,128)(2,1)S(1)} %collective-permute-done.1.refs_0_.refs_2_), channel_id=1, source_target_pairs={{0,2},{1,5},{2,0},{3,7},{4,6},{5,1},{6,4},{7,3},{8,10},{9,13},{10,... | collective-permute-start | bytes 1769480 | tf_op jit(solution)/shard_map/ppermute | solution.py:186
  43.2 15.7 %collective-permute-start.10 = (bf16[96,2048]{1,0:T(8,128)(2,1)S(1)}, bf16[96,2048]{1,0:T(8,128)(2,1)S(1)}, u32[]{:S(2)}, u32[]{:S(2)}) collective-permute-start(bf16[96,2048]{1,0:T(8,128)(2,1)S(1)} %get-tuple-element.87), channel_id=1, source_target_pairs={{0,4},{1,3},{2,6},{3,1},{4,0},{5,7},{6,2},{7,5},{8,12},{9,11},{10,... | collective-permute-start | bytes 1179656 | tf_op jit(solution)/shard_map/ppermute | solution.py:186
  43.7 15.4 %collective-permute-start.11 = (bf16[96,2048]{1,0:T(8,128)(2,1)S(1)}, bf16[96,2048]{1,0:T(8,128)(2,1)S(1)}, u32[]{:S(2)}, u32[]{:S(2)}) collective-permute-start(bf16[96,2048]{1,0:T(8,128)(2,1)S(1)} %get-tuple-element.88), channel_id=1, source_target_pairs={{0,5},{1,2},{2,7},{3,0},{4,1},{5,6},{6,3},{7,4},{8,13},{9,10},{10,... | collective-permute-start | bytes 1179656 | tf_op jit(solution)/shard_map/ppermute | solution.py:186
  59.1 15.7 %collective-permute-start.12 = (bf16[144,2048]{1,0:T(8,128)(2,1)S(1)}, bf16[144,2048]{1,0:T(8,128)(2,1)S(1)}, u32[]{:S(2)}, u32[]{:S(2)}) collective-permute-start(bf16[144,2048]{1,0:T(8,128)(2,1)S(1)} %collective-permute-done.2.refs_0_.refs_3_), channel_id=1, source_target_pairs={{0,2},{1,5},{2,0},{3,7},{4,6},{5,1},{6,4},{7,3},{8,10},{9,13},{10,... | collective-permute-start | bytes 1769480 | tf_op jit(solution)/shard_map/ppermute | solution.py:186
  61.2 11.5 %collective-permute-start.18 = (bf16[96,2048]{1,0:T(8,128)(2,1)S(1)}, bf16[96,2048]{1,0:T(8,128)(2,1)S(1)}, u32[]{:S(2)}, u32[]{:S(2)}) collective-permute-start(bf16[96,2048]{1,0:T(8,128)(2,1)S(1)} %get-tuple-element.106), channel_id=1, source_target_pairs={{0,5},{1,2},{2,7},{3,0},{4,1},{5,6},{6,3},{7,4},{8,13},{9,10},{10,... | collective-permute-start | bytes 1179656 | tf_op jit(solution)/shard_map/ppermute | solution.py:186
  61.2 14.7 %collective-permute-start.17 = (bf16[96,2048]{1,0:T(8,128)(2,1)S(1)}, bf16[96,2048]{1,0:T(8,128)(2,1)S(1)}, u32[]{:S(2)}, u32[]{:S(2)}) collective-permute-start(bf16[96,2048]{1,0:T(8,128)(2,1)S(1)} %get-tuple-element.104), channel_id=1, source_target_pairs={{0,4},{1,3},{2,6},{3,1},{4,0},{5,7},{6,2},{7,5},{8,12},{9,11},{10,... | collective-permute-start | bytes 1179656 | tf_op jit(solution)/shard_map/ppermute | solution.py:186
  62.0 13.9 %collective-permute-start.16 = (bf16[96,2048]{1,0:T(8,128)(2,1)S(1)}, bf16[96,2048]{1,0:T(8,128)(2,1)S(1)}, u32[]{:S(2)}, u32[]{:S(2)}) collective-permute-start(bf16[96,2048]{1,0:T(8,128)(2,1)S(1)} %get-tuple-element.102), channel_id=1, source_target_pairs={{0,1},{1,0},{2,3},{3,2},{4,5},{5,4},{6,7},{7,6},{8,9},{9,8},{10,11... | collective-permute-start | bytes 1179656 | tf_op jit(solution)/shard_map/ppermute | solution.py:186
  66.9 12.3 %collective-permute-start.13 = (bf16[96,2048]{1,0:T(8,128)(2,1)S(1)}, bf16[96,2048]{1,0:T(8,128)(2,1)S(1)}, u32[]{:S(2)}, u32[]{:S(2)}) collective-permute-start(bf16[96,2048]{1,0:T(8,128)(2,1)S(1)} %get-tuple-element.96), channel_id=1, source_target_pairs={{1,0},{0,1},{3,2},{2,3},{5,4},{4,5},{7,6},{6,7},{9,8},{8,9},{11,10... | collective-permute-start | bytes 1179656 | tf_op jit(solution)/shard_map/ppermute | solution.py:269
  72.7 10.3 %collective-permute-start.14 = (bf16[96,2048]{1,0:T(8,128)(2,1)S(1)}, bf16[96,2048]{1,0:T(8,128)(2,1)S(1)}, u32[]{:S(2)}, u32[]{:S(2)}) collective-permute-start(bf16[96,2048]{1,0:T(8,128)(2,1)S(1)} %get-tuple-element.97), channel_id=1, source_target_pairs={{4,0},{3,1},{6,2},{1,3},{0,4},{7,5},{2,6},{5,7},{12,8},{11,9},{14,... | collective-permute-start | bytes 1179656 | tf_op jit(solution)/shard_map/ppermute | solution.py:269
  74.8 11.5 %collective-permute-start.15 = (bf16[96,2048]{1,0:T(8,128)(2,1)S(1)}, bf16[96,2048]{1,0:T(8,128)(2,1)S(1)}, u32[]{:S(2)}, u32[]{:S(2)}) collective-permute-start(bf16[96,2048]{1,0:T(8,128)(2,1)S(1)} %get-tuple-element.98), channel_id=1, source_target_pairs={{5,0},{2,1},{7,2},{0,3},{1,4},{6,5},{3,6},{4,7},{13,8},{10,9},{15,... | collective-permute-start | bytes 1179656 | tf_op jit(solution)/shard_map/ppermute | solution.py:269
  75.9 18.9 %collective-permute-start.21 = (bf16[96,2048]{1,0:T(8,128)(2,1)S(1)}, bf16[96,2048]{1,0:T(8,128)(2,1)S(1)}, u32[]{:S(2)}, u32[]{:S(2)}) collective-permute-start(bf16[96,2048]{1,0:T(8,128)(2,1)S(1)} %get-tuple-element.114), channel_id=1, source_target_pairs={{0,5},{1,2},{2,7},{3,0},{4,1},{5,6},{6,3},{7,4},{8,13},{9,10},{10,... | collective-permute-start | bytes 1179656 | tf_op jit(solution)/shard_map/ppermute | solution.py:186
  78.4 17.1 %collective-permute-start.20 = (bf16[96,2048]{1,0:T(8,128)(2,1)S(1)}, bf16[96,2048]{1,0:T(8,128)(2,1)S(1)}, u32[]{:S(2)}, u32[]{:S(2)}) collective-permute-start(bf16[96,2048]{1,0:T(8,128)(2,1)S(1)} %get-tuple-element.112), channel_id=1, source_target_pairs={{0,4},{1,3},{2,6},{3,1},{4,0},{5,7},{6,2},{7,5},{8,12},{9,11},{10,... | collective-permute-start | bytes 1179656 | tf_op jit(solution)/shard_map/ppermute | solution.py:186
  79.2 17.6 %collective-permute-start.19 = (bf16[96,2048]{1,0:T(8,128)(2,1)S(1)}, bf16[96,2048]{1,0:T(8,128)(2,1)S(1)}, u32[]{:S(2)}, u32[]{:S(2)}) collective-permute-start(bf16[96,2048]{1,0:T(8,128)(2,1)S(1)} %get-tuple-element.110), channel_id=1, source_target_pairs={{0,1},{1,0},{2,3},{3,2},{4,5},{5,4},{6,7},{7,6},{8,9},{9,8},{10,11... | collective-permute-start | bytes 1179656 | tf_op jit(solution)/shard_map/ppermute | solution.py:186
  88.4 13.8 %collective-permute-start.22 = (bf16[128,2048]{1,0:T(8,128)(2,1)S(1)}, bf16[128,2048]{1,0:T(8,128)(2,1)S(1)}, u32[]{:S(2)}, u32[]{:S(2)}) collective-permute-start(bf16[128,2048]{1,0:T(8,128)(2,1)S(1)} %get-tuple-element.117), channel_id=1, source_target_pairs={{2,0},{5,1},{0,2},{7,3},{6,4},{1,5},{4,6},{3,7},{10,8},{13,9},{8,1... | collective-permute-start | bytes 1572872 | tf_op jit(solution)/shard_map/ppermute | solution.py:269
  94.8 9.8 %collective-permute-start.23 = (bf16[96,2048]{1,0:T(8,128)(2,1)S(1)}, bf16[96,2048]{1,0:T(8,128)(2,1)S(1)}, u32[]{:S(2)}, u32[]{:S(2)}) collective-permute-start(bf16[96,2048]{1,0:T(8,128)(2,1)S(1)} %get-tuple-element.119), channel_id=1, source_target_pairs={{1,0},{0,1},{3,2},{2,3},{5,4},{4,5},{7,6},{6,7},{9,8},{8,9},{11,10... | collective-permute-start | bytes 1179656 | tf_op jit(solution)/shard_map/ppermute | solution.py:269
  94.8 12.1 %collective-permute-start.24 = (bf16[96,2048]{1,0:T(8,128)(2,1)S(1)}, bf16[96,2048]{1,0:T(8,128)(2,1)S(1)}, u32[]{:S(2)}, u32[]{:S(2)}) collective-permute-start(bf16[96,2048]{1,0:T(8,128)(2,1)S(1)} %get-tuple-element.120), channel_id=1, source_target_pairs={{4,0},{3,1},{6,2},{1,3},{0,4},{7,5},{2,6},{5,7},{12,8},{11,9},{14,... | collective-permute-start | bytes 1179656 | tf_op jit(solution)/shard_map/ppermute | solution.py:269
  95.5 11.9 %collective-permute-start.25 = (bf16[96,2048]{1,0:T(8,128)(2,1)S(1)}, bf16[96,2048]{1,0:T(8,128)(2,1)S(1)}, u32[]{:S(2)}, u32[]{:S(2)}) collective-permute-start(bf16[96,2048]{1,0:T(8,128)(2,1)S(1)} %get-tuple-element.121), channel_id=1, source_target_pairs={{5,0},{2,1},{7,2},{0,3},{1,4},{6,5},{3,6},{4,7},{13,8},{10,9},{15,... | collective-permute-start | bytes 1179656 | tf_op jit(solution)/shard_map/ppermute | solution.py:269
  102.2 14.8 %collective-permute-start.28 = (bf16[128,2048]{1,0:T(8,128)(2,1)S(1)}, bf16[128,2048]{1,0:T(8,128)(2,1)S(1)}, u32[]{:S(2)}, u32[]{:S(2)}) collective-permute-start(bf16[128,2048]{1,0:T(8,128)(2,1)S(1)} %add.119), channel_id=1, source_target_pairs={{0,8},{8,16},{16,24},{24,0},{1,9},{9,17},{17,25},{25,1},{2,10},{10... | collective-permute-start | bytes 1572872 | tf_op jit(solution)/shard_map/ppermute | solution.py:189
  104.6 7.0 %collective-permute-start.29 = (bf16[96,2048]{1,0:T(8,128)(2,1)S(1)}, bf16[96,2048]{1,0:T(8,128)(2,1)S(1)}, u32[]{:S(2)}, u32[]{:S(2)}) collective-permute-start(bf16[96,2048]{1,0:T(8,128)(2,1)S(1)} %get-tuple-element.127), channel_id=1, source_target_pairs={{1,0},{0,1},{3,2},{2,3},{5,4},{4,5},{7,6},{6,7},{9,8},{8,9},{11,10... | collective-permute-start | bytes 1179656 | tf_op jit(solution)/shard_map/ppermute | solution.py:269
  109.5 7.6 %collective-permute-start.26 = (bf16[64,2048]{1,0:T(8,128)(2,1)S(1)}, bf16[64,2048]{1,0:T(8,128)(2,1)S(1)}, u32[]{:S(2)}, u32[]{:S(2)}) collective-permute-start(bf16[64,2048]{1,0:T(8,128)(2,1)S(1)} %get-tuple-element.124), channel_id=1, source_target_pairs={{2,0},{5,1},{0,2},{7,3},{6,4},{1,5},{4,6},{3,7},{10,8},{13,9},{8,1... | collective-permute-start | bytes 786440 | tf_op jit(solution)/shard_map/ppermute | solution.py:269
  110.8 11.8 %collective-permute-start.27 = (bf16[64,2048]{1,0:T(8,128)(2,1)S(1)}, bf16[64,2048]{1,0:T(8,128)(2,1)S(1)}, u32[]{:S(2)}, u32[]{:S(2)}) collective-permute-start(bf16[64,2048]{1,0:T(8,128)(2,1)S(1)} %get-tuple-element.125), channel_id=1, source_target_pairs={{2,0},{5,1},{0,2},{7,3},{6,4},{1,5},{4,6},{3,7},{10,8},{13,9},{8,1... | collective-permute-start | bytes 786440 | tf_op jit(solution)/shard_map/ppermute | solution.py:269
  111.6 12.9 %collective-permute-start.30 = (bf16[96,2048]{1,0:T(8,128)(2,1)S(1)}, bf16[96,2048]{1,0:T(8,128)(2,1)S(1)}, u32[]{:S(2)}, u32[]{:S(2)}) collective-permute-start(bf16[96,2048]{1,0:T(8,128)(2,1)S(1)} %get-tuple-element.129), channel_id=1, source_target_pairs={{4,0},{3,1},{6,2},{1,3},{0,4},{7,5},{2,6},{5,7},{12,8},{11,9},{14,... | collective-permute-start | bytes 1179656 | tf_op jit(solution)/shard_map/ppermute | solution.py:269
  117.0 10.2 %collective-permute-start.31 = (bf16[96,2048]{1,0:T(8,128)(2,1)S(1)}, bf16[96,2048]{1,0:T(8,128)(2,1)S(1)}, u32[]{:S(2)}, u32[]{:S(2)}) collective-permute-start(bf16[96,2048]{1,0:T(8,128)(2,1)S(1)} %get-tuple-element.131), channel_id=1, source_target_pairs={{5,0},{2,1},{7,2},{0,3},{1,4},{6,5},{3,6},{4,7},{13,8},{10,9},{15,... | collective-permute-start | bytes 1179656 | tf_op jit(solution)/shard_map/ppermute | solution.py:269
  122.9 15.8 %collective-permute-start.34 = (bf16[128,2048]{1,0:T(8,128)(2,1)S(1)}, bf16[128,2048]{1,0:T(8,128)(2,1)S(1)}, u32[]{:S(2)}, u32[]{:S(2)}) collective-permute-start(bf16[128,2048]{1,0:T(8,128)(2,1)S(1)} %add.120), channel_id=1, source_target_pairs={{0,8},{8,16},{16,24},{24,0},{1,9},{9,17},{17,25},{25,1},{2,10},{10... | collective-permute-start | bytes 1572872 | tf_op jit(solution)/shard_map/ppermute | solution.py:189
  129.3 10.2 %collective-permute-start.32 = (bf16[64,2048]{1,0:T(8,128)(2,1)S(1)}, bf16[64,2048]{1,0:T(8,128)(2,1)S(1)}, u32[]{:S(2)}, u32[]{:S(2)}) collective-permute-start(bf16[64,2048]{1,0:T(8,128)(2,1)S(1)} %get-tuple-element.133), channel_id=1, source_target_pairs={{2,0},{5,1},{0,2},{7,3},{6,4},{1,5},{4,6},{3,7},{10,8},{13,9},{8,1... | collective-permute-start | bytes 786440 | tf_op jit(solution)/shard_map/ppermute | solution.py:269
  130.6 11.9 %collective-permute-start.33 = (bf16[64,2048]{1,0:T(8,128)(2,1)S(1)}, bf16[64,2048]{1,0:T(8,128)(2,1)S(1)}, u32[]{:S(2)}, u32[]{:S(2)}) collective-permute-start(bf16[64,2048]{1,0:T(8,128)(2,1)S(1)} %get-tuple-element.134), channel_id=1, source_target_pairs={{2,0},{5,1},{0,2},{7,3},{6,4},{1,5},{4,6},{3,7},{10,8},{13,9},{8,1... | collective-permute-start | bytes 786440 | tf_op jit(solution)/shard_map/ppermute | solution.py:269
  131.4 12.9 %collective-permute-start.35 = (bf16[96,2048]{1,0:T(8,128)(2,1)S(1)}, bf16[96,2048]{1,0:T(8,128)(2,1)S(1)}, u32[]{:S(2)}, u32[]{:S(2)}) collective-permute-start(bf16[96,2048]{1,0:T(8,128)(2,1)S(1)} %get-tuple-element.137), channel_id=1, source_target_pairs={{1,0},{0,1},{3,2},{2,3},{5,4},{4,5},{7,6},{6,7},{9,8},{8,9},{11,10... | collective-permute-start | bytes 1179656 | tf_op jit(solution)/shard_map/ppermute | solution.py:269
  131.4 12.9 %collective-permute-start.36 = (bf16[96,2048]{1,0:T(8,128)(2,1)S(1)}, bf16[96,2048]{1,0:T(8,128)(2,1)S(1)}, u32[]{:S(2)}, u32[]{:S(2)}) collective-permute-start(bf16[96,2048]{1,0:T(8,128)(2,1)S(1)} %get-tuple-element.139), channel_id=1, source_target_pairs={{4,0},{3,1},{6,2},{1,3},{0,4},{7,5},{2,6},{5,7},{12,8},{11,9},{14,... | collective-permute-start | bytes 1179656 | tf_op jit(solution)/shard_map/ppermute | solution.py:269
  138.6 7.4 %collective-permute-start.37 = (bf16[96,2048]{1,0:T(8,128)(2,1)S(1)}, bf16[96,2048]{1,0:T(8,128)(2,1)S(1)}, u32[]{:S(2)}, u32[]{:S(2)}) collective-permute-start(bf16[96,2048]{1,0:T(8,128)(2,1)S(1)} %get-tuple-element.141), channel_id=1, source_target_pairs={{5,0},{2,1},{7,2},{0,3},{1,4},{6,5},{3,6},{4,7},{13,8},{10,9},{15,... | collective-permute-start | bytes 1179656 | tf_op jit(solution)/shard_map/ppermute | solution.py:269
  142.7 14.6 %collective-permute-start.40 = (bf16[128,2048]{1,0:T(8,128)(2,1)S(1)}, bf16[128,2048]{1,0:T(8,128)(2,1)S(1)}, u32[]{:S(2)}, u32[]{:S(2)}) collective-permute-start(bf16[128,2048]{1,0:T(8,128)(2,1)S(1)} %add.121), channel_id=1, source_target_pairs={{0,8},{8,16},{16,24},{24,0},{1,9},{9,17},{17,25},{25,1},{2,10},{10... | collective-permute-start | bytes 1572872 | tf_op jit(solution)/shard_map/ppermute | solution.py:189
  148.1 6.4 %collective-permute-start.38 = (bf16[64,2048]{1,0:T(8,128)(2,1)S(1)}, bf16[64,2048]{1,0:T(8,128)(2,1)S(1)}, u32[]{:S(2)}, u32[]{:S(2)}) collective-permute-start(bf16[64,2048]{1,0:T(8,128)(2,1)S(1)} %get-tuple-element.143), channel_id=1, source_target_pairs={{2,0},{5,1},{0,2},{7,3},{6,4},{1,5},{4,6},{3,7},{10,8},{13,9},{8,1... | collective-permute-start | bytes 786440 | tf_op jit(solution)/shard_map/ppermute | solution.py:269
  149.7 7.7 %collective-permute-start.39 = (bf16[64,2048]{1,0:T(8,128)(2,1)S(1)}, bf16[64,2048]{1,0:T(8,128)(2,1)S(1)}, u32[]{:S(2)}, u32[]{:S(2)}) collective-permute-start(bf16[64,2048]{1,0:T(8,128)(2,1)S(1)} %get-tuple-element.144), channel_id=1, source_target_pairs={{2,0},{5,1},{0,2},{7,3},{6,4},{1,5},{4,6},{3,7},{10,8},{13,9},{8,1... | collective-permute-start | bytes 786440 | tf_op jit(solution)/shard_map/ppermute | solution.py:269

commit v4 on v3

--- a/solution.py
+++ b/solution.py
@@ -355,7 +355,7 @@
         back.append(send_back(results) if 0 < i < last else list(results))
         mark = results[0]
         if i == 0:
-            blocks[1][0] = after(blocks[1][0], mark)
+            blocks[1][0] = after(blocks[1][0], mark, sources[2])
             sent = select(blocks[1])
             mark = sent[0]
             here = send_rows(sent)

time: 159 us -> 160 us (level)
  waiting for transfers between devices: 77.8 us -> 87.3 us
  starting transfers between devices: 42.9 us -> 34.4 us
    ppermute x19, waiting for transfers between devices: 35 us -> 42 us  [shift_back(): return lax.ppermute(array, 'expert', pairs)]
    ppermute x6, starting transfers between devices: 8.67 us -> 2.97 us  [shift_plane(): lax.ppermute(array, 'rep', [(r, (r + by) % reps) for r in range(reps)])]
    ppermute x16, waiting for transfers between devices: 15.7 us -> 20 us  [shift_owner(): lax.ppermute(array, 'expert', pairs if by >= 0 else [(b, a) for a, b in p...]
    ppermute x19, starting transfers between devices: 15.6 us -> 12.6 us  [shift_back(): return lax.ppermute(array, 'expert', pairs)]
    ppermute x6, waiting for transfers between devices: 27.1 us -> 25.3 us  [shift_plane(): lax.ppermute(array, 'rep', [(r, (r + by) % reps) for r in range(reps)])]
  transfers between devices with their start and end apart: 41 -> 41, of which waited for: 23 -> 25; matrix products, arithmetic and copies ran while one was open for 1% -> 1% of each run, Pallas kernels for 18% -> 17%
where the time goes in v4:
time: 160 us; the launch traced here: 159 us
  waiting for transfers between devices  87.3 us (55%)
  starting transfers between devices  34.4 us (22%)
  Pallas kernels  29.4 us (18%)
  local copies, waits for them, and re-layouts  6.97 us (4%)
    ppermute x19, waiting for transfers between devices, shift_back(): return lax.ppermute(array, 'expert', pairs)  42 us
    ppermute x6, waiting for transfers between devices, shift_plane(): lax.ppermute(array, 'rep', [(r, (r + by) % reps) for r in range(reps)])  25.3 us
    ppermute x16, waiting for transfers between devices, shift_owner(): lax.ppermute(array, 'expert', pairs if by >= 0 else [(b, a) for a, b in p...  20 us
    ppermute x16, starting transfers between devices, shift_owner(): lax.ppermute(array, 'expert', pairs if by >= 0 else [(b, a) for a, b in p...  18.8 us
    pallas_call x4, Pallas kernels, apply_experts(): pl.pallas_call(functools.partial(experts_kernel, count), out_shape=[jax.S...  15.3 us
    ppermute x19, starting transfers between devices, shift_back(): return lax.ppermute(array, 'expert', pairs)  12.6 us
    pallas_call x4, Pallas kernels, combine(): pl.pallas_call(functools.partial(combine_kernel, rows, cap, top, dense, h...  8.22 us
    unnamed x16, local copies, waits for them, and re-layouts  6.97 us
  transfers between devices with their start and end apart: 41, of which 25 were waited for; matrix products, arithmetic and copies ran while one was open for 1% of the time, Pallas kernels for 17%

profile of v4, /device:TPU:0, one launch (start us, length us, event | category | flops | bytes accessed | tf_op | source)
XLA Modules:
  0.0 159.3 jit_solution(10117409915953994510)
XLA Ops:
  0.0 1.0 copy-done
  1.0 0.8 copy-done.1
  1.8 0.7 copy-done.2
  2.5 0.7 copy-done.3
  3.4 3.0 %collective-permute-start.3 = (bf16[144,2048]{1,0:T(8,128)(2,1)S(1)}, bf16[144,2048]{1,0:T(8,128)(2,1)S(1)}, u32[]{:S(2)}, u32[]{:S(2)}) collective-permute-start(bf16[144,2048]{1,0:T(8,128)(2,1)S(1)} %pack.1.refs_0_), channel_id=1, source_target_pairs={{0,2},{1,5},{2,0},{3,7},{4,6},{5,1},{6,4},{7,3},{8,10},{9,13},{10,... | collective-permute-start | bytes 1769480 | tf_op jit(solution)/shard_map/ppermute | solution.py:186
  6.4 1.6 collective-permute-start
  8.1 0.9 compare_convert_fusion.groups_ref
  9.0 5.3 %collective-permute-done.3.refs_1_ = bf16[144,2048]{1,0:T(8,128)(2,1)S(1)} collective-permute-done((bf16[144,2048]{1,0:T(8,128)(2,1)S(1)}, bf16[144,2048]{1,0:T(8,128)(2,1)S(1)}, u32[]{:S(2)}, u32[]{:S(2)}) %collective-permute-start.3) | collective-permute-done | bytes 589856 | tf_op jit(solution)/shard_map/ppermute | solution.py:186
  14.3 1.0 select.24
  15.4 2.1 %collective-permute-start.5 = (bf16[96,2048]{1,0:T(8,128)(2,1)S(1)}, bf16[96,2048]{1,0:T(8,128)(2,1)S(1)}, u32[]{:S(2)}, u32[]{:S(2)}) collective-permute-start(bf16[96,2048]{1,0:T(8,128)(2,1)S(1)} %get-tuple-element.76), channel_id=1, source_target_pairs={{0,4},{1,3},{2,6},{3,1},{4,0},{5,7},{6,2},{7,5},{8,12},{9,11},{10,... | collective-permute-start | bytes 1179656 | tf_op jit(solution)/shard_map/ppermute | solution.py:186
  17.5 1.2 collective-permute-start.6
  18.8 4.3 %collective-permute-done.refs_0_.refs_1_ = bf16[144,2048]{1,0:T(8,128)(2,1)S(1)} collective-permute-done((bf16[144,2048]{1,0:T(8,128)(2,1)S(1)}, bf16[144,2048]{1,0:T(8,128)(2,1)S(1)}, u32[]{:S(2)}, u32[]{:S(2)}) %collective-permute-start) | collective-permute-done | bytes 589856 | tf_op jit(solution)/shard_map/ppermute | solution.py:189
  23.3 2.0 %collective-permute-start.7 = (bf16[144,2048]{1,0:T(8,128)(2,1)S(1)}, bf16[144,2048]{1,0:T(8,128)(2,1)S(1)}, u32[]{:S(2)}, u32[]{:S(2)}) collective-permute-start(bf16[144,2048]{1,0:T(8,128)(2,1)S(1)} %collective-permute-done.refs_0_.refs_1_), channel_id=1, source_target_pairs={{0,2},{1,5},{2,0},{3,7},{4,6},{5,1},{6,4},{7,3},{8,10},{9,13},{10,... | collective-permute-start | bytes 1769480 | tf_op jit(solution)/shard_map/ppermute | solution.py:186
  25.3 3.7 %collective-permute-done.6.refs_3_ = bf16[96,2048]{1,0:T(8,128)(2,1)S(1)} collective-permute-done((bf16[96,2048]{1,0:T(8,128)(2,1)S(1)}, bf16[96,2048]{1,0:T(8,128)(2,1)S(1)}, u32[]{:S(2)}, u32[]{:S(2)}) %collective-permute-start.6) | collective-permute-done | bytes 393248 | tf_op jit(solution)/shard_map/ppermute | solution.py:186
  29.0 1.9 %copy-done.5 = bf16[1,2048,768]{2,1,0:T(8,128)(2,1)S(1)} copy-done((bf16[1,2048,768]{2,1,0:T(8,128)(2,1)S(1)}, bf16[1,2048,768]{2,1,0:T(8,128)(2,1)}, u32[]{:S(2)}) %copy-start.5) | copy-done | bytes 3145752
  30.9 1.9 %copy-done.7 = bf16[1,768,2048]{2,1,0:T(8,128)(2,1)S(1)} copy-done((bf16[1,768,2048]{2,1,0:T(8,128)(2,1)S(1)}, bf16[1,768,2048]{2,1,0:T(8,128)(2,1)}, u32[]{:S(2)}) %copy-start.7) | copy-done | bytes 3145752
  32.8 3.8 %experts.4 = (bf16[96,2048]{1,0:T(8,128)(2,1)S(1)}, bf16[96,2048]{1,0:T(8,128)(2,1)S(1)}, bf16[96,2048]{1,0:T(8,128)(2,1)S(1)}, bf16[96,2048]{1,0:T(8,128)(2,1)S(1)}) custom-call(bf16[96,2048]{1,0:T(8,128)(2,1)S(1)} %get-tuple-element.78.refs_0_, bf16[96,2048]{1,0:T(8,128)(2,1)S(1)} %collective-permute-done.4.refs_1_, ...), custom_call_target="tpu_custom_call" | custom-call | flops 4000000000 | tf_op jit(solution)/shard_map/experts/pallas_call | solution.py:249
  36.6 2.2 %collective-permute-done.1.refs_0_.refs_2_ = bf16[144,2048]{1,0:T(8,128)(2,1)S(1)} collective-permute-done((bf16[144,2048]{1,0:T(8,128)(2,1)S(1)}, bf16[144,2048]{1,0:T(8,128)(2,1)S(1)}, u32[]{:S(2)}, u32[]{:S(2)}) %collective-permute-start.1) | collective-permute-done | bytes 589856 | tf_op jit(solution)/shard_map/ppermute | solution.py:189
  38.9 1.0 select.25
  40.0 0.4 collective-permute-start.2
  40.4 1.3 collective-permute-done.8.refs_1_
  41.7 2.7 %collective-permute-start.9 = (bf16[144,2048]{1,0:T(8,128)(2,1)S(1)}, bf16[144,2048]{1,0:T(8,128)(2,1)S(1)}, u32[]{:S(2)}, u32[]{:S(2)}) collective-permute-start(bf16[144,2048]{1,0:T(8,128)(2,1)S(1)} %collective-permute-done.1.refs_0_.refs_2_), channel_id=1, source_target_pairs={{0,2},{1,5},{2,0},{3,7},{4,6},{5,1},{6,4},{7,3},{8,10},{9,13},{10,... | collective-permute-start | bytes 1769480 | tf_op jit(solution)/shard_map/ppermute | solution.py:186
  44.4 1.2 collective-permute-start.11
  45.6 11.9 %collective-permute-done.2.refs_0_.refs_3_ = bf16[144,2048]{1,0:T(8,128)(2,1)S(1)} collective-permute-done((bf16[144,2048]{1,0:T(8,128)(2,1)S(1)}, bf16[144,2048]{1,0:T(8,128)(2,1)S(1)}, u32[]{:S(2)}, u32[]{:S(2)}) %collective-permute-start.2) | collective-permute-done | bytes 589856 | tf_op jit(solution)/shard_map/ppermute | solution.py:189
  57.5 1.0 collective-permute-done.9.refs_1_
  58.5 1.0 select.26
  59.6 0.6 collective-permute-done.11.refs_3_
  60.1 1.7 %collective-permute-start.12 = (bf16[144,2048]{1,0:T(8,128)(2,1)S(1)}, bf16[144,2048]{1,0:T(8,128)(2,1)S(1)}, u32[]{:S(2)}, u32[]{:S(2)}) collective-permute-start(bf16[144,2048]{1,0:T(8,128)(2,1)S(1)} %collective-permute-done.2.refs_0_.refs_3_), channel_id=1, source_target_pairs={{0,2},{1,5},{2,0},{3,7},{4,6},{5,1},{6,4},{7,3},{8,10},{9,13},{10,... | collective-permute-start | bytes 1769480 | tf_op jit(solution)/shard_map/ppermute | solution.py:186
  62.0 1.8 %collective-permute-start.16 = (bf16[96,2048]{1,0:T(8,128)(2,1)S(1)}, bf16[96,2048]{1,0:T(8,128)(2,1)S(1)}, u32[]{:S(2)}, u32[]{:S(2)}) collective-permute-start(bf16[96,2048]{1,0:T(8,128)(2,1)S(1)} %get-tuple-element.102), channel_id=1, source_target_pairs={{0,1},{1,0},{2,3},{3,2},{4,5},{5,4},{6,7},{7,6},{8,9},{9,8},{10,11... | collective-permute-start | bytes 1179656 | tf_op jit(solution)/shard_map/ppermute | solution.py:186
  63.8 3.8 %experts.5 = (bf16[96,2048]{1,0:T(8,128)(2,1)S(1)}, bf16[96,2048]{1,0:T(8,128)(2,1)S(1)}, bf16[96,2048]{1,0:T(8,128)(2,1)S(1)}, bf16[96,2048]{1,0:T(8,128)(2,1)S(1)}) custom-call(bf16[96,2048]{1,0:T(8,128)(2,1)S(1)} %get-tuple-element.90.refs_0_, bf16[96,2048]{1,0:T(8,128)(2,1)S(1)} %collective-permute-done.8.refs_1_, ...), custom_call_target="tpu_custom_call" | custom-call | flops 4000000000 | tf_op jit(solution)/shard_map/experts/pallas_call | solution.py:249
  67.7 5.6 %collective-permute-done.18.refs_3_ = bf16[96,2048]{1,0:T(8,128)(2,1)S(1)} collective-permute-done((bf16[96,2048]{1,0:T(8,128)(2,1)S(1)}, bf16[96,2048]{1,0:T(8,128)(2,1)S(1)}, u32[]{:S(2)}, u32[]{:S(2)}) %collective-permute-start.18) | collective-permute-done | bytes 393248 | tf_op jit(solution)/shard_map/ppermute | solution.py:186
  73.4 2.2 %collective-permute-done.12.refs_1_ = bf16[144,2048]{1,0:T(8,128)(2,1)S(1)} collective-permute-done((bf16[144,2048]{1,0:T(8,128)(2,1)S(1)}, bf16[144,2048]{1,0:T(8,128)(2,1)S(1)}, u32[]{:S(2)}, u32[]{:S(2)}) %collective-permute-start.12) | collective-permute-done | bytes 589856 | tf_op jit(solution)/shard_map/ppermute | solution.py:186
  75.6 0.8 collective-permute-start.15
  76.4 1.0 select.27
  77.5 1.2 collective-permute-start.21
  78.6 1.6 collective-permute-start.20
  80.3 3.2 %collective-permute-done.14.refs_4_ = bf16[96,2048]{1,0:T(8,128)(2,1)S(1)} collective-permute-done((bf16[96,2048]{1,0:T(8,128)(2,1)S(1)}, bf16[96,2048]{1,0:T(8,128)(2,1)S(1)}, u32[]{:S(2)}, u32[]{:S(2)}) %collective-permute-start.14) | collective-permute-done | bytes 393248 | tf_op jit(solution)/shard_map/ppermute | solution.py:269
  83.5 3.6 %collective-permute-done.15.refs_5_ = bf16[96,2048]{1,0:T(8,128)(2,1)S(1)} collective-permute-done((bf16[96,2048]{1,0:T(8,128)(2,1)S(1)}, bf16[96,2048]{1,0:T(8,128)(2,1)S(1)}, u32[]{:S(2)}, u32[]{:S(2)}) %collective-permute-start.15) | collective-permute-done | bytes 393248 | tf_op jit(solution)/shard_map/ppermute | solution.py:269
  87.1 2.1 %combine.4 = (f32[128,2048]{1,0:T(8,128)S(1)}, bf16[128,2048]{1,0:T(8,128)(2,1)S(1)}) custom-call(f32[4,32]{1,0:T(4,128)S(1)} %compare_convert_fusion.groups_ref, bf16[32,2048]{1,0:T(8,128)(2,1)S(1)} %router.1.router_ref, bf16[144,2048]{1,0:T(8,128)(2,1)S(1)} %collective-permute-done.refs_0_.refs_1_, bf16[144,2048]{1,0:T(8,128)(2,1)S(1)} %collective-permute-done.7.refs_1_, ...), custom_call_target="tpu_custom_call" | custom-call | flops 2000000000 | tf_op jit(solution)/shard_map/combine/pallas_call | solution.py:272
  89.2 2.6 %collective-permute-start.22 = (bf16[128,2048]{1,0:T(8,128)(2,1)S(1)}, bf16[128,2048]{1,0:T(8,128)(2,1)S(1)}, u32[]{:S(2)}, u32[]{:S(2)}) collective-permute-start(bf16[128,2048]{1,0:T(8,128)(2,1)S(1)} %get-tuple-element.117), channel_id=1, source_target_pairs={{2,0},{5,1},{0,2},{7,3},{6,4},{1,5},{4,6},{3,7},{10,8},{13,9},{8,1... | collective-permute-start | bytes 1572872 | tf_op jit(solution)/shard_map/ppermute | solution.py:269
  91.7 3.8 %experts.6 = (bf16[96,2048]{1,0:T(8,128)(2,1)S(1)}, bf16[96,2048]{1,0:T(8,128)(2,1)S(1)}, bf16[96,2048]{1,0:T(8,128)(2,1)S(1)}, bf16[96,2048]{1,0:T(8,128)(2,1)S(1)}) custom-call(bf16[96,2048]{1,0:T(8,128)(2,1)S(1)} %get-tuple-element.100.refs_0_, bf16[96,2048]{1,0:T(8,128)(2,1)S(1)} %collective-permute-done.16.refs_1_, ...), custom_call_target="tpu_custom_call" | custom-call | flops 4000000000 | tf_op jit(solution)/shard_map/experts/pallas_call | solution.py:249
  96.0 1.9 %collective-permute-start.25 = (bf16[96,2048]{1,0:T(8,128)(2,1)S(1)}, bf16[96,2048]{1,0:T(8,128)(2,1)S(1)}, u32[]{:S(2)}, u32[]{:S(2)}) collective-permute-start(bf16[96,2048]{1,0:T(8,128)(2,1)S(1)} %get-tuple-element.121), channel_id=1, source_target_pairs={{5,0},{2,1},{7,2},{0,3},{1,4},{6,5},{3,6},{4,7},{13,8},{10,9},{15,... | collective-permute-start | bytes 1179656 | tf_op jit(solution)/shard_map/ppermute | solution.py:269
  97.9 3.8 %experts.7 = (bf16[96,2048]{1,0:T(8,128)(2,1)S(1)}, bf16[96,2048]{1,0:T(8,128)(2,1)S(1)}, bf16[96,2048]{1,0:T(8,128)(2,1)S(1)}, bf16[96,2048]{1,0:T(8,128)(2,1)S(1)}) custom-call(bf16[96,2048]{1,0:T(8,128)(2,1)S(1)} %get-tuple-element.108.refs_0_, bf16[96,2048]{1,0:T(8,128)(2,1)S(1)} %collective-permute-done.19.refs_1_, ...), custom_call_target="tpu_custom_call" | custom-call | flops 4000000000 | tf_op jit(solution)/shard_map/experts/pallas_call | solution.py:249
  101.7 1.5 collective-permute-done.22.refs_0_
  103.3 0.5 collective-permute-start.28
  103.8 3.9 %collective-permute-done.24.refs_4_ = bf16[96,2048]{1,0:T(8,128)(2,1)S(1)} collective-permute-done((bf16[96,2048]{1,0:T(8,128)(2,1)S(1)}, bf16[96,2048]{1,0:T(8,128)(2,1)S(1)}, u32[]{:S(2)}, u32[]{:S(2)}) %collective-permute-start.24) | collective-permute-done | bytes 393248 | tf_op jit(solution)/shard_map/ppermute | solution.py:269
  107.8 0.6 collective-permute-done.25.refs_5_
  108.3 2.1 %combine.5 = (f32[128,2048]{1,0:T(8,128)S(1)}, bf16[64,2048]{1,0:T(8,128)(2,1)S(1)}, bf16[64,2048]{1,0:T(8,128)(2,1)S(1)}) custom-call(f32[4,32]{1,0:T(4,128)S(1)} %compare_convert_fusion.groups_ref, bf16[32,2048]{1,0:T(8,128)(2,1)S(1)} %router.1.router_ref, bf16[144,2048]{1,0:T(8,128)(2,1)S(1)} %collective-permute-done.1.refs_0_.refs_2_, ...), custom_call_target="tpu_custom_call" | custom-call | flops 2000000000 | tf_op jit(solution)/shard_map/combine/pallas_call | solution.py:272
  110.4 2.0 %collective-permute-start.26 = (bf16[64,2048]{1,0:T(8,128)(2,1)S(1)}, bf16[64,2048]{1,0:T(8,128)(2,1)S(1)}, u32[]{:S(2)}, u32[]{:S(2)}) collective-permute-start(bf16[64,2048]{1,0:T(8,128)(2,1)S(1)} %get-tuple-element.124), channel_id=1, source_target_pairs={{2,0},{5,1},{0,2},{7,3},{6,4},{1,5},{4,6},{3,7},{10,8},{13,9},{8,1... | collective-permute-start | bytes 786440 | tf_op jit(solution)/shard_map/ppermute | solution.py:269
  112.7 5.5 %collective-permute-done.26.refs_0_ = bf16[64,2048]{1,0:T(8,128)(2,1)S(1)} collective-permute-done((bf16[64,2048]{1,0:T(8,128)(2,1)S(1)}, bf16[64,2048]{1,0:T(8,128)(2,1)S(1)}, u32[]{:S(2)}, u32[]{:S(2)}) %collective-permute-start.26) | collective-permute-done | bytes 262176 | tf_op jit(solution)/shard_map/ppermute | solution.py:269
  118.2 5.3 %collective-permute-done.27.refs_1_ = bf16[64,2048]{1,0:T(8,128)(2,1)S(1)} collective-permute-done((bf16[64,2048]{1,0:T(8,128)(2,1)S(1)}, bf16[64,2048]{1,0:T(8,128)(2,1)S(1)}, u32[]{:S(2)}, u32[]{:S(2)}) %collective-permute-start.27) | collective-permute-done | bytes 262176 | tf_op jit(solution)/shard_map/ppermute | solution.py:269
  124.0 0.6 collective-permute-done.30.refs_4_
  124.5 3.7 %collective-permute-done.31.refs_5_ = bf16[96,2048]{1,0:T(8,128)(2,1)S(1)} collective-permute-done((bf16[96,2048]{1,0:T(8,128)(2,1)S(1)}, bf16[96,2048]{1,0:T(8,128)(2,1)S(1)}, u32[]{:S(2)}, u32[]{:S(2)}) %collective-permute-start.31) | collective-permute-done | bytes 393248 | tf_op jit(solution)/shard_map/ppermute | solution.py:269
  128.2 2.1 %combine.6 = (f32[128,2048]{1,0:T(8,128)S(1)}, bf16[64,2048]{1,0:T(8,128)(2,1)S(1)}, bf16[64,2048]{1,0:T(8,128)(2,1)S(1)}) custom-call(f32[4,32]{1,0:T(4,128)S(1)} %compare_convert_fusion.groups_ref, bf16[32,2048]{1,0:T(8,128)(2,1)S(1)} %router.1.router_ref, bf16[144,2048]{1,0:T(8,128)(2,1)S(1)} %collective-permute-done.2.refs_0_.refs_3_, ...), custom_call_target="tpu_custom_call" | custom-call | flops 2000000000 | tf_op jit(solution)/shard_map/combine/pallas_call | solution.py:272
  130.3 1.2 collective-permute-start.32
  131.5 0.9 collective-permute-start.33
  132.7 6.8 %collective-permute-done.34.refs_2_ = bf16[128,2048]{1,0:T(8,128)(2,1)S(1)} collective-permute-done((bf16[128,2048]{1,0:T(8,128)(2,1)S(1)}, bf16[128,2048]{1,0:T(8,128)(2,1)S(1)}, u32[]{:S(2)}, u32[]{:S(2)}) %collective-permute-start.34) | collective-permute-done | bytes 524320 | tf_op jit(solution)/shard_map/ppermute | solution.py:189
  139.5 4.0 %collective-permute-done.33.refs_1_ = bf16[64,2048]{1,0:T(8,128)(2,1)S(1)} collective-permute-done((bf16[64,2048]{1,0:T(8,128)(2,1)S(1)}, bf16[64,2048]{1,0:T(8,128)(2,1)S(1)}, u32[]{:S(2)}, u32[]{:S(2)}) %collective-permute-start.33) | collective-permute-done | bytes 262176 | tf_op jit(solution)/shard_map/ppermute | solution.py:269
  143.9 3.0 %collective-permute-done.37.refs_5_ = bf16[96,2048]{1,0:T(8,128)(2,1)S(1)} collective-permute-done((bf16[96,2048]{1,0:T(8,128)(2,1)S(1)}, bf16[96,2048]{1,0:T(8,128)(2,1)S(1)}, u32[]{:S(2)}, u32[]{:S(2)}) %collective-permute-start.37) | collective-permute-done | bytes 393248 | tf_op jit(solution)/shard_map/ppermute | solution.py:269
  146.9 2.1 %combine.7 = (f32[128,2048]{1,0:T(8,128)S(1)}, bf16[64,2048]{1,0:T(8,128)(2,1)S(1)}, bf16[64,2048]{1,0:T(8,128)(2,1)S(1)}) custom-call(f32[4,32]{1,0:T(4,128)S(1)} %compare_convert_fusion.groups_ref, bf16[32,2048]{1,0:T(8,128)(2,1)S(1)} %router.1.router_ref, bf16[144,2048]{1,0:T(8,128)(2,1)S(1)} %pack.1.refs_0_, ...), custom_call_target="tpu_custom_call" | custom-call | flops 2000000000 | tf_op jit(solution)/shard_map/combine/pallas_call | solution.py:272
  149.0 1.7 %collective-permute-start.38 = (bf16[64,2048]{1,0:T(8,128)(2,1)S(1)}, bf16[64,2048]{1,0:T(8,128)(2,1)S(1)}, u32[]{:S(2)}, u32[]{:S(2)}) collective-permute-start(bf16[64,2048]{1,0:T(8,128)(2,1)S(1)} %get-tuple-element.143), channel_id=1, source_target_pairs={{2,0},{5,1},{0,2},{7,3},{6,4},{1,5},{4,6},{3,7},{10,8},{13,9},{8,1... | collective-permute-start | bytes 786440 | tf_op jit(solution)/shard_map/ppermute | solution.py:269
  151.1 4.3 %collective-permute-done.38.refs_0_ = bf16[64,2048]{1,0:T(8,128)(2,1)S(1)} collective-permute-done((bf16[64,2048]{1,0:T(8,128)(2,1)S(1)}, bf16[64,2048]{1,0:T(8,128)(2,1)S(1)}, u32[]{:S(2)}, u32[]{:S(2)}) %collective-permute-start.38) | collective-permute-done | bytes 262176 | tf_op jit(solution)/shard_map/ppermute | solution.py:269
  155.4 2.8 %collective-permute-done.39.refs_1_ = bf16[64,2048]{1,0:T(8,128)(2,1)S(1)} collective-permute-done((bf16[64,2048]{1,0:T(8,128)(2,1)S(1)}, bf16[64,2048]{1,0:T(8,128)(2,1)S(1)}, u32[]{:S(2)}, u32[]{:S(2)}) %collective-permute-start.39) | collective-permute-done | bytes 262176 | tf_op jit(solution)/shard_map/ppermute | solution.py:269
  158.3 1.0 add.122
  (54 shorter events, 3.4 us)
Async XLA Ops:
  0.0 1.0 copy-start
  1.0 0.8 copy-start.1
  1.8 0.7 copy-start.2
  2.5 0.7 copy-start.3
  3.4 10.9 %collective-permute-start.3 = (bf16[144,2048]{1,0:T(8,128)(2,1)S(1)}, bf16[144,2048]{1,0:T(8,128)(2,1)S(1)}, u32[]{:S(2)}, u32[]{:S(2)}) collective-permute-start(bf16[144,2048]{1,0:T(8,128)(2,1)S(1)} %pack.1.refs_0_), channel_id=1, source_target_pairs={{0,2},{1,5},{2,0},{3,7},{4,6},{5,1},{6,4},{7,3},{8,10},{9,13},{10,... | collective-permute-start | bytes 1769480 | tf_op jit(solution)/shard_map/ppermute | solution.py:186
  6.4 16.7 %collective-permute-start = (bf16[144,2048]{1,0:T(8,128)(2,1)S(1)}, bf16[144,2048]{1,0:T(8,128)(2,1)S(1)}, u32[]{:S(2)}, u32[]{:S(2)}) collective-permute-start(bf16[144,2048]{1,0:T(8,128)(2,1)S(1)} %pack.1.refs_0_), channel_id=1, source_target_pairs={{0,8},{8,16},{16,24},{24,0},{1,9},{9,17},{17,25},{25,1},{2,10},{10... | collective-permute-start | bytes 1769480 | tf_op jit(solution)/shard_map/ppermute | solution.py:189
  8.0 21.0 %copy-start.4 = (bf16[1,2048,768]{2,1,0:T(8,128)(2,1)S(1)}, bf16[1,2048,768]{2,1,0:T(8,128)(2,1)}, u32[]{:S(2)}) copy-start(bf16[1,2048,768]{2,1,0:T(8,128)(2,1)} %refs_4_.7) | copy-start | bytes 9437188
  15.3 7.8 %collective-permute-start.4 = (bf16[96,2048]{1,0:T(8,128)(2,1)S(1)}, bf16[96,2048]{1,0:T(8,128)(2,1)S(1)}, u32[]{:S(2)}, u32[]{:S(2)}) collective-permute-start(bf16[96,2048]{1,0:T(8,128)(2,1)S(1)} %get-tuple-element.75), channel_id=1, source_target_pairs={{0,1},{1,0},{2,3},{3,2},{4,5},{5,4},{6,7},{7,6},{8,9},{9,8},{10,11... | collective-permute-start | bytes 1179656 | tf_op jit(solution)/shard_map/ppermute | solution.py:186
  15.4 7.9 %collective-permute-start.5 = (bf16[96,2048]{1,0:T(8,128)(2,1)S(1)}, bf16[96,2048]{1,0:T(8,128)(2,1)S(1)}, u32[]{:S(2)}, u32[]{:S(2)}) collective-permute-start(bf16[96,2048]{1,0:T(8,128)(2,1)S(1)} %get-tuple-element.76), channel_id=1, source_target_pairs={{0,4},{1,3},{2,6},{3,1},{4,0},{5,7},{6,2},{7,5},{8,12},{9,11},{10,... | collective-permute-start | bytes 1179656 | tf_op jit(solution)/shard_map/ppermute | solution.py:186
  17.5 11.5 %collective-permute-start.6 = (bf16[96,2048]{1,0:T(8,128)(2,1)S(1)}, bf16[96,2048]{1,0:T(8,128)(2,1)S(1)}, u32[]{:S(2)}, u32[]{:S(2)}) collective-permute-start(bf16[96,2048]{1,0:T(8,128)(2,1)S(1)} %get-tuple-element.79), channel_id=1, source_target_pairs={{0,5},{1,2},{2,7},{3,0},{4,1},{5,6},{6,3},{7,4},{8,13},{9,10},{10,... | collective-permute-start | bytes 1179656 | tf_op jit(solution)/shard_map/ppermute | solution.py:186
  23.1 15.8 %collective-permute-start.1 = (bf16[144,2048]{1,0:T(8,128)(2,1)S(1)}, bf16[144,2048]{1,0:T(8,128)(2,1)S(1)}, u32[]{:S(2)}, u32[]{:S(2)}) collective-permute-start(bf16[144,2048]{1,0:T(8,128)(2,1)S(1)} %collective-permute-done.refs_0_.refs_1_), channel_id=1, source_target_pairs={{0,8},{8,16},{16,24},{24,0},{1,9},{9,17},{17,25},{25,1},{2,10},{10... | collective-permute-start | bytes 1769480 | tf_op jit(solution)/shard_map/ppermute | solution.py:189
  23.3 15.6 %collective-permute-start.7 = (bf16[144,2048]{1,0:T(8,128)(2,1)S(1)}, bf16[144,2048]{1,0:T(8,128)(2,1)S(1)}, u32[]{:S(2)}, u32[]{:S(2)}) collective-permute-start(bf16[144,2048]{1,0:T(8,128)(2,1)S(1)} %collective-permute-done.refs_0_.refs_1_), channel_id=1, source_target_pairs={{0,2},{1,5},{2,0},{3,7},{4,6},{5,1},{6,4},{7,3},{8,10},{9,13},{10,... | collective-permute-start | bytes 1769480 | tf_op jit(solution)/shard_map/ppermute | solution.py:186
  29.0 1.9 %copy-start.5 = (bf16[1,2048,768]{2,1,0:T(8,128)(2,1)S(1)}, bf16[1,2048,768]{2,1,0:T(8,128)(2,1)}, u32[]{:S(2)}) copy-start(bf16[1,2048,768]{2,1,0:T(8,128)(2,1)} %refs_5_.7) | copy-start | bytes 9437188
  30.9 1.9 %copy-start.7 = (bf16[1,768,2048]{2,1,0:T(8,128)(2,1)S(1)}, bf16[1,768,2048]{2,1,0:T(8,128)(2,1)}, u32[]{:S(2)}) copy-start(bf16[1,768,2048]{2,1,0:T(8,128)(2,1)} %refs_6_.7) | copy-start | bytes 9437188
  38.9 24.9 %copy-start.6 = (bf16[1,2048,768]{2,1,0:T(8,128)(2,1)S(1)}, bf16[1,2048,768]{2,1,0:T(8,128)(2,1)}, u32[]{:S(2)}) copy-start(bf16[1,2048,768]{2,1,0:T(8,128)(2,1)} %refs_5_.7) | copy-start | bytes 9437188
  39.9 1.8 %collective-permute-start.8 = (bf16[96,2048]{1,0:T(8,128)(2,1)S(1)}, bf16[96,2048]{1,0:T(8,128)(2,1)S(1)}, u32[]{:S(2)}, u32[]{:S(2)}) collective-permute-start(bf16[96,2048]{1,0:T(8,128)(2,1)S(1)} %get-tuple-element.83), channel_id=1, source_target_pairs={{0,1},{1,0},{2,3},{3,2},{4,5},{5,4},{6,7},{7,6},{8,9},{9,8},{10,11... | collective-permute-start | bytes 1179656 | tf_op jit(solution)/shard_map/ppermute | solution.py:186
  40.0 17.5 %collective-permute-start.2 = (bf16[144,2048]{1,0:T(8,128)(2,1)S(1)}, bf16[144,2048]{1,0:T(8,128)(2,1)S(1)}, u32[]{:S(2)}, u32[]{:S(2)}) collective-permute-start(bf16[144,2048]{1,0:T(8,128)(2,1)S(1)} %collective-permute-done.1.refs_0_.refs_2_), channel_id=1, source_target_pairs={{0,8},{8,16},{16,24},{24,0},{1,9},{9,17},{17,25},{25,1},{2,10},{10... | collective-permute-start | bytes 1769480 | tf_op jit(solution)/shard_map/ppermute | solution.py:189
  41.7 16.8 %collective-permute-start.9 = (bf16[144,2048]{1,0:T(8,128)(2,1)S(1)}, bf16[144,2048]{1,0:T(8,128)(2,1)S(1)}, u32[]{:S(2)}, u32[]{:S(2)}) collective-permute-start(bf16[144,2048]{1,0:T(8,128)(2,1)S(1)} %collective-permute-done.1.refs_0_.refs_2_), channel_id=1, source_target_pairs={{0,2},{1,5},{2,0},{3,7},{4,6},{5,1},{6,4},{7,3},{8,10},{9,13},{10,... | collective-permute-start | bytes 1769480 | tf_op jit(solution)/shard_map/ppermute | solution.py:186
  44.4 15.2 %collective-permute-start.10 = (bf16[96,2048]{1,0:T(8,128)(2,1)S(1)}, bf16[96,2048]{1,0:T(8,128)(2,1)S(1)}, u32[]{:S(2)}, u32[]{:S(2)}) collective-permute-start(bf16[96,2048]{1,0:T(8,128)(2,1)S(1)} %get-tuple-element.87), channel_id=1, source_target_pairs={{0,4},{1,3},{2,6},{3,1},{4,0},{5,7},{6,2},{7,5},{8,12},{9,11},{10,... | collective-permute-start | bytes 1179656 | tf_op jit(solution)/shard_map/ppermute | solution.py:186
  44.4 15.7 %collective-permute-start.11 = (bf16[96,2048]{1,0:T(8,128)(2,1)S(1)}, bf16[96,2048]{1,0:T(8,128)(2,1)S(1)}, u32[]{:S(2)}, u32[]{:S(2)}) collective-permute-start(bf16[96,2048]{1,0:T(8,128)(2,1)S(1)} %get-tuple-element.88), channel_id=1, source_target_pairs={{0,5},{1,2},{2,7},{3,0},{4,1},{5,6},{6,3},{7,4},{8,13},{9,10},{10,... | collective-permute-start | bytes 1179656 | tf_op jit(solution)/shard_map/ppermute | solution.py:186
  60.1 15.5 %collective-permute-start.12 = (bf16[144,2048]{1,0:T(8,128)(2,1)S(1)}, bf16[144,2048]{1,0:T(8,128)(2,1)S(1)}, u32[]{:S(2)}, u32[]{:S(2)}) collective-permute-start(bf16[144,2048]{1,0:T(8,128)(2,1)S(1)} %collective-permute-done.2.refs_0_.refs_3_), channel_id=1, source_target_pairs={{0,2},{1,5},{2,0},{3,7},{4,6},{5,1},{6,4},{7,3},{8,10},{9,13},{10,... | collective-permute-start | bytes 1769480 | tf_op jit(solution)/shard_map/ppermute | solution.py:186
  61.9 11.4 %collective-permute-start.18 = (bf16[96,2048]{1,0:T(8,128)(2,1)S(1)}, bf16[96,2048]{1,0:T(8,128)(2,1)S(1)}, u32[]{:S(2)}, u32[]{:S(2)}) collective-permute-start(bf16[96,2048]{1,0:T(8,128)(2,1)S(1)} %get-tuple-element.106), channel_id=1, source_target_pairs={{0,5},{1,2},{2,7},{3,0},{4,1},{5,6},{6,3},{7,4},{8,13},{9,10},{10,... | collective-permute-start | bytes 1179656 | tf_op jit(solution)/shard_map/ppermute | solution.py:186
  61.9 15.6 %collective-permute-start.17 = (bf16[96,2048]{1,0:T(8,128)(2,1)S(1)}, bf16[96,2048]{1,0:T(8,128)(2,1)S(1)}, u32[]{:S(2)}, u32[]{:S(2)}) collective-permute-start(bf16[96,2048]{1,0:T(8,128)(2,1)S(1)} %get-tuple-element.104), channel_id=1, source_target_pairs={{0,4},{1,3},{2,6},{3,1},{4,0},{5,7},{6,2},{7,5},{8,12},{9,11},{10,... | collective-permute-start | bytes 1179656 | tf_op jit(solution)/shard_map/ppermute | solution.py:186
  62.0 15.5 %collective-permute-start.16 = (bf16[96,2048]{1,0:T(8,128)(2,1)S(1)}, bf16[96,2048]{1,0:T(8,128)(2,1)S(1)}, u32[]{:S(2)}, u32[]{:S(2)}) collective-permute-start(bf16[96,2048]{1,0:T(8,128)(2,1)S(1)} %get-tuple-element.102), channel_id=1, source_target_pairs={{0,1},{1,0},{2,3},{3,2},{4,5},{5,4},{6,7},{7,6},{8,9},{9,8},{10,11... | collective-permute-start | bytes 1179656 | tf_op jit(solution)/shard_map/ppermute | solution.py:186
  67.6 12.6 %collective-permute-start.13 = (bf16[96,2048]{1,0:T(8,128)(2,1)S(1)}, bf16[96,2048]{1,0:T(8,128)(2,1)S(1)}, u32[]{:S(2)}, u32[]{:S(2)}) collective-permute-start(bf16[96,2048]{1,0:T(8,128)(2,1)S(1)} %get-tuple-element.96), channel_id=1, source_target_pairs={{1,0},{0,1},{3,2},{2,3},{5,4},{4,5},{7,6},{6,7},{9,8},{8,9},{11,10... | collective-permute-start | bytes 1179656 | tf_op jit(solution)/shard_map/ppermute | solution.py:269
  73.3 10.2 %collective-permute-start.14 = (bf16[96,2048]{1,0:T(8,128)(2,1)S(1)}, bf16[96,2048]{1,0:T(8,128)(2,1)S(1)}, u32[]{:S(2)}, u32[]{:S(2)}) collective-permute-start(bf16[96,2048]{1,0:T(8,128)(2,1)S(1)} %get-tuple-element.97), channel_id=1, source_target_pairs={{4,0},{3,1},{6,2},{1,3},{0,4},{7,5},{2,6},{5,7},{12,8},{11,9},{14,... | collective-permute-start | bytes 1179656 | tf_op jit(solution)/shard_map/ppermute | solution.py:269
  75.6 11.5 %collective-permute-start.15 = (bf16[96,2048]{1,0:T(8,128)(2,1)S(1)}, bf16[96,2048]{1,0:T(8,128)(2,1)S(1)}, u32[]{:S(2)}, u32[]{:S(2)}) collective-permute-start(bf16[96,2048]{1,0:T(8,128)(2,1)S(1)} %get-tuple-element.98), channel_id=1, source_target_pairs={{5,0},{2,1},{7,2},{0,3},{1,4},{6,5},{3,6},{4,7},{13,8},{10,9},{15,... | collective-permute-start | bytes 1179656 | tf_op jit(solution)/shard_map/ppermute | solution.py:269
  77.5 18.2 %collective-permute-start.21 = (bf16[96,2048]{1,0:T(8,128)(2,1)S(1)}, bf16[96,2048]{1,0:T(8,128)(2,1)S(1)}, u32[]{:S(2)}, u32[]{:S(2)}) collective-permute-start(bf16[96,2048]{1,0:T(8,128)(2,1)S(1)} %get-tuple-element.114), channel_id=1, source_target_pairs={{0,5},{1,2},{2,7},{3,0},{4,1},{5,6},{6,3},{7,4},{8,13},{9,10},{10,... | collective-permute-start | bytes 1179656 | tf_op jit(solution)/shard_map/ppermute | solution.py:186
  78.6 17.4 %collective-permute-start.20 = (bf16[96,2048]{1,0:T(8,128)(2,1)S(1)}, bf16[96,2048]{1,0:T(8,128)(2,1)S(1)}, u32[]{:S(2)}, u32[]{:S(2)}) collective-permute-start(bf16[96,2048]{1,0:T(8,128)(2,1)S(1)} %get-tuple-element.112), channel_id=1, source_target_pairs={{0,4},{1,3},{2,6},{3,1},{4,0},{5,7},{6,2},{7,5},{8,12},{9,11},{10,... | collective-permute-start | bytes 1179656 | tf_op jit(solution)/shard_map/ppermute | solution.py:186
  80.2 17.7 %collective-permute-start.19 = (bf16[96,2048]{1,0:T(8,128)(2,1)S(1)}, bf16[96,2048]{1,0:T(8,128)(2,1)S(1)}, u32[]{:S(2)}, u32[]{:S(2)}) collective-permute-start(bf16[96,2048]{1,0:T(8,128)(2,1)S(1)} %get-tuple-element.110), channel_id=1, source_target_pairs={{0,1},{1,0},{2,3},{3,2},{4,5},{5,4},{6,7},{7,6},{8,9},{9,8},{10,11... | collective-permute-start | bytes 1179656 | tf_op jit(solution)/shard_map/ppermute | solution.py:186
  89.2 14.1 %collective-permute-start.22 = (bf16[128,2048]{1,0:T(8,128)(2,1)S(1)}, bf16[128,2048]{1,0:T(8,128)(2,1)S(1)}, u32[]{:S(2)}, u32[]{:S(2)}) collective-permute-start(bf16[128,2048]{1,0:T(8,128)(2,1)S(1)} %get-tuple-element.117), channel_id=1, source_target_pairs={{2,0},{5,1},{0,2},{7,3},{6,4},{1,5},{4,6},{3,7},{10,8},{13,9},{8,1... | collective-permute-start | bytes 1572872 | tf_op jit(solution)/shard_map/ppermute | solution.py:269
  95.6 8.3 %collective-permute-start.23 = (bf16[96,2048]{1,0:T(8,128)(2,1)S(1)}, bf16[96,2048]{1,0:T(8,128)(2,1)S(1)}, u32[]{:S(2)}, u32[]{:S(2)}) collective-permute-start(bf16[96,2048]{1,0:T(8,128)(2,1)S(1)} %get-tuple-element.119), channel_id=1, source_target_pairs={{1,0},{0,1},{3,2},{2,3},{5,4},{4,5},{7,6},{6,7},{9,8},{8,9},{11,10... | collective-permute-start | bytes 1179656 | tf_op jit(solution)/shard_map/ppermute | solution.py:269
  95.6 12.1 %collective-permute-start.24 = (bf16[96,2048]{1,0:T(8,128)(2,1)S(1)}, bf16[96,2048]{1,0:T(8,128)(2,1)S(1)}, u32[]{:S(2)}, u32[]{:S(2)}) collective-permute-start(bf16[96,2048]{1,0:T(8,128)(2,1)S(1)} %get-tuple-element.120), channel_id=1, source_target_pairs={{4,0},{3,1},{6,2},{1,3},{0,4},{7,5},{2,6},{5,7},{12,8},{11,9},{14,... | collective-permute-start | bytes 1179656 | tf_op jit(solution)/shard_map/ppermute | solution.py:269
  96.0 12.3 %collective-permute-start.25 = (bf16[96,2048]{1,0:T(8,128)(2,1)S(1)}, bf16[96,2048]{1,0:T(8,128)(2,1)S(1)}, u32[]{:S(2)}, u32[]{:S(2)}) collective-permute-start(bf16[96,2048]{1,0:T(8,128)(2,1)S(1)} %get-tuple-element.121), channel_id=1, source_target_pairs={{5,0},{2,1},{7,2},{0,3},{1,4},{6,5},{3,6},{4,7},{13,8},{10,9},{15,... | collective-permute-start | bytes 1179656 | tf_op jit(solution)/shard_map/ppermute | solution.py:269
  103.3 14.9 %collective-permute-start.28 = (bf16[128,2048]{1,0:T(8,128)(2,1)S(1)}, bf16[128,2048]{1,0:T(8,128)(2,1)S(1)}, u32[]{:S(2)}, u32[]{:S(2)}) collective-permute-start(bf16[128,2048]{1,0:T(8,128)(2,1)S(1)} %add.119), channel_id=1, source_target_pairs={{0,8},{8,16},{16,24},{24,0},{1,9},{9,17},{17,25},{25,1},{2,10},{10... | collective-permute-start | bytes 1572872 | tf_op jit(solution)/shard_map/ppermute | solution.py:189
  103.8 8.7 %collective-permute-start.29 = (bf16[96,2048]{1,0:T(8,128)(2,1)S(1)}, bf16[96,2048]{1,0:T(8,128)(2,1)S(1)}, u32[]{:S(2)}, u32[]{:S(2)}) collective-permute-start(bf16[96,2048]{1,0:T(8,128)(2,1)S(1)} %get-tuple-element.127), channel_id=1, source_target_pairs={{1,0},{0,1},{3,2},{2,3},{5,4},{4,5},{7,6},{6,7},{9,8},{8,9},{11,10... | collective-permute-start | bytes 1179656 | tf_op jit(solution)/shard_map/ppermute | solution.py:269
  110.4 7.8 %collective-permute-start.26 = (bf16[64,2048]{1,0:T(8,128)(2,1)S(1)}, bf16[64,2048]{1,0:T(8,128)(2,1)S(1)}, u32[]{:S(2)}, u32[]{:S(2)}) collective-permute-start(bf16[64,2048]{1,0:T(8,128)(2,1)S(1)} %get-tuple-element.124), channel_id=1, source_target_pairs={{2,0},{5,1},{0,2},{7,3},{6,4},{1,5},{4,6},{3,7},{10,8},{13,9},{8,1... | collective-permute-start | bytes 786440 | tf_op jit(solution)/shard_map/ppermute | solution.py:269
  112.4 11.2 %collective-permute-start.27 = (bf16[64,2048]{1,0:T(8,128)(2,1)S(1)}, bf16[64,2048]{1,0:T(8,128)(2,1)S(1)}, u32[]{:S(2)}, u32[]{:S(2)}) collective-permute-start(bf16[64,2048]{1,0:T(8,128)(2,1)S(1)} %get-tuple-element.125), channel_id=1, source_target_pairs={{2,0},{5,1},{0,2},{7,3},{6,4},{1,5},{4,6},{3,7},{10,8},{13,9},{8,1... | collective-permute-start | bytes 786440 | tf_op jit(solution)/shard_map/ppermute | solution.py:269
  112.5 12.1 %collective-permute-start.30 = (bf16[96,2048]{1,0:T(8,128)(2,1)S(1)}, bf16[96,2048]{1,0:T(8,128)(2,1)S(1)}, u32[]{:S(2)}, u32[]{:S(2)}) collective-permute-start(bf16[96,2048]{1,0:T(8,128)(2,1)S(1)} %get-tuple-element.129), channel_id=1, source_target_pairs={{4,0},{3,1},{6,2},{1,3},{0,4},{7,5},{2,6},{5,7},{12,8},{11,9},{14,... | collective-permute-start | bytes 1179656 | tf_op jit(solution)/shard_map/ppermute | solution.py:269
  118.2 10.0 %collective-permute-start.31 = (bf16[96,2048]{1,0:T(8,128)(2,1)S(1)}, bf16[96,2048]{1,0:T(8,128)(2,1)S(1)}, u32[]{:S(2)}, u32[]{:S(2)}) collective-permute-start(bf16[96,2048]{1,0:T(8,128)(2,1)S(1)} %get-tuple-element.131), channel_id=1, source_target_pairs={{5,0},{2,1},{7,2},{0,3},{1,4},{6,5},{3,6},{4,7},{13,8},{10,9},{15,... | collective-permute-start | bytes 1179656 | tf_op jit(solution)/shard_map/ppermute | solution.py:269
  123.7 15.8 %collective-permute-start.34 = (bf16[128,2048]{1,0:T(8,128)(2,1)S(1)}, bf16[128,2048]{1,0:T(8,128)(2,1)S(1)}, u32[]{:S(2)}, u32[]{:S(2)}) collective-permute-start(bf16[128,2048]{1,0:T(8,128)(2,1)S(1)} %add.120), channel_id=1, source_target_pairs={{0,8},{8,16},{16,24},{24,0},{1,9},{9,17},{17,25},{25,1},{2,10},{10... | collective-permute-start | bytes 1572872 | tf_op jit(solution)/shard_map/ppermute | solution.py:189
  130.3 9.2 %collective-permute-start.32 = (bf16[64,2048]{1,0:T(8,128)(2,1)S(1)}, bf16[64,2048]{1,0:T(8,128)(2,1)S(1)}, u32[]{:S(2)}, u32[]{:S(2)}) collective-permute-start(bf16[64,2048]{1,0:T(8,128)(2,1)S(1)} %get-tuple-element.133), channel_id=1, source_target_pairs={{2,0},{5,1},{0,2},{7,3},{6,4},{1,5},{4,6},{3,7},{10,8},{13,9},{8,1... | collective-permute-start | bytes 786440 | tf_op jit(solution)/shard_map/ppermute | solution.py:269
  131.5 12.0 %collective-permute-start.33 = (bf16[64,2048]{1,0:T(8,128)(2,1)S(1)}, bf16[64,2048]{1,0:T(8,128)(2,1)S(1)}, u32[]{:S(2)}, u32[]{:S(2)}) collective-permute-start(bf16[64,2048]{1,0:T(8,128)(2,1)S(1)} %get-tuple-element.134), channel_id=1, source_target_pairs={{2,0},{5,1},{0,2},{7,3},{6,4},{1,5},{4,6},{3,7},{10,8},{13,9},{8,1... | collective-permute-start | bytes 786440 | tf_op jit(solution)/shard_map/ppermute | solution.py:269
  132.4 11.5 %collective-permute-start.35 = (bf16[96,2048]{1,0:T(8,128)(2,1)S(1)}, bf16[96,2048]{1,0:T(8,128)(2,1)S(1)}, u32[]{:S(2)}, u32[]{:S(2)}) collective-permute-start(bf16[96,2048]{1,0:T(8,128)(2,1)S(1)} %get-tuple-element.137), channel_id=1, source_target_pairs={{1,0},{0,1},{3,2},{2,3},{5,4},{4,5},{7,6},{6,7},{9,8},{8,9},{11,10... | collective-permute-start | bytes 1179656 | tf_op jit(solution)/shard_map/ppermute | solution.py:269
  132.4 11.5 %collective-permute-start.36 = (bf16[96,2048]{1,0:T(8,128)(2,1)S(1)}, bf16[96,2048]{1,0:T(8,128)(2,1)S(1)}, u32[]{:S(2)}, u32[]{:S(2)}) collective-permute-start(bf16[96,2048]{1,0:T(8,128)(2,1)S(1)} %get-tuple-element.139), channel_id=1, source_target_pairs={{4,0},{3,1},{6,2},{1,3},{0,4},{7,5},{2,6},{5,7},{12,8},{11,9},{14,... | collective-permute-start | bytes 1179656 | tf_op jit(solution)/shard_map/ppermute | solution.py:269
  139.5 7.4 %collective-permute-start.37 = (bf16[96,2048]{1,0:T(8,128)(2,1)S(1)}, bf16[96,2048]{1,0:T(8,128)(2,1)S(1)}, u32[]{:S(2)}, u32[]{:S(2)}) collective-permute-start(bf16[96,2048]{1,0:T(8,128)(2,1)S(1)} %get-tuple-element.141), channel_id=1, source_target_pairs={{5,0},{2,1},{7,2},{0,3},{1,4},{6,5},{3,6},{4,7},{13,8},{10,9},{15,... | collective-permute-start | bytes 1179656 | tf_op jit(solution)/shard_map/ppermute | solution.py:269
  143.7 14.5 %collective-permute-start.40 = (bf16[128,2048]{1,0:T(8,128)(2,1)S(1)}, bf16[128,2048]{1,0:T(8,128)(2,1)S(1)}, u32[]{:S(2)}, u32[]{:S(2)}) collective-permute-start(bf16[128,2048]{1,0:T(8,128)(2,1)S(1)} %add.121), channel_id=1, source_target_pairs={{0,8},{8,16},{16,24},{24,0},{1,9},{9,17},{17,25},{25,1},{2,10},{10... | collective-permute-start | bytes 1572872 | tf_op jit(solution)/shard_map/ppermute | solution.py:189
  149.0 6.4 %collective-permute-start.38 = (bf16[64,2048]{1,0:T(8,128)(2,1)S(1)}, bf16[64,2048]{1,0:T(8,128)(2,1)S(1)}, u32[]{:S(2)}, u32[]{:S(2)}) collective-permute-start(bf16[64,2048]{1,0:T(8,128)(2,1)S(1)} %get-tuple-element.143), channel_id=1, source_target_pairs={{2,0},{5,1},{0,2},{7,3},{6,4},{1,5},{4,6},{3,7},{10,8},{13,9},{8,1... | collective-permute-start | bytes 786440 | tf_op jit(solution)/shard_map/ppermute | solution.py:269
  150.7 7.6 %collective-permute-start.39 = (bf16[64,2048]{1,0:T(8,128)(2,1)S(1)}, bf16[64,2048]{1,0:T(8,128)(2,1)S(1)}, u32[]{:S(2)}, u32[]{:S(2)}) collective-permute-start(bf16[64,2048]{1,0:T(8,128)(2,1)S(1)} %get-tuple-element.144), channel_id=1, source_target_pairs={{2,0},{5,1},{0,2},{7,3},{6,4},{1,5},{4,6},{3,7},{10,8},{13,9},{8,1... | collective-permute-start | bytes 786440 | tf_op jit(solution)/shard_map/ppermute | solution.py:269

commit v5 on v3

--- a/solution.py
+++ b/solution.py
@@ -364,9 +364,12 @@
             mark = add_chunk(sums, mark)
             mark, sums = combine_chunk(i - 1, HALVES, mark)
             back[last] = send_back(results, [mark], [mark, *sums[1], *travelling])
+            ahead = [*sums[1], *sums[2]]
     mark = add_chunk(sums, mark)
     mark, sums = combine_chunk(last, HALVES, mark)
-    back[0] = send_back([back[0][0]] + [after(x, mark) for x in back[0][1:]])
+    own = back[0]
+    for j in range(1, len(steps)):
+        own[j] = shift_back(after(own[j], *(ahead if j < 3 else [mark, own[2]])), *steps[j], False)
     mark = add_chunk(sums)
     back[0][0] = after(back[0][0], mark)
     own = return_sums(combine(blocks[0], back[0], router_full, HALVES))

time: 159 us -> 157 us (0.987)
  waiting for transfers between devices: 77.8 us -> 75.6 us
    ppermute x19, waiting for transfers between devices: 35 us -> 32.1 us  [shift_back(): return lax.ppermute(array, 'expert', pairs)]
where the time goes in v5:
time: 157 us
  waiting for transfers between devices  75.6 us (48%)
  starting transfers between devices  43.4 us (28%)
  Pallas kernels  29.4 us (19%)
  local copies, waits for them, and re-layouts  6.97 us (4%)
    ppermute x19, waiting for transfers between devices, shift_back(): return lax.ppermute(array, 'expert', pairs)  32.1 us
    ppermute x6, waiting for transfers between devices, shift_plane(): lax.ppermute(array, 'rep', [(r, (r + by) % reps) for r in range(reps)])  27.8 us
    ppermute x16, starting transfers between devices, shift_owner(): lax.ppermute(array, 'expert', pairs if by >= 0 else [(b, a) for a, b in p...  18.7 us
    ppermute x19, starting transfers between devices, shift_back(): return lax.ppermute(array, 'expert', pairs)  16.1 us
    ppermute x16, waiting for transfers between devices, shift_owner(): lax.ppermute(array, 'expert', pairs if by >= 0 else [(b, a) for a, b in p...  15.7 us
    pallas_call x4, Pallas kernels, apply_experts(): pl.pallas_call(functools.partial(experts_kernel, count), out_shape=[jax.S...  15.3 us
    ppermute x6, starting transfers between devices, shift_plane(): lax.ppermute(array, 'rep', [(r, (r + by) % reps) for r in range(reps)])  8.69 us
    pallas_call x4, Pallas kernels, combine(): pl.pallas_call(functools.partial(combine_kernel, rows, cap, top, dense, h...  8.22 us
  transfers between devices with their start and end apart: 41, of which 23 were waited for; matrix products, arithmetic and copies ran while one was open for 1% of the time, Pallas kernels for 18%

profile of v5, /device:TPU:0, one launch (start us, length us, event | category | flops | bytes accessed | tf_op | source)
XLA Modules:
  0.0 156.6 jit_solution(1857856158392810740)
XLA Ops:
  0.0 1.0 copy-done
  1.0 0.8 copy-done.1
  1.8 0.7 copy-done.2
  3.4 3.0 %collective-permute-start.3 = (bf16[144,2048]{1,0:T(8,128)(2,1)S(1)}, bf16[144,2048]{1,0:T(8,128)(2,1)S(1)}, u32[]{:S(2)}, u32[]{:S(2)}) collective-permute-start(bf16[144,2048]{1,0:T(8,128)(2,1)S(1)} %pack.1.refs_0_), channel_id=1, source_target_pairs={{0,2},{1,5},{2,0},{3,7},{4,6},{5,1},{6,4},{7,3},{8,10},{9,13},{10,... | collective-permute-start | bytes 1769480 | tf_op jit(solution)/shard_map/ppermute | solution.py:186
  6.4 1.6 %collective-permute-start = (bf16[144,2048]{1,0:T(8,128)(2,1)S(1)}, bf16[144,2048]{1,0:T(8,128)(2,1)S(1)}, u32[]{:S(2)}, u32[]{:S(2)}) collective-permute-start(bf16[144,2048]{1,0:T(8,128)(2,1)S(1)} %pack.1.refs_0_), channel_id=1, source_target_pairs={{0,8},{8,16},{16,24},{24,0},{1,9},{9,17},{17,25},{25,1},{2,10},{10... | collective-permute-start | bytes 1769480 | tf_op jit(solution)/shard_map/ppermute | solution.py:189
  8.1 0.9 compare_convert_fusion.groups_ref
  9.0 5.3 %collective-permute-done.3.refs_1_ = bf16[144,2048]{1,0:T(8,128)(2,1)S(1)} collective-permute-done((bf16[144,2048]{1,0:T(8,128)(2,1)S(1)}, bf16[144,2048]{1,0:T(8,128)(2,1)S(1)}, u32[]{:S(2)}, u32[]{:S(2)}) %collective-permute-start.3) | collective-permute-done | bytes 589856 | tf_op jit(solution)/shard_map/ppermute | solution.py:186
  14.3 1.0 select.24
  15.4 2.1 %collective-permute-start.5 = (bf16[96,2048]{1,0:T(8,128)(2,1)S(1)}, bf16[96,2048]{1,0:T(8,128)(2,1)S(1)}, u32[]{:S(2)}, u32[]{:S(2)}) collective-permute-start(bf16[96,2048]{1,0:T(8,128)(2,1)S(1)} %get-tuple-element.76), channel_id=1, source_target_pairs={{0,4},{1,3},{2,6},{3,1},{4,0},{5,7},{6,2},{7,5},{8,12},{9,11},{10,... | collective-permute-start | bytes 1179656 | tf_op jit(solution)/shard_map/ppermute | solution.py:186
  17.5 1.2 collective-permute-start.6
  18.8 4.3 %collective-permute-done.refs_0_.refs_1_ = bf16[144,2048]{1,0:T(8,128)(2,1)S(1)} collective-permute-done((bf16[144,2048]{1,0:T(8,128)(2,1)S(1)}, bf16[144,2048]{1,0:T(8,128)(2,1)S(1)}, u32[]{:S(2)}, u32[]{:S(2)}) %collective-permute-start) | collective-permute-done | bytes 589856 | tf_op jit(solution)/shard_map/ppermute | solution.py:189
  23.3 2.0 %collective-permute-start.7 = (bf16[144,2048]{1,0:T(8,128)(2,1)S(1)}, bf16[144,2048]{1,0:T(8,128)(2,1)S(1)}, u32[]{:S(2)}, u32[]{:S(2)}) collective-permute-start(bf16[144,2048]{1,0:T(8,128)(2,1)S(1)} %collective-permute-done.refs_0_.refs_1_), channel_id=1, source_target_pairs={{0,2},{1,5},{2,0},{3,7},{4,6},{5,1},{6,4},{7,3},{8,10},{9,13},{10,... | collective-permute-start | bytes 1769480 | tf_op jit(solution)/shard_map/ppermute | solution.py:186
  25.3 1.6 %collective-permute-start.1 = (bf16[144,2048]{1,0:T(8,128)(2,1)S(1)}, bf16[144,2048]{1,0:T(8,128)(2,1)S(1)}, u32[]{:S(2)}, u32[]{:S(2)}) collective-permute-start(bf16[144,2048]{1,0:T(8,128)(2,1)S(1)} %collective-permute-done.refs_0_.refs_1_), channel_id=1, source_target_pairs={{0,8},{8,16},{16,24},{24,0},{1,9},{9,17},{17,25},{25,1},{2,10},{10... | collective-permute-start | bytes 1769480 | tf_op jit(solution)/shard_map/ppermute | solution.py:189
  26.8 2.2 %collective-permute-done.6.refs_3_ = bf16[96,2048]{1,0:T(8,128)(2,1)S(1)} collective-permute-done((bf16[96,2048]{1,0:T(8,128)(2,1)S(1)}, bf16[96,2048]{1,0:T(8,128)(2,1)S(1)}, u32[]{:S(2)}, u32[]{:S(2)}) %collective-permute-start.6) | collective-permute-done | bytes 393248 | tf_op jit(solution)/shard_map/ppermute | solution.py:186
  29.0 1.9 %copy-done.5 = bf16[1,2048,768]{2,1,0:T(8,128)(2,1)S(1)} copy-done((bf16[1,2048,768]{2,1,0:T(8,128)(2,1)S(1)}, bf16[1,2048,768]{2,1,0:T(8,128)(2,1)}, u32[]{:S(2)}) %copy-start.5) | copy-done | bytes 3145752
  30.9 1.9 %copy-done.7 = bf16[1,768,2048]{2,1,0:T(8,128)(2,1)S(1)} copy-done((bf16[1,768,2048]{2,1,0:T(8,128)(2,1)S(1)}, bf16[1,768,2048]{2,1,0:T(8,128)(2,1)}, u32[]{:S(2)}) %copy-start.7) | copy-done | bytes 3145752
  32.8 3.8 %experts.4 = (bf16[96,2048]{1,0:T(8,128)(2,1)S(1)}, bf16[96,2048]{1,0:T(8,128)(2,1)S(1)}, bf16[96,2048]{1,0:T(8,128)(2,1)S(1)}, bf16[96,2048]{1,0:T(8,128)(2,1)S(1)}) custom-call(bf16[96,2048]{1,0:T(8,128)(2,1)S(1)} %get-tuple-element.78.refs_0_, bf16[96,2048]{1,0:T(8,128)(2,1)S(1)} %collective-permute-done.4.refs_1_, ...), custom_call_target="tpu_custom_call" | custom-call | flops 4000000000 | tf_op jit(solution)/shard_map/experts/pallas_call | solution.py:249
  36.7 1.1 select.25
  38.1 3.6 %collective-permute-done.1.refs_0_.refs_2_ = bf16[144,2048]{1,0:T(8,128)(2,1)S(1)} collective-permute-done((bf16[144,2048]{1,0:T(8,128)(2,1)S(1)}, bf16[144,2048]{1,0:T(8,128)(2,1)S(1)}, u32[]{:S(2)}, u32[]{:S(2)}) %collective-permute-start.1) | collective-permute-done | bytes 589856 | tf_op jit(solution)/shard_map/ppermute | solution.py:189
  41.7 1.5 collective-permute-start.9
  44.1 13.1 %collective-permute-done.2.refs_0_.refs_3_ = bf16[144,2048]{1,0:T(8,128)(2,1)S(1)} collective-permute-done((bf16[144,2048]{1,0:T(8,128)(2,1)S(1)}, bf16[144,2048]{1,0:T(8,128)(2,1)S(1)}, u32[]{:S(2)}, u32[]{:S(2)}) %collective-permute-start.2) | collective-permute-done | bytes 589856 | tf_op jit(solution)/shard_map/ppermute | solution.py:189
  57.2 0.7 collective-permute-done.9.refs_1_
  57.9 1.0 select.26
  59.1 2.0 %collective-permute-start.12 = (bf16[144,2048]{1,0:T(8,128)(2,1)S(1)}, bf16[144,2048]{1,0:T(8,128)(2,1)S(1)}, u32[]{:S(2)}, u32[]{:S(2)}) collective-permute-start(bf16[144,2048]{1,0:T(8,128)(2,1)S(1)} %collective-permute-done.2.refs_0_.refs_3_), channel_id=1, source_target_pairs={{0,2},{1,5},{2,0},{3,7},{4,6},{5,1},{6,4},{7,3},{8,10},{9,13},{10,... | collective-permute-start | bytes 1769480 | tf_op jit(solution)/shard_map/ppermute | solution.py:186
  61.2 0.8 collective-permute-start.17
  62.0 1.0 collective-permute-start.16
  63.0 3.8 %experts.5 = (bf16[96,2048]{1,0:T(8,128)(2,1)S(1)}, bf16[96,2048]{1,0:T(8,128)(2,1)S(1)}, bf16[96,2048]{1,0:T(8,128)(2,1)S(1)}, bf16[96,2048]{1,0:T(8,128)(2,1)S(1)}) custom-call(bf16[96,2048]{1,0:T(8,128)(2,1)S(1)} %get-tuple-element.90.refs_0_, bf16[96,2048]{1,0:T(8,128)(2,1)S(1)} %collective-permute-done.8.refs_1_, ...), custom_call_target="tpu_custom_call" | custom-call | flops 4000000000 | tf_op jit(solution)/shard_map/experts/pallas_call | solution.py:249
  67.0 5.7 %collective-permute-done.18.refs_3_ = bf16[96,2048]{1,0:T(8,128)(2,1)S(1)} collective-permute-done((bf16[96,2048]{1,0:T(8,128)(2,1)S(1)}, bf16[96,2048]{1,0:T(8,128)(2,1)S(1)}, u32[]{:S(2)}, u32[]{:S(2)}) %collective-permute-start.18) | collective-permute-done | bytes 393248 | tf_op jit(solution)/shard_map/ppermute | solution.py:186
  72.7 0.8 collective-permute-start.14
  73.4 1.4 collective-permute-done.12.refs_1_
  74.8 1.0 select.27
  75.9 2.5 %collective-permute-start.21 = (bf16[96,2048]{1,0:T(8,128)(2,1)S(1)}, bf16[96,2048]{1,0:T(8,128)(2,1)S(1)}, u32[]{:S(2)}, u32[]{:S(2)}) collective-permute-start(bf16[96,2048]{1,0:T(8,128)(2,1)S(1)} %get-tuple-element.114), channel_id=1, source_target_pairs={{0,5},{1,2},{2,7},{3,0},{4,1},{5,6},{6,3},{7,4},{8,13},{9,10},{10,... | collective-permute-start | bytes 1179656 | tf_op jit(solution)/shard_map/ppermute | solution.py:186
  78.4 0.8 collective-permute-start.20
  79.5 3.5 %collective-permute-done.14.refs_4_ = bf16[96,2048]{1,0:T(8,128)(2,1)S(1)} collective-permute-done((bf16[96,2048]{1,0:T(8,128)(2,1)S(1)}, bf16[96,2048]{1,0:T(8,128)(2,1)S(1)}, u32[]{:S(2)}, u32[]{:S(2)}) %collective-permute-start.14) | collective-permute-done | bytes 393248 | tf_op jit(solution)/shard_map/ppermute | solution.py:269
  83.0 3.3 %collective-permute-done.15.refs_5_ = bf16[96,2048]{1,0:T(8,128)(2,1)S(1)} collective-permute-done((bf16[96,2048]{1,0:T(8,128)(2,1)S(1)}, bf16[96,2048]{1,0:T(8,128)(2,1)S(1)}, u32[]{:S(2)}, u32[]{:S(2)}) %collective-permute-start.15) | collective-permute-done | bytes 393248 | tf_op jit(solution)/shard_map/ppermute | solution.py:269
  86.3 2.1 %combine.4 = (f32[128,2048]{1,0:T(8,128)S(1)}, bf16[128,2048]{1,0:T(8,128)(2,1)S(1)}) custom-call(f32[4,32]{1,0:T(4,128)S(1)} %compare_convert_fusion.groups_ref, bf16[32,2048]{1,0:T(8,128)(2,1)S(1)} %router.1.router_ref, bf16[144,2048]{1,0:T(8,128)(2,1)S(1)} %collective-permute-done.refs_0_.refs_1_, bf16[144,2048]{1,0:T(8,128)(2,1)S(1)} %collective-permute-done.7.refs_1_, ...), custom_call_target="tpu_custom_call" | custom-call | flops 2000000000 | tf_op jit(solution)/shard_map/combine/pallas_call | solution.py:272
  88.4 2.5 %collective-permute-start.22 = (bf16[128,2048]{1,0:T(8,128)(2,1)S(1)}, bf16[128,2048]{1,0:T(8,128)(2,1)S(1)}, u32[]{:S(2)}, u32[]{:S(2)}) collective-permute-start(bf16[128,2048]{1,0:T(8,128)(2,1)S(1)} %get-tuple-element.117), channel_id=1, source_target_pairs={{2,0},{5,1},{0,2},{7,3},{6,4},{1,5},{4,6},{3,7},{10,8},{13,9},{8,1... | collective-permute-start | bytes 1572872 | tf_op jit(solution)/shard_map/ppermute | solution.py:269
  90.9 3.8 %experts.6 = (bf16[96,2048]{1,0:T(8,128)(2,1)S(1)}, bf16[96,2048]{1,0:T(8,128)(2,1)S(1)}, bf16[96,2048]{1,0:T(8,128)(2,1)S(1)}, bf16[96,2048]{1,0:T(8,128)(2,1)S(1)}) custom-call(bf16[96,2048]{1,0:T(8,128)(2,1)S(1)} %get-tuple-element.100.refs_0_, bf16[96,2048]{1,0:T(8,128)(2,1)S(1)} %collective-permute-done.16.refs_1_, ...), custom_call_target="tpu_custom_call" | custom-call | flops 4000000000 | tf_op jit(solution)/shard_map/experts/pallas_call | solution.py:249
  95.5 1.3 collective-permute-start.25
  96.8 3.8 %experts.7 = (bf16[96,2048]{1,0:T(8,128)(2,1)S(1)}, bf16[96,2048]{1,0:T(8,128)(2,1)S(1)}, bf16[96,2048]{1,0:T(8,128)(2,1)S(1)}, bf16[96,2048]{1,0:T(8,128)(2,1)S(1)}) custom-call(bf16[96,2048]{1,0:T(8,128)(2,1)S(1)} %get-tuple-element.108.refs_0_, bf16[96,2048]{1,0:T(8,128)(2,1)S(1)} %collective-permute-done.19.refs_1_, ...), custom_call_target="tpu_custom_call" | custom-call | flops 4000000000 | tf_op jit(solution)/shard_map/experts/pallas_call | solution.py:249
  100.7 1.5 collective-permute-done.22.refs_0_
  102.2 2.4 %collective-permute-start.28 = (bf16[128,2048]{1,0:T(8,128)(2,1)S(1)}, bf16[128,2048]{1,0:T(8,128)(2,1)S(1)}, u32[]{:S(2)}, u32[]{:S(2)}) collective-permute-start(bf16[128,2048]{1,0:T(8,128)(2,1)S(1)} %add.119), channel_id=1, source_target_pairs={{0,8},{8,16},{16,24},{24,0},{1,9},{9,17},{17,25},{25,1},{2,10},{10... | collective-permute-start | bytes 1572872 | tf_op jit(solution)/shard_map/ppermute | solution.py:189
  104.6 2.3 %collective-permute-done.24.refs_4_ = bf16[96,2048]{1,0:T(8,128)(2,1)S(1)} collective-permute-done((bf16[96,2048]{1,0:T(8,128)(2,1)S(1)}, bf16[96,2048]{1,0:T(8,128)(2,1)S(1)}, u32[]{:S(2)}, u32[]{:S(2)}) %collective-permute-start.24) | collective-permute-done | bytes 393248 | tf_op jit(solution)/shard_map/ppermute | solution.py:269
  107.4 2.1 %combine.5 = (f32[128,2048]{1,0:T(8,128)S(1)}, bf16[64,2048]{1,0:T(8,128)(2,1)S(1)}, bf16[64,2048]{1,0:T(8,128)(2,1)S(1)}) custom-call(f32[4,32]{1,0:T(4,128)S(1)} %compare_convert_fusion.groups_ref, bf16[32,2048]{1,0:T(8,128)(2,1)S(1)} %router.1.router_ref, bf16[144,2048]{1,0:T(8,128)(2,1)S(1)} %collective-permute-done.1.refs_0_.refs_2_, ...), custom_call_target="tpu_custom_call" | custom-call | flops 2000000000 | tf_op jit(solution)/shard_map/combine/pallas_call | solution.py:272
  109.5 1.4 collective-permute-start.26
  110.8 0.7 collective-permute-start.27
  111.6 1.1 collective-permute-start.30
  112.7 4.4 %collective-permute-done.26.refs_0_ = bf16[64,2048]{1,0:T(8,128)(2,1)S(1)} collective-permute-done((bf16[64,2048]{1,0:T(8,128)(2,1)S(1)}, bf16[64,2048]{1,0:T(8,128)(2,1)S(1)}, u32[]{:S(2)}, u32[]{:S(2)}) %collective-permute-start.26) | collective-permute-done | bytes 262176 | tf_op jit(solution)/shard_map/ppermute | solution.py:269
  117.7 5.0 %collective-permute-done.27.refs_1_ = bf16[64,2048]{1,0:T(8,128)(2,1)S(1)} collective-permute-done((bf16[64,2048]{1,0:T(8,128)(2,1)S(1)}, bf16[64,2048]{1,0:T(8,128)(2,1)S(1)}, u32[]{:S(2)}, u32[]{:S(2)}) %collective-permute-start.27) | collective-permute-done | bytes 262176 | tf_op jit(solution)/shard_map/ppermute | solution.py:269
  122.7 1.1 collective-permute-start.36
  123.9 1.0 collective-permute-start.34
  124.9 3.3 %collective-permute-done.31.refs_5_ = bf16[96,2048]{1,0:T(8,128)(2,1)S(1)} collective-permute-done((bf16[96,2048]{1,0:T(8,128)(2,1)S(1)}, bf16[96,2048]{1,0:T(8,128)(2,1)S(1)}, u32[]{:S(2)}, u32[]{:S(2)}) %collective-permute-start.31) | collective-permute-done | bytes 393248 | tf_op jit(solution)/shard_map/ppermute | solution.py:269
  128.2 2.1 %combine.6 = (f32[128,2048]{1,0:T(8,128)S(1)}, bf16[64,2048]{1,0:T(8,128)(2,1)S(1)}, bf16[64,2048]{1,0:T(8,128)(2,1)S(1)}) custom-call(f32[4,32]{1,0:T(4,128)S(1)} %compare_convert_fusion.groups_ref, bf16[32,2048]{1,0:T(8,128)(2,1)S(1)} %router.1.router_ref, bf16[144,2048]{1,0:T(8,128)(2,1)S(1)} %collective-permute-done.2.refs_0_.refs_3_, ...), custom_call_target="tpu_custom_call" | custom-call | flops 2000000000 | tf_op jit(solution)/shard_map/combine/pallas_call | solution.py:272
  130.3 1.1 collective-permute-start.32
  131.4 1.0 collective-permute-start.33
  132.7 1.1 collective-permute-start.37
  133.8 6.2 %collective-permute-done.34.refs_2_ = bf16[128,2048]{1,0:T(8,128)(2,1)S(1)} collective-permute-done((bf16[128,2048]{1,0:T(8,128)(2,1)S(1)}, bf16[128,2048]{1,0:T(8,128)(2,1)S(1)}, u32[]{:S(2)}, u32[]{:S(2)}) %collective-permute-start.34) | collective-permute-done | bytes 524320 | tf_op jit(solution)/shard_map/ppermute | solution.py:189
  140.2 2.2 %collective-permute-start.40 = (bf16[128,2048]{1,0:T(8,128)(2,1)S(1)}, bf16[128,2048]{1,0:T(8,128)(2,1)S(1)}, u32[]{:S(2)}, u32[]{:S(2)}) collective-permute-start(bf16[128,2048]{1,0:T(8,128)(2,1)S(1)} %add.121), channel_id=1, source_target_pairs={{0,8},{8,16},{16,24},{24,0},{1,9},{9,17},{17,25},{25,1},{2,10},{10... | collective-permute-start | bytes 1572872 | tf_op jit(solution)/shard_map/ppermute | solution.py:189
  142.4 1.3 collective-permute-done.37.refs_5_
  143.7 2.1 %combine.7 = (f32[128,2048]{1,0:T(8,128)S(1)}, bf16[64,2048]{1,0:T(8,128)(2,1)S(1)}, bf16[64,2048]{1,0:T(8,128)(2,1)S(1)}) custom-call(f32[4,32]{1,0:T(4,128)S(1)} %compare_convert_fusion.groups_ref, bf16[32,2048]{1,0:T(8,128)(2,1)S(1)} %router.1.router_ref, bf16[144,2048]{1,0:T(8,128)(2,1)S(1)} %pack.1.refs_0_, ...), custom_call_target="tpu_custom_call" | custom-call | flops 2000000000 | tf_op jit(solution)/shard_map/combine/pallas_call | solution.py:272
  145.8 1.5 collective-permute-start.38
  147.9 4.3 %collective-permute-done.38.refs_0_ = bf16[64,2048]{1,0:T(8,128)(2,1)S(1)} collective-permute-done((bf16[64,2048]{1,0:T(8,128)(2,1)S(1)}, bf16[64,2048]{1,0:T(8,128)(2,1)S(1)}, u32[]{:S(2)}, u32[]{:S(2)}) %collective-permute-start.38) | collective-permute-done | bytes 262176 | tf_op jit(solution)/shard_map/ppermute | solution.py:269
  152.2 2.8 %collective-permute-done.39.refs_1_ = bf16[64,2048]{1,0:T(8,128)(2,1)S(1)} collective-permute-done((bf16[64,2048]{1,0:T(8,128)(2,1)S(1)}, bf16[64,2048]{1,0:T(8,128)(2,1)S(1)}, u32[]{:S(2)}, u32[]{:S(2)}) %collective-permute-start.39) | collective-permute-done | bytes 262176 | tf_op jit(solution)/shard_map/ppermute | solution.py:269
  155.6 1.0 add.122
  (54 shorter events, 6.9 us)
Async XLA Ops:
  0.0 1.0 copy-start
  1.0 0.8 copy-start.1
  1.8 0.7 copy-start.2
  2.5 0.7 copy-start.3
  3.4 10.9 %collective-permute-start.3 = (bf16[144,2048]{1,0:T(8,128)(2,1)S(1)}, bf16[144,2048]{1,0:T(8,128)(2,1)S(1)}, u32[]{:S(2)}, u32[]{:S(2)}) collective-permute-start(bf16[144,2048]{1,0:T(8,128)(2,1)S(1)} %pack.1.refs_0_), channel_id=1, source_target_pairs={{0,2},{1,5},{2,0},{3,7},{4,6},{5,1},{6,4},{7,3},{8,10},{9,13},{10,... | collective-permute-start | bytes 1769480 | tf_op jit(solution)/shard_map/ppermute | solution.py:186
  6.4 16.7 %collective-permute-start = (bf16[144,2048]{1,0:T(8,128)(2,1)S(1)}, bf16[144,2048]{1,0:T(8,128)(2,1)S(1)}, u32[]{:S(2)}, u32[]{:S(2)}) collective-permute-start(bf16[144,2048]{1,0:T(8,128)(2,1)S(1)} %pack.1.refs_0_), channel_id=1, source_target_pairs={{0,8},{8,16},{16,24},{24,0},{1,9},{9,17},{17,25},{25,1},{2,10},{10... | collective-permute-start | bytes 1769480 | tf_op jit(solution)/shard_map/ppermute | solution.py:189
  8.0 21.0 %copy-start.4 = (bf16[1,2048,768]{2,1,0:T(8,128)(2,1)S(1)}, bf16[1,2048,768]{2,1,0:T(8,128)(2,1)}, u32[]{:S(2)}) copy-start(bf16[1,2048,768]{2,1,0:T(8,128)(2,1)} %refs_4_.7) | copy-start | bytes 9437188
  15.3 7.8 %collective-permute-start.4 = (bf16[96,2048]{1,0:T(8,128)(2,1)S(1)}, bf16[96,2048]{1,0:T(8,128)(2,1)S(1)}, u32[]{:S(2)}, u32[]{:S(2)}) collective-permute-start(bf16[96,2048]{1,0:T(8,128)(2,1)S(1)} %get-tuple-element.75), channel_id=1, source_target_pairs={{0,1},{1,0},{2,3},{3,2},{4,5},{5,4},{6,7},{7,6},{8,9},{9,8},{10,11... | collective-permute-start | bytes 1179656 | tf_op jit(solution)/shard_map/ppermute | solution.py:186
  15.4 7.9 %collective-permute-start.5 = (bf16[96,2048]{1,0:T(8,128)(2,1)S(1)}, bf16[96,2048]{1,0:T(8,128)(2,1)S(1)}, u32[]{:S(2)}, u32[]{:S(2)}) collective-permute-start(bf16[96,2048]{1,0:T(8,128)(2,1)S(1)} %get-tuple-element.76), channel_id=1, source_target_pairs={{0,4},{1,3},{2,6},{3,1},{4,0},{5,7},{6,2},{7,5},{8,12},{9,11},{10,... | collective-permute-start | bytes 1179656 | tf_op jit(solution)/shard_map/ppermute | solution.py:186
  17.5 11.5 %collective-permute-start.6 = (bf16[96,2048]{1,0:T(8,128)(2,1)S(1)}, bf16[96,2048]{1,0:T(8,128)(2,1)S(1)}, u32[]{:S(2)}, u32[]{:S(2)}) collective-permute-start(bf16[96,2048]{1,0:T(8,128)(2,1)S(1)} %get-tuple-element.79), channel_id=1, source_target_pairs={{0,5},{1,2},{2,7},{3,0},{4,1},{5,6},{6,3},{7,4},{8,13},{9,10},{10,... | collective-permute-start | bytes 1179656 | tf_op jit(solution)/shard_map/ppermute | solution.py:186
  23.3 13.4 %collective-permute-start.7 = (bf16[144,2048]{1,0:T(8,128)(2,1)S(1)}, bf16[144,2048]{1,0:T(8,128)(2,1)S(1)}, u32[]{:S(2)}, u32[]{:S(2)}) collective-permute-start(bf16[144,2048]{1,0:T(8,128)(2,1)S(1)} %collective-permute-done.refs_0_.refs_1_), channel_id=1, source_target_pairs={{0,2},{1,5},{2,0},{3,7},{4,6},{5,1},{6,4},{7,3},{8,10},{9,13},{10,... | collective-permute-start | bytes 1769480 | tf_op jit(solution)/shard_map/ppermute | solution.py:186
  25.3 16.4 %collective-permute-start.1 = (bf16[144,2048]{1,0:T(8,128)(2,1)S(1)}, bf16[144,2048]{1,0:T(8,128)(2,1)S(1)}, u32[]{:S(2)}, u32[]{:S(2)}) collective-permute-start(bf16[144,2048]{1,0:T(8,128)(2,1)S(1)} %collective-permute-done.refs_0_.refs_1_), channel_id=1, source_target_pairs={{0,8},{8,16},{16,24},{24,0},{1,9},{9,17},{17,25},{25,1},{2,10},{10... | collective-permute-start | bytes 1769480 | tf_op jit(solution)/shard_map/ppermute | solution.py:189
  29.0 1.9 %copy-start.5 = (bf16[1,2048,768]{2,1,0:T(8,128)(2,1)S(1)}, bf16[1,2048,768]{2,1,0:T(8,128)(2,1)}, u32[]{:S(2)}) copy-start(bf16[1,2048,768]{2,1,0:T(8,128)(2,1)} %refs_5_.7) | copy-start | bytes 9437188
  30.9 1.9 %copy-start.7 = (bf16[1,768,2048]{2,1,0:T(8,128)(2,1)S(1)}, bf16[1,768,2048]{2,1,0:T(8,128)(2,1)}, u32[]{:S(2)}) copy-start(bf16[1,768,2048]{2,1,0:T(8,128)(2,1)} %refs_6_.7) | copy-start | bytes 9437188
  36.6 26.4 %copy-start.6 = (bf16[1,2048,768]{2,1,0:T(8,128)(2,1)S(1)}, bf16[1,2048,768]{2,1,0:T(8,128)(2,1)}, u32[]{:S(2)}) copy-start(bf16[1,2048,768]{2,1,0:T(8,128)(2,1)} %refs_5_.7) | copy-start | bytes 9437188
  37.7 4.0 %collective-permute-start.8 = (bf16[96,2048]{1,0:T(8,128)(2,1)S(1)}, bf16[96,2048]{1,0:T(8,128)(2,1)S(1)}, u32[]{:S(2)}, u32[]{:S(2)}) collective-permute-start(bf16[96,2048]{1,0:T(8,128)(2,1)S(1)} %get-tuple-element.83), channel_id=1, source_target_pairs={{0,1},{1,0},{2,3},{3,2},{4,5},{5,4},{6,7},{7,6},{8,9},{9,8},{10,11... | collective-permute-start | bytes 1179656 | tf_op jit(solution)/shard_map/ppermute | solution.py:186
  41.7 15.5 %collective-permute-start.2 = (bf16[144,2048]{1,0:T(8,128)(2,1)S(1)}, bf16[144,2048]{1,0:T(8,128)(2,1)S(1)}, u32[]{:S(2)}, u32[]{:S(2)}) collective-permute-start(bf16[144,2048]{1,0:T(8,128)(2,1)S(1)} %collective-permute-done.1.refs_0_.refs_2_), channel_id=1, source_target_pairs={{0,8},{8,16},{16,24},{24,0},{1,9},{9,17},{17,25},{25,1},{2,10},{10... | collective-permute-start | bytes 1769480 | tf_op jit(solution)/shard_map/ppermute | solution.py:189
  41.7 16.2 %collective-permute-start.9 = (bf16[144,2048]{1,0:T(8,128)(2,1)S(1)}, bf16[144,2048]{1,0:T(8,128)(2,1)S(1)}, u32[]{:S(2)}, u32[]{:S(2)}) collective-permute-start(bf16[144,2048]{1,0:T(8,128)(2,1)S(1)} %collective-permute-done.1.refs_0_.refs_2_), channel_id=1, source_target_pairs={{0,2},{1,5},{2,0},{3,7},{4,6},{5,1},{6,4},{7,3},{8,10},{9,13},{10,... | collective-permute-start | bytes 1769480 | tf_op jit(solution)/shard_map/ppermute | solution.py:186
  43.2 15.7 %collective-permute-start.10 = (bf16[96,2048]{1,0:T(8,128)(2,1)S(1)}, bf16[96,2048]{1,0:T(8,128)(2,1)S(1)}, u32[]{:S(2)}, u32[]{:S(2)}) collective-permute-start(bf16[96,2048]{1,0:T(8,128)(2,1)S(1)} %get-tuple-element.87), channel_id=1, source_target_pairs={{0,4},{1,3},{2,6},{3,1},{4,0},{5,7},{6,2},{7,5},{8,12},{9,11},{10,... | collective-permute-start | bytes 1179656 | tf_op jit(solution)/shard_map/ppermute | solution.py:186
  43.7 15.4 %collective-permute-start.11 = (bf16[96,2048]{1,0:T(8,128)(2,1)S(1)}, bf16[96,2048]{1,0:T(8,128)(2,1)S(1)}, u32[]{:S(2)}, u32[]{:S(2)}) collective-permute-start(bf16[96,2048]{1,0:T(8,128)(2,1)S(1)} %get-tuple-element.88), channel_id=1, source_target_pairs={{0,5},{1,2},{2,7},{3,0},{4,1},{5,6},{6,3},{7,4},{8,13},{9,10},{10,... | collective-permute-start | bytes 1179656 | tf_op jit(solution)/shard_map/ppermute | solution.py:186
  59.1 15.7 %collective-permute-start.12 = (bf16[144,2048]{1,0:T(8,128)(2,1)S(1)}, bf16[144,2048]{1,0:T(8,128)(2,1)S(1)}, u32[]{:S(2)}, u32[]{:S(2)}) collective-permute-start(bf16[144,2048]{1,0:T(8,128)(2,1)S(1)} %collective-permute-done.2.refs_0_.refs_3_), channel_id=1, source_target_pairs={{0,2},{1,5},{2,0},{3,7},{4,6},{5,1},{6,4},{7,3},{8,10},{9,13},{10,... | collective-permute-start | bytes 1769480 | tf_op jit(solution)/shard_map/ppermute | solution.py:186
  61.2 11.5 %collective-permute-start.18 = (bf16[96,2048]{1,0:T(8,128)(2,1)S(1)}, bf16[96,2048]{1,0:T(8,128)(2,1)S(1)}, u32[]{:S(2)}, u32[]{:S(2)}) collective-permute-start(bf16[96,2048]{1,0:T(8,128)(2,1)S(1)} %get-tuple-element.106), channel_id=1, source_target_pairs={{0,5},{1,2},{2,7},{3,0},{4,1},{5,6},{6,3},{7,4},{8,13},{9,10},{10,... | collective-permute-start | bytes 1179656 | tf_op jit(solution)/shard_map/ppermute | solution.py:186
  61.2 14.7 %collective-permute-start.17 = (bf16[96,2048]{1,0:T(8,128)(2,1)S(1)}, bf16[96,2048]{1,0:T(8,128)(2,1)S(1)}, u32[]{:S(2)}, u32[]{:S(2)}) collective-permute-start(bf16[96,2048]{1,0:T(8,128)(2,1)S(1)} %get-tuple-element.104), channel_id=1, source_target_pairs={{0,4},{1,3},{2,6},{3,1},{4,0},{5,7},{6,2},{7,5},{8,12},{9,11},{10,... | collective-permute-start | bytes 1179656 | tf_op jit(solution)/shard_map/ppermute | solution.py:186
  62.0 13.9 %collective-permute-start.16 = (bf16[96,2048]{1,0:T(8,128)(2,1)S(1)}, bf16[96,2048]{1,0:T(8,128)(2,1)S(1)}, u32[]{:S(2)}, u32[]{:S(2)}) collective-permute-start(bf16[96,2048]{1,0:T(8,128)(2,1)S(1)} %get-tuple-element.102), channel_id=1, source_target_pairs={{0,1},{1,0},{2,3},{3,2},{4,5},{5,4},{6,7},{7,6},{8,9},{9,8},{10,11... | collective-permute-start | bytes 1179656 | tf_op jit(solution)/shard_map/ppermute | solution.py:186
  66.9 12.3 %collective-permute-start.13 = (bf16[96,2048]{1,0:T(8,128)(2,1)S(1)}, bf16[96,2048]{1,0:T(8,128)(2,1)S(1)}, u32[]{:S(2)}, u32[]{:S(2)}) collective-permute-start(bf16[96,2048]{1,0:T(8,128)(2,1)S(1)} %get-tuple-element.96), channel_id=1, source_target_pairs={{1,0},{0,1},{3,2},{2,3},{5,4},{4,5},{7,6},{6,7},{9,8},{8,9},{11,10... | collective-permute-start | bytes 1179656 | tf_op jit(solution)/shard_map/ppermute | solution.py:269
  72.7 10.3 %collective-permute-start.14 = (bf16[96,2048]{1,0:T(8,128)(2,1)S(1)}, bf16[96,2048]{1,0:T(8,128)(2,1)S(1)}, u32[]{:S(2)}, u32[]{:S(2)}) collective-permute-start(bf16[96,2048]{1,0:T(8,128)(2,1)S(1)} %get-tuple-element.97), channel_id=1, source_target_pairs={{4,0},{3,1},{6,2},{1,3},{0,4},{7,5},{2,6},{5,7},{12,8},{11,9},{14,... | collective-permute-start | bytes 1179656 | tf_op jit(solution)/shard_map/ppermute | solution.py:269
  74.8 11.5 %collective-permute-start.15 = (bf16[96,2048]{1,0:T(8,128)(2,1)S(1)}, bf16[96,2048]{1,0:T(8,128)(2,1)S(1)}, u32[]{:S(2)}, u32[]{:S(2)}) collective-permute-start(bf16[96,2048]{1,0:T(8,128)(2,1)S(1)} %get-tuple-element.98), channel_id=1, source_target_pairs={{5,0},{2,1},{7,2},{0,3},{1,4},{6,5},{3,6},{4,7},{13,8},{10,9},{15,... | collective-permute-start | bytes 1179656 | tf_op jit(solution)/shard_map/ppermute | solution.py:269
  75.9 18.9 %collective-permute-start.21 = (bf16[96,2048]{1,0:T(8,128)(2,1)S(1)}, bf16[96,2048]{1,0:T(8,128)(2,1)S(1)}, u32[]{:S(2)}, u32[]{:S(2)}) collective-permute-start(bf16[96,2048]{1,0:T(8,128)(2,1)S(1)} %get-tuple-element.114), channel_id=1, source_target_pairs={{0,5},{1,2},{2,7},{3,0},{4,1},{5,6},{6,3},{7,4},{8,13},{9,10},{10,... | collective-permute-start | bytes 1179656 | tf_op jit(solution)/shard_map/ppermute | solution.py:186
  78.4 17.1 %collective-permute-start.20 = (bf16[96,2048]{1,0:T(8,128)(2,1)S(1)}, bf16[96,2048]{1,0:T(8,128)(2,1)S(1)}, u32[]{:S(2)}, u32[]{:S(2)}) collective-permute-start(bf16[96,2048]{1,0:T(8,128)(2,1)S(1)} %get-tuple-element.112), channel_id=1, source_target_pairs={{0,4},{1,3},{2,6},{3,1},{4,0},{5,7},{6,2},{7,5},{8,12},{9,11},{10,... | collective-permute-start | bytes 1179656 | tf_op jit(solution)/shard_map/ppermute | solution.py:186
  79.2 17.6 %collective-permute-start.19 = (bf16[96,2048]{1,0:T(8,128)(2,1)S(1)}, bf16[96,2048]{1,0:T(8,128)(2,1)S(1)}, u32[]{:S(2)}, u32[]{:S(2)}) collective-permute-start(bf16[96,2048]{1,0:T(8,128)(2,1)S(1)} %get-tuple-element.110), channel_id=1, source_target_pairs={{0,1},{1,0},{2,3},{3,2},{4,5},{5,4},{6,7},{7,6},{8,9},{9,8},{10,11... | collective-permute-start | bytes 1179656 | tf_op jit(solution)/shard_map/ppermute | solution.py:186
  88.4 13.8 %collective-permute-start.22 = (bf16[128,2048]{1,0:T(8,128)(2,1)S(1)}, bf16[128,2048]{1,0:T(8,128)(2,1)S(1)}, u32[]{:S(2)}, u32[]{:S(2)}) collective-permute-start(bf16[128,2048]{1,0:T(8,128)(2,1)S(1)} %get-tuple-element.117), channel_id=1, source_target_pairs={{2,0},{5,1},{0,2},{7,3},{6,4},{1,5},{4,6},{3,7},{10,8},{13,9},{8,1... | collective-permute-start | bytes 1572872 | tf_op jit(solution)/shard_map/ppermute | solution.py:269
  94.8 9.8 %collective-permute-start.23 = (bf16[96,2048]{1,0:T(8,128)(2,1)S(1)}, bf16[96,2048]{1,0:T(8,128)(2,1)S(1)}, u32[]{:S(2)}, u32[]{:S(2)}) collective-permute-start(bf16[96,2048]{1,0:T(8,128)(2,1)S(1)} %get-tuple-element.119), channel_id=1, source_target_pairs={{1,0},{0,1},{3,2},{2,3},{5,4},{4,5},{7,6},{6,7},{9,8},{8,9},{11,10... | collective-permute-start | bytes 1179656 | tf_op jit(solution)/shard_map/ppermute | solution.py:269
  94.8 12.1 %collective-permute-start.24 = (bf16[96,2048]{1,0:T(8,128)(2,1)S(1)}, bf16[96,2048]{1,0:T(8,128)(2,1)S(1)}, u32[]{:S(2)}, u32[]{:S(2)}) collective-permute-start(bf16[96,2048]{1,0:T(8,128)(2,1)S(1)} %get-tuple-element.120), channel_id=1, source_target_pairs={{4,0},{3,1},{6,2},{1,3},{0,4},{7,5},{2,6},{5,7},{12,8},{11,9},{14,... | collective-permute-start | bytes 1179656 | tf_op jit(solution)/shard_map/ppermute | solution.py:269
  95.5 11.9 %collective-permute-start.25 = (bf16[96,2048]{1,0:T(8,128)(2,1)S(1)}, bf16[96,2048]{1,0:T(8,128)(2,1)S(1)}, u32[]{:S(2)}, u32[]{:S(2)}) collective-permute-start(bf16[96,2048]{1,0:T(8,128)(2,1)S(1)} %get-tuple-element.121), channel_id=1, source_target_pairs={{5,0},{2,1},{7,2},{0,3},{1,4},{6,5},{3,6},{4,7},{13,8},{10,9},{15,... | collective-permute-start | bytes 1179656 | tf_op jit(solution)/shard_map/ppermute | solution.py:269
  102.2 14.8 %collective-permute-start.28 = (bf16[128,2048]{1,0:T(8,128)(2,1)S(1)}, bf16[128,2048]{1,0:T(8,128)(2,1)S(1)}, u32[]{:S(2)}, u32[]{:S(2)}) collective-permute-start(bf16[128,2048]{1,0:T(8,128)(2,1)S(1)} %add.119), channel_id=1, source_target_pairs={{0,8},{8,16},{16,24},{24,0},{1,9},{9,17},{17,25},{25,1},{2,10},{10... | collective-permute-start | bytes 1572872 | tf_op jit(solution)/shard_map/ppermute | solution.py:189
  104.6 7.0 %collective-permute-start.29 = (bf16[96,2048]{1,0:T(8,128)(2,1)S(1)}, bf16[96,2048]{1,0:T(8,128)(2,1)S(1)}, u32[]{:S(2)}, u32[]{:S(2)}) collective-permute-start(bf16[96,2048]{1,0:T(8,128)(2,1)S(1)} %get-tuple-element.127), channel_id=1, source_target_pairs={{1,0},{0,1},{3,2},{2,3},{5,4},{4,5},{7,6},{6,7},{9,8},{8,9},{11,10... | collective-permute-start | bytes 1179656 | tf_op jit(solution)/shard_map/ppermute | solution.py:269
  109.5 7.6 %collective-permute-start.26 = (bf16[64,2048]{1,0:T(8,128)(2,1)S(1)}, bf16[64,2048]{1,0:T(8,128)(2,1)S(1)}, u32[]{:S(2)}, u32[]{:S(2)}) collective-permute-start(bf16[64,2048]{1,0:T(8,128)(2,1)S(1)} %get-tuple-element.124), channel_id=1, source_target_pairs={{2,0},{5,1},{0,2},{7,3},{6,4},{1,5},{4,6},{3,7},{10,8},{13,9},{8,1... | collective-permute-start | bytes 786440 | tf_op jit(solution)/shard_map/ppermute | solution.py:269
  110.8 11.8 %collective-permute-start.27 = (bf16[64,2048]{1,0:T(8,128)(2,1)S(1)}, bf16[64,2048]{1,0:T(8,128)(2,1)S(1)}, u32[]{:S(2)}, u32[]{:S(2)}) collective-permute-start(bf16[64,2048]{1,0:T(8,128)(2,1)S(1)} %get-tuple-element.125), channel_id=1, source_target_pairs={{2,0},{5,1},{0,2},{7,3},{6,4},{1,5},{4,6},{3,7},{10,8},{13,9},{8,1... | collective-permute-start | bytes 786440 | tf_op jit(solution)/shard_map/ppermute | solution.py:269
  111.6 13.3 %collective-permute-start.30 = (bf16[96,2048]{1,0:T(8,128)(2,1)S(1)}, bf16[96,2048]{1,0:T(8,128)(2,1)S(1)}, u32[]{:S(2)}, u32[]{:S(2)}) collective-permute-start(bf16[96,2048]{1,0:T(8,128)(2,1)S(1)} %get-tuple-element.129), channel_id=1, source_target_pairs={{4,0},{3,1},{6,2},{1,3},{0,4},{7,5},{2,6},{5,7},{12,8},{11,9},{14,... | collective-permute-start | bytes 1179656 | tf_op jit(solution)/shard_map/ppermute | solution.py:269
  117.0 11.1 %collective-permute-start.31 = (bf16[96,2048]{1,0:T(8,128)(2,1)S(1)}, bf16[96,2048]{1,0:T(8,128)(2,1)S(1)}, u32[]{:S(2)}, u32[]{:S(2)}) collective-permute-start(bf16[96,2048]{1,0:T(8,128)(2,1)S(1)} %get-tuple-element.131), channel_id=1, source_target_pairs={{5,0},{2,1},{7,2},{0,3},{1,4},{6,5},{3,6},{4,7},{13,8},{10,9},{15,... | collective-permute-start | bytes 1179656 | tf_op jit(solution)/shard_map/ppermute | solution.py:269
  122.7 10.1 %collective-permute-start.36 = (bf16[96,2048]{1,0:T(8,128)(2,1)S(1)}, bf16[96,2048]{1,0:T(8,128)(2,1)S(1)}, u32[]{:S(2)}, u32[]{:S(2)}) collective-permute-start(bf16[96,2048]{1,0:T(8,128)(2,1)S(1)} %get-tuple-element.139), channel_id=1, source_target_pairs={{4,0},{3,1},{6,2},{1,3},{0,4},{7,5},{2,6},{5,7},{12,8},{11,9},{14,... | collective-permute-start | bytes 1179656 | tf_op jit(solution)/shard_map/ppermute | solution.py:269
  123.9 16.1 %collective-permute-start.34 = (bf16[128,2048]{1,0:T(8,128)(2,1)S(1)}, bf16[128,2048]{1,0:T(8,128)(2,1)S(1)}, u32[]{:S(2)}, u32[]{:S(2)}) collective-permute-start(bf16[128,2048]{1,0:T(8,128)(2,1)S(1)} %add.120), channel_id=1, source_target_pairs={{0,8},{8,16},{16,24},{24,0},{1,9},{9,17},{17,25},{25,1},{2,10},{10... | collective-permute-start | bytes 1572872 | tf_op jit(solution)/shard_map/ppermute | solution.py:189
  130.3 9.8 %collective-permute-start.32 = (bf16[64,2048]{1,0:T(8,128)(2,1)S(1)}, bf16[64,2048]{1,0:T(8,128)(2,1)S(1)}, u32[]{:S(2)}, u32[]{:S(2)}) collective-permute-start(bf16[64,2048]{1,0:T(8,128)(2,1)S(1)} %get-tuple-element.133), channel_id=1, source_target_pairs={{2,0},{5,1},{0,2},{7,3},{6,4},{1,5},{4,6},{3,7},{10,8},{13,9},{8,1... | collective-permute-start | bytes 786440 | tf_op jit(solution)/shard_map/ppermute | solution.py:269
  131.4 8.7 %collective-permute-start.33 = (bf16[64,2048]{1,0:T(8,128)(2,1)S(1)}, bf16[64,2048]{1,0:T(8,128)(2,1)S(1)}, u32[]{:S(2)}, u32[]{:S(2)}) collective-permute-start(bf16[64,2048]{1,0:T(8,128)(2,1)S(1)} %get-tuple-element.134), channel_id=1, source_target_pairs={{2,0},{5,1},{0,2},{7,3},{6,4},{1,5},{4,6},{3,7},{10,8},{13,9},{8,1... | collective-permute-start | bytes 786440 | tf_op jit(solution)/shard_map/ppermute | solution.py:269
  132.3 10.1 %collective-permute-start.35 = (bf16[96,2048]{1,0:T(8,128)(2,1)S(1)}, bf16[96,2048]{1,0:T(8,128)(2,1)S(1)}, u32[]{:S(2)}, u32[]{:S(2)}) collective-permute-start(bf16[96,2048]{1,0:T(8,128)(2,1)S(1)} %get-tuple-element.137), channel_id=1, source_target_pairs={{1,0},{0,1},{3,2},{2,3},{5,4},{4,5},{7,6},{6,7},{9,8},{8,9},{11,10... | collective-permute-start | bytes 1179656 | tf_op jit(solution)/shard_map/ppermute | solution.py:269
  132.7 11.0 %collective-permute-start.37 = (bf16[96,2048]{1,0:T(8,128)(2,1)S(1)}, bf16[96,2048]{1,0:T(8,128)(2,1)S(1)}, u32[]{:S(2)}, u32[]{:S(2)}) collective-permute-start(bf16[96,2048]{1,0:T(8,128)(2,1)S(1)} %get-tuple-element.141), channel_id=1, source_target_pairs={{5,0},{2,1},{7,2},{0,3},{1,4},{6,5},{3,6},{4,7},{13,8},{10,9},{15,... | collective-permute-start | bytes 1179656 | tf_op jit(solution)/shard_map/ppermute | solution.py:269
  140.2 15.3 %collective-permute-start.40 = (bf16[128,2048]{1,0:T(8,128)(2,1)S(1)}, bf16[128,2048]{1,0:T(8,128)(2,1)S(1)}, u32[]{:S(2)}, u32[]{:S(2)}) collective-permute-start(bf16[128,2048]{1,0:T(8,128)(2,1)S(1)} %add.121), channel_id=1, source_target_pairs={{0,8},{8,16},{16,24},{24,0},{1,9},{9,17},{17,25},{25,1},{2,10},{10... | collective-permute-start | bytes 1572872 | tf_op jit(solution)/shard_map/ppermute | solution.py:189
  145.8 6.4 %collective-permute-start.38 = (bf16[64,2048]{1,0:T(8,128)(2,1)S(1)}, bf16[64,2048]{1,0:T(8,128)(2,1)S(1)}, u32[]{:S(2)}, u32[]{:S(2)}) collective-permute-start(bf16[64,2048]{1,0:T(8,128)(2,1)S(1)} %get-tuple-element.143), channel_id=1, source_target_pairs={{2,0},{5,1},{0,2},{7,3},{6,4},{1,5},{4,6},{3,7},{10,8},{13,9},{8,1... | collective-permute-start | bytes 786440 | tf_op jit(solution)/shard_map/ppermute | solution.py:269
  147.3 7.7 %collective-permute-start.39 = (bf16[64,2048]{1,0:T(8,128)(2,1)S(1)}, bf16[64,2048]{1,0:T(8,128)(2,1)S(1)}, u32[]{:S(2)}, u32[]{:S(2)}) collective-permute-start(bf16[64,2048]{1,0:T(8,128)(2,1)S(1)} %get-tuple-element.144), channel_id=1, source_target_pairs={{2,0},{5,1},{0,2},{7,3},{6,4},{1,5},{4,6},{3,7},{10,8},{13,9},{8,1... | collective-permute-start | bytes 786440 | tf_op jit(solution)/shard_map/ppermute | solution.py:269
